TPU v7x, 256 devices: a whole 4x4x8 slice. The times are simulated.
256 devices in a mesh: dp: 8 (over x, z_lo), ctx: 32 (over y, z_hi, core).
Axes of the slice: x: 4, y: 4, z: 8 (z_hi: 4, z_lo: 2; z = z_hi * 2 + z_lo), core: 2. Of those that a mesh axis runs over, the one named last changes fastest.
Arguments:
- queries: bfloat16 [32768, 8192], P(('dp', 'ctx')), may hold values from -16 to 16
- out_grad: bfloat16 [32768, 8192], P(('dp', 'ctx')), may hold values from -6 to 6
- enc_states: bfloat16 [3072, 1024], P(('dp', 'ctx')), may hold values from -8 to 8
- w_key: bfloat16 [1024, 8192], P('dp', 'ctx'), may hold values from -1 to 1
- w_value: bfloat16 [1024, 8192], P('dp', 'ctx'), may hold values from -0.1875 to 0.1875
- dec_segments: int32 [32768], P(('dp', 'ctx')), may hold values from 0 to 3, as said below
- enc_segments: int32 [3072], P(('dp', 'ctx')), may hold values from 0 to 3, as said below
Outputs:
- query_grad: bfloat16 [32768, 8192], P(('dp', 'ctx'))
- enc_grad: bfloat16 [3072, 1024], P(('dp', 'ctx'))
- w_key_grad: float32 [1024, 8192], P('dp', 'ctx')
- w_value_grad: float32 [1024, 8192], P('dp', 'ctx')
Inputs may be any that keep to these rules, and one draw needn't show every extreme that they name: `dec_segments`: within each pack the ids never fall along the tokens, and each of the 4 ids has one or more decoder tokens in the pack. `enc_segments`: within each pack the ids never fall along the tokens, and each of the 4 ids has two or more encoder tokens in the pack.
All inputs are finite; a program needn't handle non-finite values.
Results may differ from a plain program's by a relative error of at most 0.019.
Values may be sent and summed in bfloat16 or wider, within the bound.
No kernel may reach another device: no remote copies, remote signals or barrier semaphores. Data moves between devices by JAX's collectives and lax.ppermute only.
A program may use at most 64 MiB of HBM per device.

v0:
```python
import math

import jax
import jax.numpy as jnp
from jax import lax
from jax.sharding import PartitionSpec as P

HEAD_DIM = 128


def side_by_side(arrays, axis, dim, along):
    ends, at = ([], 0)
    for a in arrays[:-1]:
        at += a.shape[along]
        ends.append(at)
    both = jnp.concatenate(arrays, axis=along)
    return tuple(jnp.split(lax.all_gather(both, axis, axis=dim, tiled=True), ends, axis=along))


def sent_to_all(value, axis):
    size = lax.axis_size(axis)
    return lax.all_to_all(
        jnp.broadcast_to(value[None], (size, *value.shape)), axis, 0, 0, tiled=True
    )


def joined_along(pieces, dim):
    pieces = jnp.moveaxis(pieces, 0, dim)
    lengths = pieces.shape
    return pieces.reshape(*lengths[:dim], lengths[dim] * lengths[dim + 1], *lengths[dim + 2 :])


def gathered_copies(value, axis, dim):
    pieces = sent_to_all(value, axis)
    return joined_along(pieces, dim)


def split_up(value, dim, size):
    lengths = value.shape
    pieces = value.reshape(*lengths[:dim], size, lengths[dim] // size, *lengths[dim + 1 :])
    return jnp.moveaxis(pieces, dim, 0)


def sum_at_owner(value, axis, dim):
    pieces = split_up(value, dim, lax.axis_size(axis))
    arrived = lax.all_to_all(pieces, axis, split_axis=0, concat_axis=0, tiled=True)
    return arrived.astype(jnp.float32).sum(axis=0)


def in_one_piece(arrays, axis, dim, along):
    ends, at = ([], 0)
    for a in arrays[:-1]:
        at += a.shape[along]
        ends.append(at)
    both = jnp.concatenate(arrays, axis=along)
    return tuple(
        jnp.split(lax.psum_scatter(both, axis, scatter_dimension=dim, tiled=True), ends, axis=along)
    )


def attend(queries, out_grads, key_rows, value_rows, query_ids, key_ids):
    length, full_width = queries.shape
    key_count = key_rows.shape[0]
    head_count = full_width // HEAD_DIM
    group_size = min(head_count, 16)
    column_count = group_size * HEAD_DIM
    row_count = math.gcd(length, 1024)

    def head_group(number):
        column_start = number * column_count
        key_block = key_rows.reshape(key_count, group_size, HEAD_DIM)
        value_block = value_rows.reshape(key_count, group_size, HEAD_DIM)

        def query_block(totals, block_number):
            first_row = block_number * row_count
            query_part = lax.dynamic_slice(
                queries, (first_row, column_start), (row_count, column_count)
            ).reshape(row_count, group_size, HEAD_DIM)
            grad_part = lax.dynamic_slice(
                out_grads, (first_row, column_start), (row_count, column_count)
            ).reshape(row_count, group_size, HEAD_DIM)
            block_ids = lax.dynamic_slice_in_dim(query_ids, first_row, row_count, 0)
            allowed = block_ids[:, None] == key_ids[None, :]
            scores = jnp.einsum(
                "qhd,khd->hqk", query_part, key_block, preferred_element_type=jnp.float32
            )
            scores = jnp.where(allowed[None], scores, -jnp.inf)
            highest = jnp.max(scores, axis=2, keepdims=True)
            weights = jnp.exp(scores - highest)
            probability = weights / jnp.sum(weights, axis=2, keepdims=True)
            upstream = jnp.einsum(
                "qhd,khd->hqk", grad_part, value_block, preferred_element_type=jnp.float32
            )
            row_dot = jnp.sum(probability * upstream, axis=2, keepdims=True)
            score_grad = (probability * (upstream - row_dot)).astype(jnp.bfloat16)
            rounded = probability.astype(jnp.bfloat16)
            key_total = totals[0] + jnp.einsum(
                "hqk,qhd->khd", score_grad, query_part, preferred_element_type=jnp.float32
            )
            value_total = totals[1] + jnp.einsum(
                "hqk,qhd->khd", rounded, grad_part, preferred_element_type=jnp.float32
            )
            totals = (key_total, value_total)
            query_grad = jnp.einsum(
                "hqk,khd->qhd", score_grad, key_block, preferred_element_type=jnp.float32
            ).astype(jnp.bfloat16)
            return (totals, query_grad.reshape(row_count, column_count))

        zeros = jnp.zeros((key_count, group_size, HEAD_DIM), jnp.float32)
        totals, query_grads = lax.scan(
            query_block, (zeros, zeros), jnp.arange(length // row_count, dtype=jnp.int32)
        )
        results = ()
        results = results + (query_grads.reshape(length, column_count),)
        results = results + (
            totals[0].reshape(key_count, column_count),
            totals[1].reshape(key_count, column_count),
        )
        return results

    pieces = lax.map(head_group, jnp.arange(head_count // group_size, dtype=jnp.int32))
    return tuple(
        (jnp.moveaxis(piece, 0, 1).reshape(piece.shape[1], full_width) for piece in pieces)
    )


def body(queries, out_grad, enc_states, w_key, w_value, dec_segments, enc_segments):
    encoder, key_ids = (
        lax.all_gather(enc_states, "ctx", axis=0, tiled=True),
        lax.all_gather(enc_segments, "ctx", axis=0, tiled=True),
    )
    key_weight, value_weight = side_by_side((w_key, w_value), "dp", 0, 1)
    key_part = jnp.dot(encoder, key_weight, preferred_element_type=jnp.float32).astype(jnp.bfloat16)
    value_part = jnp.dot(encoder, value_weight, preferred_element_type=jnp.float32).astype(
        jnp.bfloat16
    )
    local_queries, local_grads = (
        lax.all_to_all(queries, "ctx", split_axis=1, concat_axis=0, tiled=True),
        lax.all_to_all(out_grad, "ctx", split_axis=1, concat_axis=0, tiled=True),
    )
    query_ids = gathered_copies(dec_segments, "ctx", 0)
    head_grad, key_grad, value_grad = attend(
        local_queries, local_grads, key_part, value_part, query_ids, key_ids
    )
    query_grad = lax.all_to_all(head_grad, "ctx", split_axis=0, concat_axis=1, tiled=True)
    key_round = key_grad.astype(jnp.bfloat16)
    value_round = value_grad.astype(jnp.bfloat16)
    across = (((1,), (1,)), ((), ()))
    partial_value = lax.dot_general(
        key_round, key_weight, across, preferred_element_type=jnp.float32
    )
    partial_value = partial_value + lax.dot_general(
        value_round, value_weight, across, preferred_element_type=jnp.float32
    )
    enc_grad = sum_at_owner(partial_value.astype(jnp.bfloat16), "ctx", 0).astype(jnp.bfloat16)
    down = (((0,), (0,)), ((), ()))
    key_term = lax.dot_general(encoder, key_round, down, preferred_element_type=jnp.float32)
    value_term = lax.dot_general(encoder, value_round, down, preferred_element_type=jnp.float32)
    w_key_grad, w_value_grad = tuple(
        (
            part.astype(jnp.float32)
            for part in in_one_piece(
                (key_term.astype(jnp.bfloat16), value_term.astype(jnp.bfloat16)), "dp", 0, 1
            )
        )
    )
    return (query_grad, enc_grad, w_key_grad, w_value_grad)


def solution(mesh):
    in_specs = (
        P(("dp", "ctx"), None),
        P(("dp", "ctx"), None),
        P(("dp", "ctx"), None),
        P("dp", "ctx"),
        P("dp", "ctx"),
        P(("dp", "ctx")),
        P(("dp", "ctx")),
    )
    out_specs = (P(("dp", "ctx"), None), P(("dp", "ctx"), None), P("dp", "ctx"), P("dp", "ctx"))
    return jax.shard_map(body, mesh=mesh, in_specs=in_specs, out_specs=out_specs, check_vma=False)
```

profile of v0, /device:TPU:2, one launch (start us, length us, event | category | flops | bytes accessed | tf_op | source)
XLA Modules:
  0.0 415.0 jit_solution(9430888007886917703)
XLA Ops:
  7.2 4.1 copy.68
  11.2 11.5 %all-to-all-start = ((bf16[128,32,256]{0,2,1:T(8,128)(2,1)}), bf16[128,32,256]{0,2,1:T(8,128)(2,1)S(1)}, u32[]{:S(2)}, u32[]{:S(2)}) async-start(bf16[128,32,256]{0,2,1:T(8,128)(2,1)} %bitcast.99), calls=%async_computation | async-start | bytes 4194304 | tf_op jit(solution)/shard_map/all_to_all | solution.py:138
  22.7 4.1 copy.70
  26.8 47.3 %all-to-all-done = bf16[128,32,256]{0,2,1:T(8,128)(2,1)S(1)} async-done(((bf16[128,32,256]{0,2,1:T(8,128)(2,1)}), bf16[128,32,256]{0,2,1:T(8,128)(2,1)S(1)}, u32[]{:S(2)}, u32[]{:S(2)}) %all-to-all-start) | async-done | bytes 2097184 | tf_op jit(solution)/shard_map/all_to_all | solution.py:138
  74.2 1.3 copy-done.4
  75.5 4.8 %all-to-all-start.2 = ((bf16[128,32,256]{0,2,1:T(8,128)(2,1)}), bf16[128,32,256]{0,2,1:T(8,128)(2,1)}, u32[]{:S(2)}, u32[]{:S(2)}) async-start(bf16[128,32,256]{0,2,1:T(8,128)(2,1)} %bitcast.97), calls=%async_computation.2 | async-start | bytes 4194304 | tf_op jit(solution)/shard_map/all_to_all | solution.py:139
  81.1 101.7 %all-gather = bf16[32,12,1024]{2,1,0:T(8,128)(2,1)S(1)} all-gather(bf16[1,12,1024]{2,1,0:T(8,128)(2,1)S(1)} %bitcast.108), channel_id=1, replica_groups=mesh['dp'=8,'ctx'=32] {'ctx'}, dimensions={0}, use_global_device_ids=true | all-gather | bytes 811008 | tf_op jit(solution)/shard_map/all_gather | solution.py:129
  184.6 12.3 %all-reduce = s32[384]{0:T(512)S(1)} all-reduce(s32[384]{0:T(512)S(1)} %dynamic-update-slice), channel_id=1, replica_groups=mesh['dp'=8,'ctx'=32] {'ctx'}, use_global_device_ids=true, to_apply=%add | all-reduce | flops 384 | bytes 3072
  196.9 1.5 convolution_convert_fusion.3
  199.1 9.5 %all-to-all-start.1 = ((s32[32,1,128]{2,1,0:T(1,128)}), s32[32,1,128]{2,1,0:T(1,128)}, u32[]{:S(2)}, u32[]{:S(2)}) async-start(s32[32,1,128]{2,1,0:T(1,128)} %broadcast_in_dim.41), calls=%async_computation.1 | async-start | bytes 32768 | tf_op jit(solution)/shard_map/all_to_all | solution.py:22
  208.6 2.2 convolution_convert_fusion.4
  211.6 3.3 copy.69
  214.9 4.1 copy.71
  219.0 62.6 %while.27 = (s32[]{:T(128)}, f32[384,2,128]{0,2,1:T(8,128)S(1)}, f32[384,2,128]{0,2,1:T(8,128)}, bf16[4,1024,256]{2,1,0:T(8,128)(2,1)}, s32[4]{0:T(128)S(1)}, /*...) while((s32[]{:T(128)}, f32[384,2,128]{0,2,1:T(8,128)S(1)}, ...), condition=%wide.region_4.5_spmd.clone, body=%wide.region_0.4_spmd.clone.sunk | while | flops 1017117056 | bytes 58062732 | solution.py:110
  221.1 1.1 broadcast_compare_fusion.2
  222.2 1.1 constant_dynamic-slice_fusion.3
  223.3 1.0 copy.98
  224.3 1.0 copy.99
  225.3 2.5 fusion.69
  227.9 2.6 fusion.71
  236.6 1.1 broadcast_compare_fusion.2
  237.7 1.1 constant_dynamic-slice_fusion.3
  238.8 1.0 copy.98
  239.9 1.0 copy.99
  240.9 2.5 fusion.69
  243.4 2.7 fusion.71
  252.3 1.1 broadcast_compare_fusion.2
  253.4 1.1 constant_dynamic-slice_fusion.3
  254.5 1.0 copy.98
  255.5 1.0 copy.99
  256.6 2.5 fusion.69
  259.1 2.7 fusion.71
  268.0 1.1 broadcast_compare_fusion.2
  269.1 1.1 constant_dynamic-slice_fusion.3
  270.2 1.0 copy.98
  271.2 1.0 copy.99
  272.2 2.5 fusion.69
  274.8 2.7 fusion.71
  281.6 1.1 convert_element_type.68
  282.7 1.5 fusion.22
  284.8 39.8 %all_to_all.68 = bf16[32,12,1024]{2,1,0:T(8,128)(2,1)} all-to-all(bf16[32,12,1024]{2,1,0:T(8,128)(2,1)S(1)} %reshape.98), channel_id=1, replica_groups=mesh['dp'=8,'ctx'=32] {'ctx'}, dimensions={0} | all-to-all | bytes 1572864 | tf_op jit(solution)/shard_map/all_to_all | solution.py:46
  324.6 4.5 %all-to-all-start.3 = ((bf16[32,128,256]{2,1,0:T(8,128)(2,1)}), bf16[32,128,256]{2,1,0:T(8,128)(2,1)S(1)}, u32[]{:S(2)}, u32[]{:S(2)}) async-start(bf16[32,128,256]{2,1,0:T(8,128)(2,1)} %bitcast.102), calls=%async_computation.3 | async-start | bytes 4194304 | tf_op jit(solution)/shard_map/all_to_all | solution.py:145
  330.0 1.0 pad_maximum_fusion
  331.1 2.4 copy.86
  334.3 64.2 %reduce-scatter.4.cloned.1.call-done = bf16[128,512]{1,0:T(8,128)(2,1)} async-done(((bf16[1024,512]{1,0:T(8,128)(2,1)}), bf16[128,512]{1,0:T(8,128)(2,1)}) %reduce-scatter.4.cloned.1.call-update) | async-done | bytes 131088
  398.5 0.9 fusion.26
  401.2 2.9 copy.76
  404.1 4.1 copy.77
  (130 shorter events, 29.4 us)
Async XLA Ops:
  11.2 62.9 %all-to-all-start = ((bf16[128,32,256]{0,2,1:T(8,128)(2,1)}), bf16[128,32,256]{0,2,1:T(8,128)(2,1)S(1)}, u32[]{:S(2)}, u32[]{:S(2)}) async-start(bf16[128,32,256]{0,2,1:T(8,128)(2,1)} %bitcast.99), calls=%async_computation | async-start | bytes 4194304 | tf_op jit(solution)/shard_map/all_to_all | solution.py:138
  74.2 1.3 copy-start.4
  74.2 6.2 %copy-start.11 = (bf16[128,256]{1,0:T(8,128)(2,1)S(1)}, bf16[128,256]{1,0:T(8,128)(2,1)}, u32[]{:S(2)}) copy-start(bf16[128,256]{1,0:T(8,128)(2,1)} %param.13) | copy-start | bytes 196612
  74.2 6.2 %copy-start.12 = (bf16[128,256]{1,0:T(8,128)(2,1)S(1)}, bf16[128,256]{1,0:T(8,128)(2,1)}, u32[]{:S(2)}) copy-start(bf16[128,256]{1,0:T(8,128)(2,1)} %param.12) | copy-start | bytes 196612
  74.2 6.9 %copy-start.13 = (bf16[12,1024]{1,0:T(8,128)(2,1)S(1)}, bf16[12,1024]{1,0:T(8,128)(2,1)}, u32[]{:S(2)}) copy-start(bf16[12,1024]{1,0:T(8,128)(2,1)} %param.11) | copy-start | bytes 73732
  75.5 123.0 %all-to-all-start.2 = ((bf16[128,32,256]{0,2,1:T(8,128)(2,1)}), bf16[128,32,256]{0,2,1:T(8,128)(2,1)}, u32[]{:S(2)}, u32[]{:S(2)}) async-start(bf16[128,32,256]{0,2,1:T(8,128)(2,1)} %bitcast.97), calls=%async_computation.2 | async-start | bytes 4194304 | tf_op jit(solution)/shard_map/all_to_all | solution.py:139
  80.3 102.7 %copy-start.16 = (u32[256]{0:T(256)S(1)}, u32[256]{0:T(256)}, u32[]{:S(2)}) copy-start(u32[256]{0:T(256)} %constant.64) | copy-start | bytes 3076
  80.3 104.1 %copy-start.15 = (s32[12]{0:T(128)S(1)}, s32[12]{0:T(128)}, u32[]{:S(2)}) copy-start(s32[12]{0:T(128)} %param.15) | copy-start | bytes 148
  80.3 116.6 %all-gather.3.cloned.1.call-start = ((), (), s32[]{:S(2)}) async-start(), calls=%async_computation.6 | async-start | bytes 1179648 | tf_op jit(solution)/shard_map/all_gather | solution.py:17
  81.1 117.4 %copy-start.14 = (s32[128]{0:T(128)S(1)}, s32[128]{0:T(128)}, u32[]{:S(2)}) copy-start(s32[128]{0:T(128)} %param.14) | copy-start | bytes 1540
  183.0 31.9 %copy-start.5 = (bf16[384,1024]{1,0:T(8,128)(2,1)}, bf16[384,1024]{1,0:T(8,128)(2,1)S(1)}, u32[]{:S(2)}) copy-start(bf16[384,1024]{1,0:T(8,128)(2,1)S(1)} %reshape.103) | copy-start | bytes 2359300
  199.1 19.9 %all-to-all-start.1 = ((s32[32,1,128]{2,1,0:T(1,128)}), s32[32,1,128]{2,1,0:T(1,128)}, u32[]{:S(2)}, u32[]{:S(2)}) async-start(s32[32,1,128]{2,1,0:T(1,128)} %broadcast_in_dim.41), calls=%async_computation.1 | async-start | bytes 32768 | tf_op jit(solution)/shard_map/all_to_all | solution.py:22
  219.0 6.3 %copy-start.2 = (bf16[4096,256]{1,0:T(8,128)(2,1)}, bf16[4096,256]{1,0:T(8,128)(2,1)S(1)}, u32[]{:S(2)}) copy-start(bf16[4096,256]{1,0:T(8,128)(2,1)S(1)} %get-tuple-element.377) | copy-start | bytes 6291460 | tf_op jit(solution)/shard_map/while/body/eval_jaxpr/while
  227.9 2.6 copy-start.1
  227.9 2.6 copy-start.10
  231.0 1.0 copy-start
  232.1 0.9 copy-start.7
  233.0 1.6 copy-start.3
  234.6 6.3 %copy-start.2 = (bf16[4096,256]{1,0:T(8,128)(2,1)}, bf16[4096,256]{1,0:T(8,128)(2,1)S(1)}, u32[]{:S(2)}) copy-start(bf16[4096,256]{1,0:T(8,128)(2,1)S(1)} %get-tuple-element.377) | copy-start | bytes 6291460 | tf_op jit(solution)/shard_map/while/body/eval_jaxpr/while
  243.4 2.7 copy-start.1
  243.4 2.7 copy-start.10
  246.7 1.0 copy-start
  247.7 0.9 copy-start.7
  248.7 1.6 copy-start.3
  250.3 6.3 %copy-start.2 = (bf16[4096,256]{1,0:T(8,128)(2,1)}, bf16[4096,256]{1,0:T(8,128)(2,1)S(1)}, u32[]{:S(2)}) copy-start(bf16[4096,256]{1,0:T(8,128)(2,1)S(1)} %get-tuple-element.377) | copy-start | bytes 6291460 | tf_op jit(solution)/shard_map/while/body/eval_jaxpr/while
  259.1 2.7 copy-start.1
  259.1 2.7 copy-start.10
  262.4 1.0 copy-start
  263.4 0.9 copy-start.7
  264.3 1.6 copy-start.3
  265.9 6.3 %copy-start.2 = (bf16[4096,256]{1,0:T(8,128)(2,1)}, bf16[4096,256]{1,0:T(8,128)(2,1)S(1)}, u32[]{:S(2)}) copy-start(bf16[4096,256]{1,0:T(8,128)(2,1)S(1)} %get-tuple-element.377) | copy-start | bytes 6291460 | tf_op jit(solution)/shard_map/while/body/eval_jaxpr/while
  274.8 2.7 copy-start.1
  274.8 2.7 copy-start.10
  278.0 1.0 copy-start
  279.1 0.9 copy-start.7
  280.0 1.6 copy-start.3
  281.6 2.6 copy-start.9
  324.6 4.6 %copy-start.6 = (bf16[384,1024]{1,0:T(8,128)(2,1)S(1)}, bf16[384,1024]{1,0:T(8,128)(2,1)}, u32[]{:S(2)}) copy-start(bf16[384,1024]{1,0:T(8,128)(2,1)} %copy-done.5) | copy-start | bytes 2359300
  324.6 76.6 %all-to-all-start.3 = ((bf16[32,128,256]{2,1,0:T(8,128)(2,1)}), bf16[32,128,256]{2,1,0:T(8,128)(2,1)S(1)}, u32[]{:S(2)}, u32[]{:S(2)}) async-start(bf16[32,128,256]{2,1,0:T(8,128)(2,1)} %bitcast.102), calls=%async_computation.3 | async-start | bytes 4194304 | tf_op jit(solution)/shard_map/all_to_all | solution.py:145
  329.1 69.4 %reduce-scatter.4.cloned.1.call-start = ((), (), s32[]{:S(2)}) async-start(), calls=%async_computation.7 | async-start | bytes 1179648
  331.1 2.4 copy-start.8
Sparse Core Ops, SparseCore 0:
  83.5 68.7 all-gather.2
  333.6 64.8 reduce-scatter.3
where the time goes:
time: 419 us; the launch traced here: 415 us
  blocking collectives  154 us (37%)
  waiting for transfers between devices  112 us (27%)
  local copies, waits for them, and re-layouts  56.4 us (13%)
  matrix products  33.8 us (8%)
  starting transfers between devices  30.3 us (7%)
  between operations  15 us (4%)
  other arithmetic  11.1 us (3%)
    all_gather x1, blocking collectives, body(): lax.all_gather(enc_states, 'ctx', axis=0, tiled=True)  102 us
    unnamed x3, waiting for transfers between devices  64.2 us
    all_to_all x1, waiting for transfers between devices, body(): lax.all_to_all(queries, 'ctx', split_axis=1, concat_axis=0, tiled=True)  47.3 us
    all_to_all x1, blocking collectives, sum_at_owner(): lax.all_to_all(pieces, axis, split_axis=0, concat_axis=0, tiled=True)  39.8 us
    unnamed x35, local copies, waits for them, and re-layouts  19.7 us
    unnamed x1, blocking collectives  12.3 us
    all_to_all x1, starting transfers between devices, body(): lax.all_to_all(queries, 'ctx', split_axis=1, concat_axis=0, tiled=True)  11.5 us
    dot_general x4, matrix products, query_block(): jnp.einsum('hqk,qhd->khd', rounded, grad_part, preferred_element_type=jnp...  10.5 us
  transfers between devices with their start and end apart: 6, of which 2 were waited for; matrix products, arithmetic and copies ran while one was open for 6% of the time, Pallas kernels for 0%

commit v1 on v0

v1 whole, which is shorter than its diff:
```python
import functools

import jax
import jax.numpy as jnp
from jax import lax
from jax.experimental import pallas as pl
from jax.experimental.pallas import tpu as pltpu
from jax.sharding import PartitionSpec as P

HEAD_DIM = 128
NY, NZ, NC = 4, 4, 2
NX, NL = 4, 2
PEERS = NY * NC
ROWS = 128
KEYS = 384
ENC_ROWS = 12
FEATURES = 256
SHARED_Z = [[(y * NZ + z) * NC + c for y in range(NY) for c in range(NC)] for z in range(NZ)]
GROUPS = ((1, 3), (2, 0))
BF16, F32 = jnp.bfloat16, jnp.float32


def place():
    me = lax.axis_index("ctx")
    return me // (NZ * NC), (me // NC) % NZ, me % NC


def shift(value, dy=0, dz=0, dc=0):
    pairs = [
        ((y * NZ + z) * NC + c, (((y + dy) % NY) * NZ + (z + dz) % NZ) * NC + (c + dc) % NC)
        for y in range(NY)
        for z in range(NZ)
        for c in range(NC)
    ]
    return lax.ppermute(value, "ctx", pairs)


def by_owner(mine, arrived, me):
    blocks = [mine, *arrived]
    n = len(blocks)
    return jnp.stack([lax.select_n((owner - me) % n, *blocks) for owner in range(n)])


def gather_encoder(block):
    y, z, c = place()
    along_z = by_owner(block, [shift(block, dz=-d) for d in range(1, NZ)], z)
    along_y = by_owner(along_z, [shift(along_z, dy=-d) for d in range(1, NY)], y)
    other = shift(along_y, dc=1)
    first = c == 0
    both = jnp.stack([jnp.where(first, along_y, other), jnp.where(first, other, along_y)], axis=2)
    return both.reshape(NY * NZ * NC, *block.shape)


def sum_encoder(part):
    y, z, c = place()

    def at(value, index, axis):
        return lax.dynamic_index_in_dim(value, index, axis, keepdims=False)

    arrived = shift(at(part, 1 - c, 2), dc=1)
    total = (at(part, c, 2).astype(F32) + arrived.astype(F32)).astype(BF16)
    arrived = [shift(at(total, (y + d) % NY, 0), dy=d) for d in range(1, NY)]
    total = sum((a.astype(F32) for a in arrived), at(total, y, 0).astype(F32)).astype(BF16)
    arrived = [shift(at(total, (z + d) % NZ, 0), dz=d) for d in range(1, NZ)]
    return sum((a.astype(F32) for a in arrived), at(total, z, 0).astype(F32)).astype(BF16)


def columns_of(owner_y, distance, owner_c):
    z = lax.rem(lax.div(lax.axis_index("ctx"), NC), NZ)
    block = (owner_y * NZ + lax.rem(z + distance, NZ)) * NC + owner_c
    return pl.ds(pl.multiple_of(block * FEATURES, FEATURES), FEATURES)


def pack_kernel(group, queries, grads, out, sems):
    copies = []
    for peer in range(PEERS):
        for which, source in enumerate((queries, grads)):
            for i, distance in enumerate(group):
                copies.append(
                    pltpu.make_async_copy(
                        source.at[:, columns_of(peer // NC, distance, peer % NC)],
                        out.at[peer, which, :, pl.ds(i * FEATURES, FEATURES)],
                        sems.at[len(copies)],
                    )
                )
    for copy in copies:
        copy.start()
    for copy in copies:
        copy.wait()


def pack(group, queries, grads):
    shape = (PEERS, 2, ROWS, len(group) * FEATURES)
    return pl.pallas_call(
        functools.partial(pack_kernel, group),
        out_shape=jax.ShapeDtypeStruct(shape, BF16),
        in_specs=[pl.BlockSpec(memory_space=pl.ANY)] * 2,
        out_specs=pl.BlockSpec(memory_space=pl.ANY),
        scratch_shapes=[pltpu.SemaphoreType.DMA((PEERS * 2 * len(group),))],
        cost_estimate=pl.CostEstimate(flops=0, bytes_accessed=4 * PEERS * 2 * ROWS * len(group) * FEATURES, transcendentals=0),
    )(queries, grads)


def unpack_kernel(*refs):
    arrived, out, sems = refs[:-2], refs[-2], refs[-1]
    copies = []
    for group, source in zip(GROUPS, arrived, strict=True):
        for peer in range(PEERS):
            for i, distance in enumerate(group):
                copies.append(
                    pltpu.make_async_copy(
                        source.at[peer, :, pl.ds(i * FEATURES, FEATURES)],
                        out.at[:, columns_of(peer // NC, distance, peer % NC)],
                        sems.at[len(copies)],
                    )
                )
    for copy in copies:
        copy.start()
    for copy in copies:
        copy.wait()


def unpack(arrived):
    width = PEERS * NZ * FEATURES
    return pl.pallas_call(
        unpack_kernel,
        out_shape=jax.ShapeDtypeStruct((ROWS, width), BF16),
        in_specs=[pl.BlockSpec(memory_space=pl.ANY)] * len(arrived),
        out_specs=pl.BlockSpec(memory_space=pl.ANY),
        scratch_shapes=[pltpu.SemaphoreType.DMA((PEERS * NZ,))],
        cost_estimate=pl.CostEstimate(flops=0, bytes_accessed=4 * ROWS * width, transcendentals=0),
    )(*arrived)


def attend_kernel(ends, rows, key, value, query_grad, key_grad, value_grad, bias):
    tile = NC * ROWS

    @pl.when(pl.program_id(0) == 0)
    def _():
        z = lax.rem(lax.div(lax.axis_index("ctx"), NC), NZ)
        keys_at = lax.broadcasted_iota(jnp.int32, (KEYS, tile), 0)
        for y in range(NY):
            token = (y * NZ + z) * tile + lax.broadcasted_iota(jnp.int32, (1, tile), 1)
            low = jnp.zeros((1, tile), jnp.int32)
            high = jnp.full((1, tile), ends[0], jnp.int32)
            for d in range(3):
                past = token >= ends[3 + d]
                low = jnp.where(past, ends[d], low)
                high = jnp.where(past, ends[d + 1] if d < 2 else KEYS, high)
            allowed = (keys_at >= low) & (keys_at < high)
            bias[:, pl.ds(y * tile, tile)] = jnp.where(allowed, 0.0, -jnp.inf)

    keys, values = key[0], value[0]
    keys_turned = keys.T
    key_total = jnp.zeros((KEYS, HEAD_DIM), F32)
    value_total = jnp.zeros((KEYS, HEAD_DIM), F32)
    last = (((1,), (1,)), ((), ()))
    for y in range(NY):
        query = rows[pl.ds(y * NC, NC), 0].reshape(tile, HEAD_DIM)
        grad = rows[pl.ds(y * NC, NC), 1].reshape(tile, HEAD_DIM)
        scores = lax.dot_general(keys, query, last, preferred_element_type=F32)
        scores = scores + bias[:, pl.ds(y * tile, tile)]
        weights = jnp.exp(scores - jnp.max(scores, axis=0, keepdims=True))
        probability = weights * (1.0 / jnp.sum(weights, axis=0, keepdims=True))
        upstream = lax.dot_general(values, grad, last, preferred_element_type=F32)
        row_dot = jnp.sum(probability * upstream, axis=0, keepdims=True)
        score_grad = (probability * (upstream - row_dot)).astype(BF16)
        rounded = probability.astype(BF16)
        key_total += jnp.dot(score_grad, query, preferred_element_type=F32)
        value_total += jnp.dot(rounded, grad, preferred_element_type=F32)
        turned = jnp.dot(keys_turned, score_grad, preferred_element_type=F32)
        query_grad[pl.ds(y * NC, NC)] = turned.T.astype(BF16).reshape(NC, ROWS, HEAD_DIM)
    key_grad[0] = key_total.astype(BF16)
    value_grad[0] = value_total.astype(BF16)


def attend(ends, rows, key_values):
    count = key_values.shape[0]
    heads = FEATURES // HEAD_DIM
    elements = count * heads * PEERS * ROWS * KEYS
    block = (1, KEYS, HEAD_DIM)
    in_block = lambda h, ends: (h // heads, 0, h % heads)
    grads = jax.ShapeDtypeStruct((count, KEYS, FEATURES), BF16)
    return pl.pallas_call(
        attend_kernel,
        out_shape=(jax.ShapeDtypeStruct((PEERS, ROWS, count * FEATURES), BF16), grads, grads),
        grid_spec=pltpu.PrefetchScalarGridSpec(
            num_scalar_prefetch=1,
            grid=(count * heads,),
            in_specs=[
                pl.BlockSpec((PEERS, 2, ROWS, HEAD_DIM), lambda h, ends: (0, 0, 0, h)),
                pl.BlockSpec(block, in_block),
                pl.BlockSpec(block, lambda h, ends: (h // heads, 0, heads + h % heads)),
            ],
            out_specs=(
                pl.BlockSpec((PEERS, ROWS, HEAD_DIM), lambda h, ends: (0, 0, h)),
                pl.BlockSpec(block, in_block),
                pl.BlockSpec(block, in_block),
            ),
            scratch_shapes=[pltpu.VMEM((KEYS, PEERS * ROWS), F32)],
        ),
        compiler_params=pltpu.CompilerParams(vmem_limit_bytes=24 * 2**20),
        cost_estimate=pl.CostEstimate(
            flops=elements * HEAD_DIM * 10, bytes_accessed=6 * 2**20, transcendentals=elements
        ),
    )(ends, rows, key_values, key_values)


def body(queries, out_grad, enc_states, w_key, w_value, dec_segments, enc_segments):
    below = [jnp.sum(ids < d) for ids in (enc_segments, dec_segments) for d in range(1, 4)]
    counts = jnp.stack(below).astype(BF16)
    last_rows = jnp.pad(counts[None], ((0, 3), (0, enc_states.shape[1] - 6)))
    gathered = gather_encoder(jnp.concatenate([enc_states, last_rows], axis=0))
    encoder = gathered[:, :ENC_ROWS].reshape(KEYS, -1)
    ends = jnp.sum(gathered[:, ENC_ROWS, :6].astype(jnp.int32), axis=0)

    own_weight = jnp.concatenate([w_key, w_value], axis=1)
    copies = jnp.broadcast_to(own_weight[None], (NX * NL, *own_weight.shape))
    weight = lax.all_to_all(copies, "dp", 0, 0, tiled=True).reshape(-1, 2 * FEATURES)

    swap = functools.partial(
        lax.all_to_all,
        axis_name="ctx",
        split_axis=0,
        concat_axis=0,
        axis_index_groups=SHARED_Z,
        tiled=True,
    )
    rows = [swap(pack(group, queries, out_grad)) for group in GROUPS]

    own = jnp.dot(encoder, weight, preferred_element_type=F32).astype(BF16)
    key_values = {d: shift(own, dz=-d) if d else own for group in GROUPS for d in group}

    total, returned = 0.0, []
    for group, arrived in zip(GROUPS, rows, strict=True):
        query_grad, key_grad, value_grad = attend(
            ends, arrived, jnp.stack([key_values[d] for d in group])
        )
        returned.append(swap(query_grad))
        for i, d in enumerate(group):
            term = jnp.concatenate([key_grad[i], value_grad[i]], axis=1)
            total = total + (shift(term, dz=d) if d else term).astype(F32)
    query_grad = unpack(returned)

    rounded = total.astype(BF16)
    part = lax.dot_general(rounded, weight, (((1,), (1,)), ((), ())), preferred_element_type=F32)
    enc_grad = sum_encoder(part.astype(BF16).reshape(NY, NZ, NC, ENC_ROWS, -1))

    term = lax.dot_general(encoder, rounded, (((0,), (0,)), ((), ())), preferred_element_type=F32)
    pieces = term.astype(BF16).reshape(NX * NL, -1, 2 * FEATURES)
    pieces = lax.all_to_all(pieces, "dp", 0, 0, tiled=True)
    weight_grad = pieces.astype(F32).sum(axis=0)
    return query_grad, enc_grad, weight_grad[:, :FEATURES], weight_grad[:, FEATURES:]


def solution(mesh):
    tokens, weights, ids = P(("dp", "ctx"), None), P("dp", "ctx"), P(("dp", "ctx"))
    return jax.shard_map(
        body,
        mesh=mesh,
        in_specs=(tokens, tokens, tokens, weights, weights, ids, ids),
        out_specs=(tokens, tokens, weights, weights),
        check_vma=False,
    )
```

time: 419 us -> 419 us (level)
  Pallas kernels: 0 us -> 218 us
  blocking collectives: 154 us -> 0 us
  local copies, waits for them, and re-layouts: 56.4 us -> 6.03 us
  starting transfers between devices: 30.3 us -> 66.1 us
  matrix products: 33.8 us -> 6.46 us
  between operations: 15 us -> 4.91 us
  other arithmetic: 11.1 us -> 6.17 us
    pallas_call x0 -> x5, Pallas kernels: none -> 218 us  [the longest x2 130 us: pack(): pl.pallas_call(functools.partial(pack_kernel, group), out_shape=jax.Shape...]
    all_gather x1 -> x0, blocking collectives: 102 us -> none  [body(): lax.all_gather(enc_states, 'ctx', axis=0, tiled=True)]
    ppermute x0 -> x20, waiting for transfers between devices: none -> 84.2 us  [shift(): return lax.ppermute(value, 'ctx', pairs)]
    unnamed x3 -> x0, waiting for transfers between devices: 64.2 us -> none
    all_to_all x1 -> x0, blocking collectives: 39.8 us -> none  [sum_at_owner(): lax.all_to_all(pieces, axis, split_axis=0, concat_axis=0, tiled=True)]
    ppermute x0 -> x20, starting transfers between devices: none -> 35.8 us  [shift(): return lax.ppermute(value, 'ctx', pairs)]
    all_to_all x4 -> x6, waiting for transfers between devices: 47.3 us -> 27.1 us  [the longest x2 27.1 us: body(): rows = [swap(pack(group, queries, out_grad)) for group in GROUPS]]
    unnamed x35 -> x18, local copies, waits for them, and re-layouts: 19.7 us -> 1.61 us
  transfers between devices with their start and end apart: 6 -> 26, of which waited for: 2 -> 14; matrix products, arithmetic and copies ran while one was open for 6% -> 4% of each run, Pallas kernels for 0% -> 36%
where the time goes in v1:
time: 419 us
  Pallas kernels  218 us (52%)
  waiting for transfers between devices  111 us (26%)
  starting transfers between devices  66.1 us (16%)
  matrix products  6.46 us (2%)
  other arithmetic  6.17 us (1%)
  local copies, waits for them, and re-layouts  6.03 us (1%)
  between operations  4.91 us (1%)
    pallas_call x2, Pallas kernels, pack(): pl.pallas_call(functools.partial(pack_kernel, group), out_shape=jax.Shape...  130 us
    ppermute x20, waiting for transfers between devices, shift(): return lax.ppermute(value, 'ctx', pairs)  84.2 us
    pallas_call x1, Pallas kernels, unpack(): pl.pallas_call(unpack_kernel, out_shape=jax.ShapeDtypeStruct((ROWS, width...  64.9 us
    ppermute x20, starting transfers between devices, shift(): return lax.ppermute(value, 'ctx', pairs)  35.8 us
    all_to_all x2, waiting for transfers between devices, body(): rows = [swap(pack(group, queries, out_grad)) for group in GROUPS]  27.1 us
    pallas_call x2, Pallas kernels, attend(): pl.pallas_call(attend_kernel, out_shape=(jax.ShapeDtypeStruct((PEERS, ROW...  22.8 us
    all_to_all x2, starting transfers between devices, body(): returned.append(swap(query_grad))  9.14 us
    all_to_all x2, starting transfers between devices, body(): rows = [swap(pack(group, queries, out_grad)) for group in GROUPS]  8.98 us
  transfers between devices with their start and end apart: 26, of which 14 were waited for; matrix products, arithmetic and copies ran while one was open for 4% of the time, Pallas kernels for 36%

profile of v1, /device:TPU:2, one launch (start us, length us, event | category | flops | bytes accessed | tf_op | source)
XLA Modules:
  0.0 418.7 jit_solution(2121295836727606026)
XLA Ops:
  0.6 64.9 %shard_map.102 = bf16[8,2,128,512]{3,2,1,0:T(8,128)(2,1)} custom-call(bf16[128,8192]{1,0:T(8,128)(2,1)} %queries.3, bf16[128,8192]{1,0:T(8,128)(2,1)} %grads.3), custom_call_target="tpu_custom_call" | custom-call | bytes 4194304 | tf_op jit(solution)/shard_map/pallas_call | solution.py:94
  65.6 4.6 %all-to-all-start = ((bf16[8,2,128,512]{3,2,1,0:T(8,128)(2,1)}), bf16[8,2,128,512]{3,2,1,0:T(8,128)(2,1)S(1)}, u32[]{:S(2)}, u32[]{:S(2)}) async-start(bf16[8,2,128,512]{3,2,1,0:T(8,128)(2,1)} %shard_map.102), calls=%async_computation | async-start | bytes 4194304 | tf_op jit(solution)/shard_map/all_to_all | solution.py:229
  70.3 27.1 %all-to-all-done.rows = bf16[8,2,128,512]{3,2,1,0:T(8,128)(2,1)S(1)} async-done(((bf16[8,2,128,512]{3,2,1,0:T(8,128)(2,1)}), bf16[8,2,128,512]{3,2,1,0:T(8,128)(2,1)S(1)}, u32[]{:S(2)}, u32[]{:S(2)}) %all-to-all-start) | async-done | bytes 2097184 | tf_op jit(solution)/shard_map/all_to_all | solution.py:229
  97.4 1.1 broadcast_in_dim.2
  98.5 6.2 %all-to-all-start.1 = ((bf16[8,128,512]{2,1,0:T(8,128)(2,1)}), bf16[8,128,512]{2,1,0:T(8,128)(2,1)}, u32[]{:S(2)}, u32[]{:S(2)}) async-start(bf16[8,128,512]{2,1,0:T(8,128)(2,1)} %broadcast_in_dim.2), calls=%async_computation.1 | async-start | bytes 2097152 | tf_op jit(solution)/shard_map/all_to_all | solution.py:219
  110.1 6.4 %collective-permute-start.1 = (bf16[16,1024]{1,0:T(8,128)(2,1)S(1)}, bf16[16,1024]{1,0:T(8,128)(2,1)S(1)}, u32[]{:S(2)}, u32[]{:S(2)}) collective-permute-start(bf16[16,1024]{1,0:T(8,128)(2,1)S(1)} %fusion.8), channel_id=1, source_target_pairs={{0,4},{1,5},{2,6},{3,7},{4,0},{5,1},{6,2},{7,3},{8,12},{9,13},{10,... | collective-permute-start | bytes 98312 | tf_op jit(solution)/shard_map/ppermute | solution.py:35
  116.4 1.5 collective-permute-start.2
  117.9 2.7 collective-permute-start
  120.6 4.2 %collective-permute-done.1 = bf16[16,1024]{1,0:T(8,128)(2,1)S(1)} collective-permute-done((bf16[16,1024]{1,0:T(8,128)(2,1)S(1)}, bf16[16,1024]{1,0:T(8,128)(2,1)S(1)}, u32[]{:S(2)}, u32[]{:S(2)}) %collective-permute-start.1) | collective-permute-done | bytes 32800 | tf_op jit(solution)/shard_map/ppermute | solution.py:35
  125.6 1.4 collective-permute-start.5
  127.0 1.9 collective-permute-start.3
  128.9 2.7 collective-permute-done.4
  131.5 1.3 collective-permute-done.5
  132.9 0.9 pad_maximum_fusion.3
  133.8 64.9 %shard_map.104 = bf16[8,2,128,512]{3,2,1,0:T(8,128)(2,1)} custom-call(bf16[128,8192]{1,0:T(8,128)(2,1)} %queries.3, bf16[128,8192]{1,0:T(8,128)(2,1)} %grads.3), custom_call_target="tpu_custom_call" | custom-call | bytes 4194304 | tf_op jit(solution)/shard_map/pallas_call | solution.py:94
  198.8 4.4 %all-to-all-start.3 = ((bf16[8,2,128,512]{3,2,1,0:T(8,128)(2,1)}), bf16[8,2,128,512]{3,2,1,0:T(8,128)(2,1)}, u32[]{:S(2)}, u32[]{:S(2)}) async-start(bf16[8,2,128,512]{3,2,1,0:T(8,128)(2,1)} %shard_map.104), calls=%async_computation.3 | async-start | bytes 4194304 | tf_op jit(solution)/shard_map/all_to_all | solution.py:229
  203.4 1.1 reshape.125
  204.4 2.0 convolution_convert_fusion.2
  206.5 1.2 collective-permute-start.8
  207.7 3.0 collective-permute-start.7
  211.4 10.4 %collective-permute-done.8 = bf16[384,512]{1,0:T(8,128)(2,1)S(1)} collective-permute-done((bf16[384,512]{1,0:T(8,128)(2,1)S(1)}, bf16[384,512]{1,0:T(8,128)(2,1)S(1)}, u32[]{:S(2)}, u32[]{:S(2)}) %collective-permute-start.8) | collective-permute-done | bytes 393248 | tf_op jit(solution)/shard_map/ppermute | solution.py:35
  221.8 22.9 %collective-permute-done.7 = bf16[384,512]{1,0:T(8,128)(2,1)S(1)} collective-permute-done((bf16[384,512]{1,0:T(8,128)(2,1)S(1)}, bf16[384,512]{1,0:T(8,128)(2,1)S(1)}, u32[]{:S(2)}, u32[]{:S(2)}) %collective-permute-start.7) | collective-permute-done | bytes 393248 | tf_op jit(solution)/shard_map/ppermute | solution.py:35
  245.0 11.2 %shard_map.103 = (bf16[8,128,512]{2,1,0:T(8,128)(2,1)}, bf16[2,384,256]{2,1,0:T(8,128)(2,1)S(1)}, bf16[2,384,256]{2,1,0:T(8,128)(2,1)S(1)}) custom-call(s32[6]{0:T(128)S(1)} %fusion.9.ends, bf16[8,2,128,512]{3,2,1,0:T(8,128)(2,1)S(1)} %all-to-all-done.rows, bf16[2,384,512]{2,1,0:T(8,128)(2,1)S(1)} %pad_maximum_fusion.1.key.value, ...), custom_call_target="tpu_custom_call" | custom-call | flops 2013265920 | bytes 6291456 | tf_op jit(solution)/shard_map/pallas_call | solution.py:184
  256.9 4.4 %all-to-all-start.2 = ((bf16[8,128,512]{2,1,0:T(8,128)(2,1)}), bf16[8,128,512]{2,1,0:T(8,128)(2,1)}, u32[]{:S(2)}, u32[]{:S(2)}) async-start(bf16[8,128,512]{2,1,0:T(8,128)(2,1)} %get-tuple-element.10), calls=%async_computation.2 | async-start | bytes 2097152 | tf_op jit(solution)/shard_map/all_to_all | solution.py:239
  261.3 11.7 %shard_map.105 = (bf16[8,128,512]{2,1,0:T(8,128)(2,1)}, bf16[2,384,256]{2,1,0:T(8,128)(2,1)S(1)}, bf16[2,384,256]{2,1,0:T(8,128)(2,1)S(1)}) custom-call(s32[6]{0:T(128)S(1)} %fusion.9.ends, bf16[8,2,128,512]{3,2,1,0:T(8,128)(2,1)} %all-to-all-done.3.rows, bf16[2,384,512]{2,1,0:T(8,128)(2,1)S(1)} %pad_maximum_fusion.2.key.value, ...), custom_call_target="tpu_custom_call" | custom-call | flops 2013265920 | bytes 6291456 | tf_op jit(solution)/shard_map/pallas_call | solution.py:184
  273.2 0.8 copy-done.1
  274.1 4.6 %collective-permute-start.11 = (bf16[384,512]{1,0:T(8,128)(2,1)S(1)}, bf16[384,512]{1,0:T(8,128)(2,1)}, u32[]{:S(2)}, u32[]{:S(2)}) collective-permute-start(bf16[384,512]{1,0:T(8,128)(2,1)S(1)} %pad_maximum_fusion.5), channel_id=1, source_target_pairs={{0,6},{1,7},{2,0},{3,1},{4,2},{5,3},{6,4},{7,5},{8,14},{9,15},{10,... | collective-permute-start | bytes 1179656 | tf_op jit(solution)/shard_map/ppermute | solution.py:35
  279.5 1.6 collective-permute-start.10
  281.1 4.7 %all-to-all-start.4 = ((bf16[8,128,512]{2,1,0:T(8,128)(2,1)}), bf16[8,128,512]{2,1,0:T(8,128)(2,1)S(1)}, u32[]{:S(2)}, u32[]{:S(2)}) async-start(bf16[8,128,512]{2,1,0:T(8,128)(2,1)} %get-tuple-element.11), calls=%async_computation.4 | async-start | bytes 2097152 | tf_op jit(solution)/shard_map/all_to_all | solution.py:239
  285.8 11.9 %collective-permute-done.12 = bf16[384,512]{1,0:T(8,128)(2,1)} collective-permute-done((bf16[384,512]{1,0:T(8,128)(2,1)S(1)}, bf16[384,512]{1,0:T(8,128)(2,1)}, u32[]{:S(2)}, u32[]{:S(2)}) %collective-permute-start.12) | collective-permute-done | bytes 393248 | tf_op jit(solution)/shard_map/ppermute | solution.py:35
  297.7 14.8 %collective-permute-done.11 = bf16[384,512]{1,0:T(8,128)(2,1)} collective-permute-done((bf16[384,512]{1,0:T(8,128)(2,1)S(1)}, bf16[384,512]{1,0:T(8,128)(2,1)}, u32[]{:S(2)}, u32[]{:S(2)}) %collective-permute-start.11) | collective-permute-done | bytes 393248 | tf_op jit(solution)/shard_map/ppermute | solution.py:35
  312.5 1.4 add_convert_fusion
  314.0 1.7 convolution_convert_fusion
  315.7 6.0 %all-to-all-start.5 = ((bf16[8,128,512]{2,1,0:T(8,128)(2,1)}), bf16[8,128,512]{2,1,0:T(8,128)(2,1)S(1)}, u32[]{:S(2)}, u32[]{:S(2)}) async-start(bf16[8,128,512]{2,1,0:T(8,128)(2,1)} %bitcast.41), calls=%async_computation.5 | async-start | bytes 2097152 | tf_op jit(solution)/shard_map/all_to_all | solution.py:251
  321.7 2.7 convolution_convert_fusion.1
  324.4 1.3 reshape.127
  325.9 1.8 collective-permute-done.13
  328.0 2.9 collective-permute-start.16
  330.9 0.9 collective-permute-start.15
  331.8 0.9 collective-permute-start.14
  332.6 4.1 collective-permute-done.16
  336.8 2.0 collective-permute-done.15
  338.8 1.7 collective-permute-done.14
  340.6 2.4 collective-permute-start.19
  343.0 3.0 collective-permute-start.18
  346.0 5.0 %collective-permute-done.18 = bf16[12,1024]{1,0:T(8,128)(2,1)S(1)} collective-permute-done((bf16[12,1024]{1,0:T(8,128)(2,1)S(1)}, bf16[12,1024]{1,0:T(8,128)(2,1)S(1)}, u32[]{:S(2)}, u32[]{:S(2)}) %collective-permute-start.18) | collective-permute-done | bytes 24608 | tf_op jit(solution)/shard_map/ppermute | solution.py:35
  351.0 1.3 collective-permute-done.17
  352.9 64.9 %shard_map.106 = bf16[128,8192]{1,0:T(8,128)(2,1)} custom-call(bf16[8,128,512]{2,1,0:T(8,128)(2,1)} %all-to-all-done.2.refs_0_, bf16[8,128,512]{2,1,0:T(8,128)(2,1)} %copy-done.2), custom_call_target="tpu_custom_call" | custom-call | bytes 4194304 | tf_op jit(solution)/shard_map/pallas_call | solution.py:125
  (62 shorter events, 7.3 us)
Async XLA Ops:
  65.6 4.6 %copy-start.5 = (bf16[128,256]{1,0:T(8,128)(2,1)S(1)}, bf16[128,256]{1,0:T(8,128)(2,1)}, u32[]{:S(2)}) copy-start(bf16[128,256]{1,0:T(8,128)(2,1)} %param.11) | copy-start | bytes 196612
  65.6 4.6 %copy-start.6 = (bf16[128,256]{1,0:T(8,128)(2,1)S(1)}, bf16[128,256]{1,0:T(8,128)(2,1)}, u32[]{:S(2)}) copy-start(bf16[128,256]{1,0:T(8,128)(2,1)} %param.10) | copy-start | bytes 196612
  65.6 31.8 %all-to-all-start = ((bf16[8,2,128,512]{3,2,1,0:T(8,128)(2,1)}), bf16[8,2,128,512]{3,2,1,0:T(8,128)(2,1)S(1)}, u32[]{:S(2)}, u32[]{:S(2)}) async-start(bf16[8,2,128,512]{3,2,1,0:T(8,128)(2,1)} %shard_map.102), calls=%async_computation | async-start | bytes 4194304 | tf_op jit(solution)/shard_map/all_to_all | solution.py:229
  70.2 34.5 %copy-start.7 = (s32[12]{0:T(128)S(1)}, s32[12]{0:T(128)}, u32[]{:S(2)}) copy-start(s32[12]{0:T(128)} %param.13) | copy-start | bytes 148
  70.2 37.1 %copy-start.8 = (s32[128]{0:T(128)S(1)}, s32[128]{0:T(128)}, u32[]{:S(2)}) copy-start(s32[128]{0:T(128)} %param.12) | copy-start | bytes 1540
  70.2 39.8 %copy-start.4 = (bf16[12,1024]{1,0:T(8,128)(2,1)S(1)}, bf16[12,1024]{1,0:T(8,128)(2,1)}, u32[]{:S(2)}) copy-start(bf16[12,1024]{1,0:T(8,128)(2,1)} %param.9) | copy-start | bytes 73732
  98.5 100.3 %all-to-all-start.1 = ((bf16[8,128,512]{2,1,0:T(8,128)(2,1)}), bf16[8,128,512]{2,1,0:T(8,128)(2,1)}, u32[]{:S(2)}, u32[]{:S(2)}) async-start(bf16[8,128,512]{2,1,0:T(8,128)(2,1)} %broadcast_in_dim.2), calls=%async_computation.1 | async-start | bytes 2097152 | tf_op jit(solution)/shard_map/all_to_all | solution.py:219
  110.1 14.7 %collective-permute-start.1 = (bf16[16,1024]{1,0:T(8,128)(2,1)S(1)}, bf16[16,1024]{1,0:T(8,128)(2,1)S(1)}, u32[]{:S(2)}, u32[]{:S(2)}) collective-permute-start(bf16[16,1024]{1,0:T(8,128)(2,1)S(1)} %fusion.8), channel_id=1, source_target_pairs={{0,4},{1,5},{2,6},{3,7},{4,0},{5,1},{6,2},{7,3},{8,12},{9,13},{10,... | collective-permute-start | bytes 98312 | tf_op jit(solution)/shard_map/ppermute | solution.py:35
  116.4 8.4 %collective-permute-start.2 = (bf16[16,1024]{1,0:T(8,128)(2,1)S(1)}, bf16[16,1024]{1,0:T(8,128)(2,1)S(1)}, u32[]{:S(2)}, u32[]{:S(2)}) collective-permute-start(bf16[16,1024]{1,0:T(8,128)(2,1)S(1)} %fusion.8), channel_id=1, source_target_pairs={{0,2},{1,3},{2,4},{3,5},{4,6},{5,7},{6,0},{7,1},{8,10},{9,11},{10,... | collective-permute-start | bytes 98312 | tf_op jit(solution)/shard_map/ppermute | solution.py:35
  117.9 6.9 %collective-permute-start = (bf16[16,1024]{1,0:T(8,128)(2,1)S(1)}, bf16[16,1024]{1,0:T(8,128)(2,1)S(1)}, u32[]{:S(2)}, u32[]{:S(2)}) collective-permute-start(bf16[16,1024]{1,0:T(8,128)(2,1)S(1)} %fusion.8), channel_id=1, source_target_pairs={{0,6},{1,7},{2,0},{3,1},{4,2},{5,3},{6,4},{7,5},{8,14},{9,15},{10,... | collective-permute-start | bytes 98312 | tf_op jit(solution)/shard_map/ppermute | solution.py:35
  124.9 6.7 %collective-permute-start.4 = (bf16[4,16,1024]{2,1,0:T(8,128)(2,1)S(1)}, bf16[4,16,1024]{2,1,0:T(8,128)(2,1)S(1)}, u32[]{:S(2)}, u32[]{:S(2)}) collective-permute-start(bf16[4,16,1024]{2,1,0:T(8,128)(2,1)S(1)} %pad_maximum_fusion.7), channel_id=1, source_target_pairs={{0,16},{1,17},{2,18},{3,19},{4,20},{5,21},{6,22},{7,23},{8,24},{9,... | collective-permute-start | bytes 393224 | tf_op jit(solution)/shard_map/ppermute | solution.py:35
  125.6 7.2 %collective-permute-start.5 = (bf16[4,16,1024]{2,1,0:T(8,128)(2,1)S(1)}, bf16[4,16,1024]{2,1,0:T(8,128)(2,1)S(1)}, u32[]{:S(2)}, u32[]{:S(2)}) collective-permute-start(bf16[4,16,1024]{2,1,0:T(8,128)(2,1)S(1)} %pad_maximum_fusion.7), channel_id=1, source_target_pairs={{0,8},{1,9},{2,10},{3,11},{4,12},{5,13},{6,14},{7,15},{8,16},{9,17... | collective-permute-start | bytes 393224 | tf_op jit(solution)/shard_map/ppermute | solution.py:35
  127.0 5.9 %collective-permute-start.3 = (bf16[4,16,1024]{2,1,0:T(8,128)(2,1)S(1)}, bf16[4,16,1024]{2,1,0:T(8,128)(2,1)S(1)}, u32[]{:S(2)}, u32[]{:S(2)}) collective-permute-start(bf16[4,16,1024]{2,1,0:T(8,128)(2,1)S(1)} %pad_maximum_fusion.7), channel_id=1, source_target_pairs={{0,24},{1,25},{2,26},{3,27},{4,28},{5,29},{6,30},{7,31},{8,0},{9,1... | collective-permute-start | bytes 393224 | tf_op jit(solution)/shard_map/ppermute | solution.py:35
  133.8 69.3 %collective-permute-start.6 = (bf16[4,4,16,1024]{3,2,1,0:T(8,128)(2,1)}, bf16[4,4,16,1024]{3,2,1,0:T(8,128)(2,1)S(1)}, u32[]{:S(2)}, u32[]{:S(2)}) collective-permute-start(bf16[4,4,16,1024]{3,2,1,0:T(8,128)(2,1)} %pad_maximum_fusion.3), channel_id=1, source_target_pairs={{0,1},{1,0},{2,3},{3,2},{4,5},{5,4},{6,7},{7,6},{8,9},{9,8},{10,11... | collective-permute-start | bytes 1572872 | tf_op jit(solution)/shard_map/ppermute | solution.py:35
  198.8 58.1 %all-to-all-start.3 = ((bf16[8,2,128,512]{3,2,1,0:T(8,128)(2,1)}), bf16[8,2,128,512]{3,2,1,0:T(8,128)(2,1)}, u32[]{:S(2)}, u32[]{:S(2)}) async-start(bf16[8,2,128,512]{3,2,1,0:T(8,128)(2,1)} %shard_map.104), calls=%async_computation.3 | async-start | bytes 4194304 | tf_op jit(solution)/shard_map/all_to_all | solution.py:229
  206.5 15.4 %collective-permute-start.8 = (bf16[384,512]{1,0:T(8,128)(2,1)S(1)}, bf16[384,512]{1,0:T(8,128)(2,1)S(1)}, u32[]{:S(2)}, u32[]{:S(2)}) collective-permute-start(bf16[384,512]{1,0:T(8,128)(2,1)S(1)} %convolution_convert_fusion.2), channel_id=1, source_target_pairs={{0,2},{1,3},{2,4},{3,5},{4,6},{5,7},{6,0},{7,1},{8,10},{9,11},{10,... | collective-permute-start | bytes 1179656 | tf_op jit(solution)/shard_map/ppermute | solution.py:35
  207.7 37.1 %collective-permute-start.7 = (bf16[384,512]{1,0:T(8,128)(2,1)S(1)}, bf16[384,512]{1,0:T(8,128)(2,1)S(1)}, u32[]{:S(2)}, u32[]{:S(2)}) collective-permute-start(bf16[384,512]{1,0:T(8,128)(2,1)S(1)} %convolution_convert_fusion.2), channel_id=1, source_target_pairs={{0,6},{1,7},{2,0},{3,1},{4,2},{5,3},{6,4},{7,5},{8,14},{9,15},{10,... | collective-permute-start | bytes 1179656 | tf_op jit(solution)/shard_map/ppermute | solution.py:35
  210.7 34.2 %collective-permute-start.9 = (bf16[384,512]{1,0:T(8,128)(2,1)S(1)}, bf16[384,512]{1,0:T(8,128)(2,1)S(1)}, u32[]{:S(2)}, u32[]{:S(2)}) collective-permute-start(bf16[384,512]{1,0:T(8,128)(2,1)S(1)} %convolution_convert_fusion.2), channel_id=1, source_target_pairs={{0,4},{1,5},{2,6},{3,7},{4,0},{5,1},{6,2},{7,3},{8,12},{9,13},{10,... | collective-permute-start | bytes 1179656 | tf_op jit(solution)/shard_map/ppermute | solution.py:35
  256.1 0.8 copy-start
  256.9 24.2 %all-to-all-start.2 = ((bf16[8,128,512]{2,1,0:T(8,128)(2,1)}), bf16[8,128,512]{2,1,0:T(8,128)(2,1)}, u32[]{:S(2)}, u32[]{:S(2)}) async-start(bf16[8,128,512]{2,1,0:T(8,128)(2,1)} %get-tuple-element.10), calls=%async_computation.2 | async-start | bytes 2097152 | tf_op jit(solution)/shard_map/all_to_all | solution.py:239
  273.0 1.0 copy-start.1
  273.1 24.6 %collective-permute-start.12 = (bf16[384,512]{1,0:T(8,128)(2,1)S(1)}, bf16[384,512]{1,0:T(8,128)(2,1)}, u32[]{:S(2)}, u32[]{:S(2)}) collective-permute-start(bf16[384,512]{1,0:T(8,128)(2,1)S(1)} %pad_maximum_fusion.6), channel_id=1, source_target_pairs={{0,4},{1,5},{2,6},{3,7},{4,0},{5,1},{6,2},{7,3},{8,12},{9,13},{10,... | collective-permute-start | bytes 1179656 | tf_op jit(solution)/shard_map/ppermute | solution.py:35
  274.1 38.5 %collective-permute-start.11 = (bf16[384,512]{1,0:T(8,128)(2,1)S(1)}, bf16[384,512]{1,0:T(8,128)(2,1)}, u32[]{:S(2)}, u32[]{:S(2)}) collective-permute-start(bf16[384,512]{1,0:T(8,128)(2,1)S(1)} %pad_maximum_fusion.5), channel_id=1, source_target_pairs={{0,6},{1,7},{2,0},{3,1},{4,2},{5,3},{6,4},{7,5},{8,14},{9,15},{10,... | collective-permute-start | bytes 1179656 | tf_op jit(solution)/shard_map/ppermute | solution.py:35
  279.5 34.5 %copy-start.3 = (bf16[384,1024]{1,0:T(8,128)(2,1)S(1)}, bf16[384,1024]{1,0:T(8,128)(2,1)}, u32[]{:S(2)}) copy-start(bf16[384,1024]{1,0:T(8,128)(2,1)} %reshape.125) | copy-start | bytes 2359300
  279.5 33.0 %collective-permute-start.10 = (bf16[384,512]{1,0:T(8,128)(2,1)}, bf16[384,512]{1,0:T(8,128)(2,1)}, u32[]{:S(2)}, u32[]{:S(2)}) collective-permute-start(bf16[384,512]{1,0:T(8,128)(2,1)} %pad_maximum_fusion.4), channel_id=1, source_target_pairs={{0,2},{1,3},{2,4},{3,5},{4,6},{5,7},{6,0},{7,1},{8,10},{9,11},{10,... | collective-permute-start | bytes 1179656 | tf_op jit(solution)/shard_map/ppermute | solution.py:35
  281.1 34.6 %all-to-all-start.4 = ((bf16[8,128,512]{2,1,0:T(8,128)(2,1)}), bf16[8,128,512]{2,1,0:T(8,128)(2,1)S(1)}, u32[]{:S(2)}, u32[]{:S(2)}) async-start(bf16[8,128,512]{2,1,0:T(8,128)(2,1)} %get-tuple-element.11), calls=%async_computation.4 | async-start | bytes 2097152 | tf_op jit(solution)/shard_map/all_to_all | solution.py:239
  315.7 8.7 %copy-start.2 = (bf16[8,128,512]{2,1,0:T(8,128)(2,1)}, bf16[8,128,512]{2,1,0:T(8,128)(2,1)S(1)}, u32[]{:S(2)}) copy-start(bf16[8,128,512]{2,1,0:T(8,128)(2,1)S(1)} %all-to-all-done.4.refs_1_) | copy-start | bytes 3145732
  315.7 102.1 %all-to-all-start.5 = ((bf16[8,128,512]{2,1,0:T(8,128)(2,1)}), bf16[8,128,512]{2,1,0:T(8,128)(2,1)S(1)}, u32[]{:S(2)}, u32[]{:S(2)}) async-start(bf16[8,128,512]{2,1,0:T(8,128)(2,1)} %bitcast.41), calls=%async_computation.5 | async-start | bytes 2097152 | tf_op jit(solution)/shard_map/all_to_all | solution.py:251
  325.7 2.0 collective-permute-start.13
  328.0 8.8 %collective-permute-start.16 = (bf16[4,12,1024]{2,1,0:T(8,128)(2,1)S(1)}, bf16[4,12,1024]{2,1,0:T(8,128)(2,1)S(1)}, u32[]{:S(2)}, u32[]{:S(2)}) collective-permute-start(bf16[4,12,1024]{2,1,0:T(8,128)(2,1)S(1)} %get-tuple-element.25), channel_id=1, source_target_pairs={{0,24},{1,25},{2,26},{3,27},{4,28},{5,29},{6,30},{7,31},{8,0},{9,1... | collective-permute-start | bytes 294920 | tf_op jit(solution)/shard_map/ppermute | solution.py:35
  330.9 7.9 %collective-permute-start.15 = (bf16[4,12,1024]{2,1,0:T(8,128)(2,1)S(1)}, bf16[4,12,1024]{2,1,0:T(8,128)(2,1)S(1)}, u32[]{:S(2)}, u32[]{:S(2)}) collective-permute-start(bf16[4,12,1024]{2,1,0:T(8,128)(2,1)S(1)} %get-tuple-element.26), channel_id=1, source_target_pairs={{0,16},{1,17},{2,18},{3,19},{4,20},{5,21},{6,22},{7,23},{8,24},{9,... | collective-permute-start | bytes 294920 | tf_op jit(solution)/shard_map/ppermute | solution.py:35
  331.8 8.7 %collective-permute-start.14 = (bf16[4,12,1024]{2,1,0:T(8,128)(2,1)S(1)}, bf16[4,12,1024]{2,1,0:T(8,128)(2,1)S(1)}, u32[]{:S(2)}, u32[]{:S(2)}) collective-permute-start(bf16[4,12,1024]{2,1,0:T(8,128)(2,1)S(1)} %get-tuple-element.24), channel_id=1, source_target_pairs={{0,8},{1,9},{2,10},{3,11},{4,12},{5,13},{6,14},{7,15},{8,16},{9,17... | collective-permute-start | bytes 294920 | tf_op jit(solution)/shard_map/ppermute | solution.py:35
  340.6 5.4 %collective-permute-start.19 = (bf16[12,1024]{1,0:T(8,128)(2,1)S(1)}, bf16[12,1024]{1,0:T(8,128)(2,1)S(1)}, u32[]{:S(2)}, u32[]{:S(2)}) collective-permute-start(bf16[12,1024]{1,0:T(8,128)(2,1)S(1)} %get-tuple-element.42), channel_id=1, source_target_pairs={{0,6},{1,7},{2,0},{3,1},{4,2},{5,3},{6,4},{7,5},{8,14},{9,15},{10,... | collective-permute-start | bytes 73736 | tf_op jit(solution)/shard_map/ppermute | solution.py:35
  343.0 7.9 %collective-permute-start.18 = (bf16[12,1024]{1,0:T(8,128)(2,1)S(1)}, bf16[12,1024]{1,0:T(8,128)(2,1)S(1)}, u32[]{:S(2)}, u32[]{:S(2)}) collective-permute-start(bf16[12,1024]{1,0:T(8,128)(2,1)S(1)} %get-tuple-element.43), channel_id=1, source_target_pairs={{0,4},{1,5},{2,6},{3,7},{4,0},{5,1},{6,2},{7,3},{8,12},{9,13},{10,... | collective-permute-start | bytes 73736 | tf_op jit(solution)/shard_map/ppermute | solution.py:35
  346.0 6.2 %collective-permute-start.17 = (bf16[12,1024]{1,0:T(8,128)(2,1)S(1)}, bf16[12,1024]{1,0:T(8,128)(2,1)S(1)}, u32[]{:S(2)}, u32[]{:S(2)}) collective-permute-start(bf16[12,1024]{1,0:T(8,128)(2,1)S(1)} %get-tuple-element.41), channel_id=1, source_target_pairs={{0,2},{1,3},{2,4},{3,5},{4,6},{5,7},{6,0},{7,1},{8,10},{9,11},{10,... | collective-permute-start | bytes 73736 | tf_op jit(solution)/shard_map/ppermute | solution.py:35

commit v2 on v1

v2 whole, which is shorter than its diff:
```python
import functools
import math

import jax
import jax.numpy as jnp
from jax import lax
from jax.experimental import pallas as pl
from jax.experimental.pallas import tpu as pltpu
from jax.sharding import PartitionSpec as P

HEAD_DIM = 128
NY, NZ, NC = 4, 4, 2
NX, NL = 4, 2
PEERS = NY * NC
ROWS = 128
KEYS = 384
ENC_ROWS = 12
FEATURES = 256
SHARED_Z = [[(y * NZ + z) * NC + c for y in range(NY) for c in range(NC)] for z in range(NZ)]
GROUPS = ((0, 2), (1, 3))
RETURNS = ((0,), (2,), (1, 3))
BF16, F32 = jnp.bfloat16, jnp.float32


def place():
    me = lax.axis_index("ctx")
    return me >> 3, (me >> 1) & 3, me & 1


def shift(value, dy=0, dz=0, dc=0):
    pairs = [
        ((y * NZ + z) * NC + c, (((y + dy) % NY) * NZ + (z + dz) % NZ) * NC + (c + dc) % NC)
        for y in range(NY)
        for z in range(NZ)
        for c in range(NC)
    ]
    return lax.ppermute(value, "ctx", pairs)


def by_owner(mine, arrived, me):
    blocks = [mine, *arrived]
    n = len(blocks)
    if n == 2:
        first = me == 0
        return jnp.stack([jnp.where(first, *blocks), jnp.where(first, *blocks[::-1])])
    return jnp.stack([lax.select_n((owner - me) & (n - 1), *blocks) for owner in range(n)])


def gather_encoder(block):
    y, z, c = place()
    along_z = by_owner(block, [shift(block, dz=-d) for d in range(1, NZ)], z)
    along_y = by_owner(along_z, [shift(along_z, dy=-d) for d in range(1, NY)], y)
    other = shift(along_y, dc=1)
    first = c == 0
    both = jnp.stack([jnp.where(first, along_y, other), jnp.where(first, other, along_y)], axis=2)
    return both.reshape(NY * NZ * NC, *block.shape)


def sum_encoder(part):
    y, z, c = place()

    def at(value, index, axis):
        start = [0] * value.ndim
        start[axis] = index
        size = [1 if i == axis else n for i, n in enumerate(value.shape)]
        return lax.dynamic_slice(value, start, size, allow_negative_indices=False).squeeze(axis)

    arrived = shift(at(part, 1 - c, 2), dc=1)
    total = (at(part, c, 2).astype(F32) + arrived.astype(F32)).astype(BF16)
    arrived = [shift(at(total, (y + d) & 3, 0), dy=d) for d in range(1, NY)]
    total = sum((a.astype(F32) for a in arrived), at(total, y, 0).astype(F32)).astype(BF16)
    arrived = [shift(at(total, (z + d) & 3, 0), dz=d) for d in range(1, NZ)]
    return sum((a.astype(F32) for a in arrived), at(total, z, 0).astype(F32)).astype(BF16)


def column_block(peer, distance, z):
    owner_y, owner_c = lax.div(peer, NC), lax.rem(peer, NC)
    return (owner_y * NZ + lax.rem(z + distance, NZ)) * NC + owner_c


def pack_kernel(z, *refs):
    sources, out = refs[:-1], refs[-1]
    for i in range(len(sources) // 2):
        for which in range(2):
            out[0, which, :, pl.ds(i * FEATURES, FEATURES)] = sources[2 * i + which][...]


def pack(group, z, queries, grads):
    shape = (2, ROWS, len(group) * FEATURES)
    columns = [
        pl.BlockSpec((ROWS, FEATURES), lambda p, z, d=d: (0, column_block(p, d, z[0])))
        for d in group
        for _ in range(2)
    ]
    return pl.pallas_call(
        pack_kernel,
        out_shape=jax.ShapeDtypeStruct((PEERS, *shape), BF16),
        grid_spec=pltpu.PrefetchScalarGridSpec(
            num_scalar_prefetch=1,
            grid=(PEERS,),
            in_specs=columns,
            out_specs=pl.BlockSpec((1, *shape), lambda p, z: (p, 0, 0, 0)),
        ),
        cost_estimate=pl.CostEstimate(
            flops=0, bytes_accessed=4 * PEERS * math.prod(shape), transcendentals=0
        ),
    )(z, *[queries, grads] * len(group))


def unpack_kernel(z, *refs):
    sources, out = refs[:-1], refs[-1]
    for group, source in zip(RETURNS, sources, strict=True):
        for i, distance in enumerate(group):
            for c in range(NC):
                at = (lax.rem(z[0] + distance, NZ) * NC + c) * FEATURES
                columns = pl.ds(pl.multiple_of(at, FEATURES), FEATURES)
                out[:, columns] = source[c, :, pl.ds(i * FEATURES, FEATURES)]


def unpack(z, arrived):
    width = NZ * NC * FEATURES
    return pl.pallas_call(
        unpack_kernel,
        out_shape=jax.ShapeDtypeStruct((ROWS, NY * width), BF16),
        grid_spec=pltpu.PrefetchScalarGridSpec(
            num_scalar_prefetch=1,
            grid=(NY,),
            in_specs=[
                pl.BlockSpec((NC, ROWS, a.shape[2]), lambda y, z: (y, 0, 0)) for a in arrived
            ],
            out_specs=pl.BlockSpec((ROWS, width), lambda y, z: (0, y)),
        ),
        cost_estimate=pl.CostEstimate(
            flops=0, bytes_accessed=4 * ROWS * NY * width, transcendentals=0
        ),
    )(z, *arrived)


def attend_kernel(ends, rows, key, value, query_grad, key_grad, value_grad, bias):
    tile = NC * ROWS

    @pl.when(pl.program_id(0) == 0)
    def _():
        z = lax.rem(lax.div(lax.axis_index("ctx"), NC), NZ)
        keys_at = lax.broadcasted_iota(jnp.int32, (KEYS, tile), 0)
        for y in range(NY):
            token = (y * NZ + z) * tile + lax.broadcasted_iota(jnp.int32, (1, tile), 1)
            low = jnp.zeros((1, tile), jnp.int32)
            high = jnp.full((1, tile), ends[0], jnp.int32)
            for d in range(3):
                past = token >= ends[3 + d]
                low = jnp.where(past, ends[d], low)
                high = jnp.where(past, ends[d + 1] if d < 2 else KEYS, high)
            allowed = (keys_at >= low) & (keys_at < high)
            bias[:, pl.ds(y * tile, tile)] = jnp.where(allowed, 0.0, -jnp.inf)

    keys, values = key[0], value[0]
    keys_turned = keys.T
    key_total = jnp.zeros((KEYS, HEAD_DIM), F32)
    value_total = jnp.zeros((KEYS, HEAD_DIM), F32)
    last = (((1,), (1,)), ((), ()))
    for y in range(NY):
        query = rows[pl.ds(y * NC, NC), 0].reshape(tile, HEAD_DIM)
        grad = rows[pl.ds(y * NC, NC), 1].reshape(tile, HEAD_DIM)
        scores = lax.dot_general(keys, query, last, preferred_element_type=F32)
        scores = scores + bias[:, pl.ds(y * tile, tile)]
        weights = jnp.exp(scores - jnp.max(scores, axis=0, keepdims=True))
        probability = weights * (1.0 / jnp.sum(weights, axis=0, keepdims=True))
        upstream = lax.dot_general(values, grad, last, preferred_element_type=F32)
        row_dot = jnp.sum(probability * upstream, axis=0, keepdims=True)
        score_grad = (probability * (upstream - row_dot)).astype(BF16)
        rounded = probability.astype(BF16)
        key_total += jnp.dot(score_grad, query, preferred_element_type=F32)
        value_total += jnp.dot(rounded, grad, preferred_element_type=F32)
        turned = jnp.dot(keys_turned, score_grad, preferred_element_type=F32)
        query_grad[pl.ds(y * NC, NC)] = turned.T.astype(BF16).reshape(NC, ROWS, HEAD_DIM)
    key_grad[0] = key_total.astype(BF16)
    value_grad[0] = value_total.astype(BF16)


def attend(ends, rows, first, keys, values):
    count = keys.shape[0]
    heads = FEATURES // HEAD_DIM
    elements = count * heads * PEERS * ROWS * KEYS
    block = (1, KEYS, HEAD_DIM)
    in_block = lambda h, ends: (h // heads, 0, h % heads)
    grads = jax.ShapeDtypeStruct((count, KEYS, FEATURES), BF16)
    return pl.pallas_call(
        attend_kernel,
        out_shape=(jax.ShapeDtypeStruct((PEERS, ROWS, count * FEATURES), BF16), grads, grads),
        grid_spec=pltpu.PrefetchScalarGridSpec(
            num_scalar_prefetch=1,
            grid=(count * heads,),
            in_specs=[
                pl.BlockSpec(
                    (PEERS, 2, ROWS, HEAD_DIM), lambda h, ends: (0, 0, 0, first * heads + h)
                ),
                pl.BlockSpec(block, in_block),
                pl.BlockSpec(block, in_block),
            ],
            out_specs=(
                pl.BlockSpec((PEERS, ROWS, HEAD_DIM), lambda h, ends: (0, 0, h)),
                pl.BlockSpec(block, in_block),
                pl.BlockSpec(block, in_block),
            ),
            scratch_shapes=[pltpu.VMEM((KEYS, PEERS * ROWS), F32)],
        ),
        compiler_params=pltpu.CompilerParams(vmem_limit_bytes=24 * 2**20),
        cost_estimate=pl.CostEstimate(
            flops=elements * HEAD_DIM * 10, bytes_accessed=6 * 2**20, transcendentals=elements
        ),
    )(ends, rows, keys, values)


def gather_weights(block):
    me = lax.axis_index("dp")
    x, low = me >> 1, me & 1

    def ahead(value, dx, dl):
        pairs = [
            (a * NL + b, (a - dx) % NX * NL + (b - dl) % NL) for a in range(NX) for b in range(NL)
        ]
        return lax.ppermute(value, "dp", pairs)

    pair = by_owner(block, [ahead(block, 0, 1)], low)
    return by_owner(pair, [ahead(pair, d, 0) for d in range(1, NX)], x).reshape(-1, block.shape[1])


def body(queries, out_grad, enc_states, w_key, w_value, dec_segments, enc_segments):
    z = place()[1]
    z_index = z.reshape(1)
    below = [jnp.sum(ids < d) for ids in (enc_segments, dec_segments) for d in range(1, 4)]
    counts = jnp.stack(below).astype(BF16)
    last_rows = jnp.pad(counts[None], ((0, 3), (0, enc_states.shape[1] - 6)))
    gathered = gather_encoder(jnp.concatenate([enc_states, last_rows], axis=0))
    encoder = gathered[:, :ENC_ROWS].reshape(KEYS, -1)
    ends = jnp.sum(gathered[:, ENC_ROWS, :6].astype(jnp.int32), axis=0)
    weight = gather_weights(jnp.concatenate([w_key, w_value], axis=1))

    swap = functools.partial(
        lax.all_to_all,
        axis_name="ctx",
        split_axis=0,
        concat_axis=0,
        axis_index_groups=SHARED_Z,
        tiled=True,
    )
    near = swap(pack(GROUPS[0], z_index, queries, out_grad))
    own = jnp.dot(encoder, weight, preferred_element_type=F32).astype(BF16)
    far_packed, near = lax.optimization_barrier((pack(GROUPS[1], z_index, queries, out_grad), near))
    far = swap(far_packed)

    ahead, behind = shift(own, dz=-1), shift(own, dz=1)
    key_of = lambda block: block[:, :FEATURES]
    value_of = lambda block: block[:, FEATURES:]
    key_opposite, value_opposite = shift(key_of(ahead), dz=-1), shift(value_of(behind), dz=1)

    back_0, key_0, value_0 = attend(ends, near, 0, key_of(own)[None], value_of(own)[None])
    back_2, key_2, value_2 = attend(ends, near, 1, key_opposite[None], value_opposite[None])
    back_1, key_1, value_1 = attend(
        ends,
        far,
        0,
        jnp.stack([key_of(ahead), key_of(behind)]),
        jnp.stack([value_of(ahead), value_of(behind)]),
    )
    query_grad = unpack(z_index, [swap(back_0), swap(back_2), swap(back_1)])

    def joined(a, b):
        return (a.astype(F32) + b.astype(F32)).astype(BF16)

    key_ahead = joined(key_1[0], shift(key_2[0], dz=1))
    value_behind = joined(value_1[1], shift(value_2[0], dz=-1))
    total = jnp.concatenate([key_0[0], value_0[0]], axis=1).astype(F32)
    total += shift(jnp.concatenate([key_ahead, value_1[0]], axis=1), dz=1).astype(F32)
    total += shift(jnp.concatenate([key_1[1], value_behind], axis=1), dz=-1).astype(F32)

    rounded = total.astype(BF16)
    part = lax.dot_general(rounded, weight, (((1,), (1,)), ((), ())), preferred_element_type=F32)
    enc_grad = sum_encoder(part.astype(BF16).reshape(NY, NZ, NC, ENC_ROWS, -1))

    term = lax.dot_general(encoder, rounded, (((0,), (0,)), ((), ())), preferred_element_type=F32)
    pieces = term.astype(BF16).reshape(NX * NL, -1, 2 * FEATURES)
    pieces = lax.all_to_all(pieces, "dp", 0, 0, tiled=True)
    weight_grad = pieces.astype(F32).sum(axis=0)
    return query_grad, enc_grad, weight_grad[:, :FEATURES], weight_grad[:, FEATURES:]


def solution(mesh):
    tokens, weights, ids = P(("dp", "ctx"), None), P("dp", "ctx"), P(("dp", "ctx"))
    return jax.shard_map(
        body,
        mesh=mesh,
        in_specs=(tokens, tokens, tokens, weights, weights, ids, ids),
        out_specs=(tokens, tokens, weights, weights),
        check_vma=False,
    )
```

time: 419 us -> 233 us (0.56)
  Pallas kernels: 218 us -> 39.4 us
  waiting for transfers between devices: 111 us -> 93.3 us
  starting transfers between devices: 66.1 us -> 70.6 us
    pallas_call x3, Pallas kernels: 195 us -> 15.1 us  [the longest x2 11.3 us: pack(): pl.pallas_call(pack_kernel, out_shape=jax.ShapeDtypeStruct((PEERS, *shape...]
    all_to_all x5, waiting for transfers between devices: 27.1 us -> 9 us  [the longest x3 9 us: body(): query_grad = unpack(z_index, [swap(back_0), swap(back_2), swap(back_1)])]
    ppermute x0 -> x4, waiting for transfers between devices: none -> 4.42 us  [ahead(): return lax.ppermute(value, 'dp', pairs)]
    ppermute x20 -> x22, waiting for transfers between devices: 84.2 us -> 79.8 us  [shift(): return lax.ppermute(value, 'ctx', pairs)]
    ppermute x20 -> x22, starting transfers between devices: 35.8 us -> 39.3 us  [shift(): return lax.ppermute(value, 'ctx', pairs)]
    pallas_call x2 -> x3, Pallas kernels: 22.8 us -> 24.3 us  [attend(): pl.pallas_call(attend_kernel, out_shape=(jax.ShapeDtypeStruct((PEERS, ROW...]
  transfers between devices with their start and end apart: 26 -> 32, of which waited for: 14 -> 15; matrix products, arithmetic and copies ran while one was open for 4% -> 8% of each run, Pallas kernels for 36% -> 17%
where the time goes in v2:
time: 233 us; the launch traced here: 231 us
  waiting for transfers between devices  93.3 us (40%)
  starting transfers between devices  70.6 us (30%)
  Pallas kernels  39.4 us (17%)
  other arithmetic  10 us (4%)
  matrix products  7.83 us (3%)
  local copies, waits for them, and re-layouts  5.08 us (2%)
  between operations  4.81 us (2%)
    ppermute x22, waiting for transfers between devices, shift(): return lax.ppermute(value, 'ctx', pairs)  79.8 us
    ppermute x22, starting transfers between devices, shift(): return lax.ppermute(value, 'ctx', pairs)  39.3 us
    pallas_call x3, Pallas kernels, attend(): pl.pallas_call(attend_kernel, out_shape=(jax.ShapeDtypeStruct((PEERS, ROW...  24.3 us
    all_to_all x3, starting transfers between devices, body(): query_grad = unpack(z_index, [swap(back_0), swap(back_2), swap(back_1)])  12.7 us
    pallas_call x2, Pallas kernels, pack(): pl.pallas_call(pack_kernel, out_shape=jax.ShapeDtypeStruct((PEERS, *shape...  11.3 us
    all_to_all x3, waiting for transfers between devices, body(): query_grad = unpack(z_index, [swap(back_0), swap(back_2), swap(back_1)])  9 us
    all_to_all x1, starting transfers between devices, body(): pieces = lax.all_to_all(pieces, 'dp', 0, 0, tiled=True)  5.78 us
  transfers between devices with their start and end apart: 32, of which 15 were waited for; matrix products, arithmetic and copies ran while one was open for 8% of the time, Pallas kernels for 17%

profile of v2, /device:TPU:2, one launch (start us, length us, event | category | flops | bytes accessed | tf_op | source)
XLA Modules:
  0.0 231.0 jit_solution(5747048168901887729)
XLA Ops:
  0.6 1.3 fusion.14
  3.9 1.3 fusion.17
  8.0 7.3 %collective-permute-start.1 = (bf16[16,1024]{1,0:T(8,128)(2,1)S(1)}, bf16[16,1024]{1,0:T(8,128)(2,1)S(1)}, u32[]{:S(2)}, u32[]{:S(2)}) collective-permute-start(bf16[16,1024]{1,0:T(8,128)(2,1)S(1)} %fusion.10), channel_id=1, source_target_pairs={{0,4},{1,5},{2,6},{3,7},{4,0},{5,1},{6,2},{7,3},{8,12},{9,13},{10,... | collective-permute-start | bytes 98312 | tf_op jit(solution)/shard_map/ppermute | solution.py:37
  15.3 1.5 collective-permute-start.2
  16.8 2.7 %collective-permute-start = (bf16[16,1024]{1,0:T(8,128)(2,1)S(1)}, bf16[16,1024]{1,0:T(8,128)(2,1)S(1)}, u32[]{:S(2)}, u32[]{:S(2)}) collective-permute-start(bf16[16,1024]{1,0:T(8,128)(2,1)S(1)} %fusion.10), channel_id=1, source_target_pairs={{0,6},{1,7},{2,0},{3,1},{4,2},{5,3},{6,4},{7,5},{8,14},{9,15},{10,... | collective-permute-start | bytes 98312 | tf_op jit(solution)/shard_map/ppermute | solution.py:37
  19.4 5.6 %shard_map.103 = bf16[8,2,128,512]{3,2,1,0:T(8,128)(2,1)} custom-call(s32[1]{0:T(128)} %bitcast.z, bf16[128,8192]{1,0:T(8,128)(2,1)} %refs_2_.3, bf16[128,8192]{1,0:T(8,128)(2,1)} %refs_3_.3, bf16[128,8192]{1,0:T(8,128)(2,1)} %refs_2_.3, bf16[128,8192]{1,0:T(8,128)(2,1)} %refs_3_.3), custom_call_target="tpu_custom_call" | custom-call | bytes 4194304 | tf_op jit(solution)/shard_map/pallas_call | solution.py:95
  25.1 4.6 %all-to-all-start = ((bf16[8,2,128,512]{3,2,1,0:T(8,128)(2,1)}), bf16[8,2,128,512]{3,2,1,0:T(8,128)(2,1)S(1)}, u32[]{:S(2)}, u32[]{:S(2)}) async-start(bf16[8,2,128,512]{3,2,1,0:T(8,128)(2,1)} %shard_map.103), calls=%async_computation | async-start | bytes 4194304 | tf_op jit(solution)/shard_map/all_to_all | solution.py:248
  30.8 5.6 %shard_map.102 = bf16[8,2,128,512]{3,2,1,0:T(8,128)(2,1)} custom-call(s32[1]{0:T(128)} %bitcast.z, bf16[128,8192]{1,0:T(8,128)(2,1)} %refs_2_.3, bf16[128,8192]{1,0:T(8,128)(2,1)} %refs_3_.3, bf16[128,8192]{1,0:T(8,128)(2,1)} %refs_2_.3, bf16[128,8192]{1,0:T(8,128)(2,1)} %refs_3_.3), custom_call_target="tpu_custom_call" | custom-call | bytes 4194304 | tf_op jit(solution)/shard_map/pallas_call | solution.py:95
  36.6 3.6 %collective-permute-start.4 = (bf16[4,16,1024]{2,1,0:T(8,128)(2,1)S(1)}, bf16[4,16,1024]{2,1,0:T(8,128)(2,1)S(1)}, u32[]{:S(2)}, u32[]{:S(2)}) collective-permute-start(bf16[4,16,1024]{2,1,0:T(8,128)(2,1)S(1)} %pad_maximum_fusion.8), channel_id=1, source_target_pairs={{0,16},{1,17},{2,18},{3,19},{4,20},{5,21},{6,22},{7,23},{8,24},{9,... | collective-permute-start | bytes 393224 | tf_op jit(solution)/shard_map/ppermute | solution.py:37
  40.7 2.7 %collective-permute-start.3 = (bf16[4,16,1024]{2,1,0:T(8,128)(2,1)S(1)}, bf16[4,16,1024]{2,1,0:T(8,128)(2,1)S(1)}, u32[]{:S(2)}, u32[]{:S(2)}) collective-permute-start(bf16[4,16,1024]{2,1,0:T(8,128)(2,1)S(1)} %pad_maximum_fusion.8), channel_id=1, source_target_pairs={{0,24},{1,25},{2,26},{3,27},{4,28},{5,29},{6,30},{7,31},{8,0},{9,1... | collective-permute-start | bytes 393224 | tf_op jit(solution)/shard_map/ppermute | solution.py:37
  43.5 2.2 collective-permute-start.9
  45.7 14.5 %collective-permute-done.4 = bf16[4,16,1024]{2,1,0:T(8,128)(2,1)S(1)} collective-permute-done((bf16[4,16,1024]{2,1,0:T(8,128)(2,1)S(1)}, bf16[4,16,1024]{2,1,0:T(8,128)(2,1)S(1)}, u32[]{:S(2)}, u32[]{:S(2)}) %collective-permute-start.4) | collective-permute-done | bytes 131104 | tf_op jit(solution)/shard_map/ppermute | solution.py:37
  60.7 1.5 collective-permute-done.5
  63.2 4.4 %collective-permute-done.8 = bf16[2,128,512]{2,1,0:T(8,128)(2,1)S(1)} collective-permute-done((bf16[2,128,512]{2,1,0:T(8,128)(2,1)S(1)}, bf16[2,128,512]{2,1,0:T(8,128)(2,1)S(1)}, u32[]{:S(2)}, u32[]{:S(2)}) %collective-permute-start.8) | collective-permute-done | bytes 262176 | tf_op jit(solution)/shard_map/ppermute | solution.py:223
  67.7 1.1 pad_maximum_fusion.1
  68.9 4.4 %all-to-all-start.3 = ((bf16[8,2,128,512]{3,2,1,0:T(8,128)(2,1)}), bf16[8,2,128,512]{3,2,1,0:T(8,128)(2,1)}, u32[]{:S(2)}, u32[]{:S(2)}) async-start(bf16[8,2,128,512]{3,2,1,0:T(8,128)(2,1)} %shard_map.102), calls=%async_computation.3 | async-start | bytes 4194304 | tf_op jit(solution)/shard_map/all_to_all | solution.py:251
  73.5 1.3 reshape.132
  74.7 2.0 convolution_convert_fusion.2
  76.9 2.9 %collective-permute-start.13 = (bf16[384,512]{1,0:T(8,128)(2,1)S(1)}, bf16[384,512]{1,0:T(8,128)(2,1)S(1)}, u32[]{:S(2)}, u32[]{:S(2)}) collective-permute-start(bf16[384,512]{1,0:T(8,128)(2,1)S(1)} %convolution_convert_fusion.2), channel_id=1, source_target_pairs={{0,2},{1,3},{2,4},{3,5},{4,6},{5,7},{6,0},{7,1},{8,10},{9,11},{10,... | collective-permute-start | bytes 1179656 | tf_op jit(solution)/shard_map/ppermute | solution.py:37
  80.7 16.9 %collective-permute-done.11 = bf16[384,512]{1,0:T(8,128)(2,1)S(1)} collective-permute-done((bf16[384,512]{1,0:T(8,128)(2,1)S(1)}, bf16[384,512]{1,0:T(8,128)(2,1)S(1)}, u32[]{:S(2)}, u32[]{:S(2)}) %collective-permute-start.11) | collective-permute-done | bytes 393248 | tf_op jit(solution)/shard_map/ppermute | solution.py:37
  97.6 1.8 collective-permute-start.12
  100.2 1.4 collective-permute-start.14
  101.6 4.0 %collective-permute-done.12 = bf16[384,256]{1,0:T(8,128)(2,1)S(1)} collective-permute-done((bf16[384,256]{1,0:T(8,128)(2,1)S(1)}, bf16[384,256]{1,0:T(8,128)(2,1)S(1)}, u32[]{:S(2)}, u32[]{:S(2)}) %collective-permute-start.12) | collective-permute-done | bytes 196640 | tf_op jit(solution)/shard_map/ppermute | solution.py:37
  105.5 6.7 %collective-permute-done.14 = bf16[384,256]{1,0:T(8,128)(2,1)S(1)} collective-permute-done((bf16[384,256]{1,0:T(8,128)(2,1)S(1)}, bf16[384,256]{1,0:T(8,128)(2,1)S(1)}, u32[]{:S(2)}, u32[]{:S(2)}) %collective-permute-start.14) | collective-permute-done | bytes 196640 | tf_op jit(solution)/shard_map/ppermute | solution.py:37
  112.3 6.3 %shard_map.105 = (bf16[8,128,256]{2,1,0:T(8,128)(2,1)}, bf16[1,384,256]{2,1,0:T(8,128)(2,1)S(1)}, bf16[1,384,256]{2,1,0:T(8,128)(2,1)S(1)}) custom-call(s32[6]{0:T(128)S(1)} %fusion.11.ends, bf16[8,2,128,512]{3,2,1,0:T(8,128)(2,1)S(1)} %all-to-all-done.rows, bf16[1,384,256]{2,1,0:T(8,128)(2,1)S(1)} %bitcast.102, bf16[1,384,256]{2,1,0:T(8,128)(2,1)S(1)} %bitcast.103), custom_call_target="tpu_custom_call" | custom-call | flops 1006632960 | bytes 6291456 | tf_op jit(solution)/shard_map/pallas_call | solution.py:188
  118.6 6.3 %shard_map.104 = (bf16[8,128,256]{2,1,0:T(8,128)(2,1)}, bf16[1,384,256]{2,1,0:T(8,128)(2,1)S(1)}, bf16[1,384,256]{2,1,0:T(8,128)(2,1)S(1)}) custom-call(s32[6]{0:T(128)S(1)} %fusion.11.ends, bf16[8,2,128,512]{3,2,1,0:T(8,128)(2,1)S(1)} %all-to-all-done.rows, bf16[1,384,256]{2,1,0:T(8,128)(2,1)S(1)} %get-tuple-element.51.key, ...), custom_call_target="tpu_custom_call" | custom-call | flops 1006632960 | bytes 6291456 | tf_op jit(solution)/shard_map/pallas_call | solution.py:188
  124.9 4.3 %all-to-all-start.1 = ((bf16[8,128,256]{2,1,0:T(8,128)(2,1)}), bf16[8,128,256]{2,1,0:T(8,128)(2,1)S(1)}, u32[]{:S(2)}, u32[]{:S(2)}) async-start(bf16[8,128,256]{2,1,0:T(8,128)(2,1)} %get-tuple-element.16), calls=%async_computation.1 | async-start | bytes 1048576 | tf_op jit(solution)/shard_map/all_to_all | solution.py:267
  130.2 3.0 %collective-permute-start.15 = (bf16[384,256]{1,0:T(8,128)(2,1)S(1)}, bf16[384,256]{1,0:T(8,128)(2,1)S(1)}, u32[]{:S(2)}, u32[]{:S(2)}) collective-permute-start(bf16[384,256]{1,0:T(8,128)(2,1)S(1)} %bitcast.100), channel_id=1, source_target_pairs={{0,2},{1,3},{2,4},{3,5},{4,6},{5,7},{6,0},{7,1},{8,10},{9,11},{10,... | collective-permute-start | bytes 589832 | tf_op jit(solution)/shard_map/ppermute | solution.py:37
  133.2 11.7 %shard_map.106 = (bf16[8,128,512]{2,1,0:T(8,128)(2,1)}, bf16[2,384,256]{2,1,0:T(8,128)(2,1)S(1)}, bf16[2,384,256]{2,1,0:T(8,128)(2,1)S(1)}) custom-call(s32[6]{0:T(128)S(1)} %fusion.11.ends, bf16[8,2,128,512]{3,2,1,0:T(8,128)(2,1)} %all-to-all-done.3.rows, bf16[2,384,256]{2,1,0:T(8,128)(2,1)S(1)} %get-tuple-element.63.key, ...), custom_call_target="tpu_custom_call" | custom-call | flops 2013265920 | bytes 6291456 | tf_op jit(solution)/shard_map/pallas_call | solution.py:188
  145.9 4.8 %all-to-all-start.2 = ((bf16[8,128,256]{2,1,0:T(8,128)(2,1)}), bf16[8,128,256]{2,1,0:T(8,128)(2,1)S(1)}, u32[]{:S(2)}, u32[]{:S(2)}) async-start(bf16[8,128,256]{2,1,0:T(8,128)(2,1)} %get-tuple-element.17), calls=%async_computation.2 | async-start | bytes 1048576 | tf_op jit(solution)/shard_map/all_to_all | solution.py:267
  150.8 1.3 collective-permute-start.18
  152.1 9.0 %all-to-all-done.2.refs_1_ = bf16[8,128,256]{2,1,0:T(8,128)(2,1)S(1)} async-done(((bf16[8,128,256]{2,1,0:T(8,128)(2,1)}), bf16[8,128,256]{2,1,0:T(8,128)(2,1)S(1)}, u32[]{:S(2)}, u32[]{:S(2)}) %all-to-all-start.2) | async-done | bytes 524320 | tf_op jit(solution)/shard_map/all_to_all | solution.py:267
  161.8 3.6 %all-to-all-start.4 = ((bf16[8,128,512]{2,1,0:T(8,128)(2,1)}), bf16[8,128,512]{2,1,0:T(8,128)(2,1)S(1)}, u32[]{:S(2)}, u32[]{:S(2)}) async-start(bf16[8,128,512]{2,1,0:T(8,128)(2,1)} %get-tuple-element.19), calls=%async_computation.4 | async-start | bytes 2097152 | tf_op jit(solution)/shard_map/all_to_all | solution.py:267
  166.9 20.8 %collective-permute-done.16 = bf16[384,512]{1,0:T(8,128)(2,1)S(1)} collective-permute-done((bf16[384,512]{1,0:T(8,128)(2,1)S(1)}, bf16[384,512]{1,0:T(8,128)(2,1)S(1)}, u32[]{:S(2)}, u32[]{:S(2)}) %collective-permute-start.16) | collective-permute-done | bytes 393248 | tf_op jit(solution)/shard_map/ppermute | solution.py:37
  187.7 3.2 %convolution_convert_fusion = bf16[1024,512]{1,0:T(8,128)(2,1)} fusion(bf16[384,1024]{1,0:T(8,128)(2,1)} %reshape.132, bf16[384,512]{1,0:T(8,128)(2,1)} %collective-permute-done.18, bf16[384,512]{1,0:T(8,128)(2,1)S(1)} %collective-permute-done.16, bf16[384,256]{1,0:T(8,128)(2,1)S(1)} %bitcast.106, bf16[384,256]{1,0:T(8,128)(2,1)S(1)} %bitcast.104), kind=kOutput, calls=%fused_computation.1 | convolution fusion | flops 404946944 | bytes 3014656 | tf_op jit(solution)/shard_map/dot_general | solution.py:282
  190.9 5.8 %all-to-all-start.5 = ((bf16[8,128,512]{2,1,0:T(8,128)(2,1)}), bf16[8,128,512]{2,1,0:T(8,128)(2,1)S(1)}, u32[]{:S(2)}, u32[]{:S(2)}) async-start(bf16[8,128,512]{2,1,0:T(8,128)(2,1)} %bitcast.112), calls=%async_computation.5 | async-start | bytes 2097152 | tf_op jit(solution)/shard_map/all_to_all | solution.py:284
  196.7 2.6 %convolution_convert_fusion.1 = bf16[384,1024]{1,0:T(8,128)(2,1)} fusion(bf16[1024,512]{1,0:T(8,128)(2,1)S(1)} %bitcast.111, bf16[384,512]{1,0:T(8,128)(2,1)} %collective-permute-done.18, bf16[384,512]{1,0:T(8,128)(2,1)} %copy-done.8, bf16[384,256]{1,0:T(8,128)(2,1)S(1)} %bitcast.107, bf16[384,256]{1,0:T(8,128)(2,1)S(1)} %bitcast.105), kind=kOutput, calls=%fused_computation.2 | convolution fusion | flops 404815872 | bytes 3014656 | tf_op jit(solution)/shard_map/dot_general | solution.py:279
  199.3 1.3 reshape.134
  200.7 1.9 collective-permute-done.19
  202.8 3.0 %collective-permute-start.22 = (bf16[4,12,1024]{2,1,0:T(8,128)(2,1)S(1)}, bf16[4,12,1024]{2,1,0:T(8,128)(2,1)S(1)}, u32[]{:S(2)}, u32[]{:S(2)}) collective-permute-start(bf16[4,12,1024]{2,1,0:T(8,128)(2,1)S(1)} %get-tuple-element.38), channel_id=1, source_target_pairs={{0,24},{1,25},{2,26},{3,27},{4,28},{5,29},{6,30},{7,31},{8,0},{9,1... | collective-permute-start | bytes 294920 | tf_op jit(solution)/shard_map/ppermute | solution.py:37
  207.5 4.2 %collective-permute-done.22 = bf16[4,12,1024]{2,1,0:T(8,128)(2,1)S(1)} collective-permute-done((bf16[4,12,1024]{2,1,0:T(8,128)(2,1)S(1)}, bf16[4,12,1024]{2,1,0:T(8,128)(2,1)S(1)}, u32[]{:S(2)}, u32[]{:S(2)}) %collective-permute-start.22) | collective-permute-done | bytes 98336 | tf_op jit(solution)/shard_map/ppermute | solution.py:37
  211.7 2.0 collective-permute-done.21
  213.7 1.7 collective-permute-done.20
  215.5 1.1 collective-permute-start.25
  216.6 2.7 %collective-permute-start.24 = (bf16[12,1024]{1,0:T(8,128)(2,1)S(1)}, bf16[12,1024]{1,0:T(8,128)(2,1)S(1)}, u32[]{:S(2)}, u32[]{:S(2)}) collective-permute-start(bf16[12,1024]{1,0:T(8,128)(2,1)S(1)} %get-tuple-element.58), channel_id=1, source_target_pairs={{0,4},{1,5},{2,6},{3,7},{4,0},{5,1},{6,2},{7,3},{8,12},{9,13},{10,... | collective-permute-start | bytes 73736 | tf_op jit(solution)/shard_map/ppermute | solution.py:37
  219.3 1.6 collective-permute-start.23
  220.9 4.1 %collective-permute-done.24 = bf16[12,1024]{1,0:T(8,128)(2,1)S(1)} collective-permute-done((bf16[12,1024]{1,0:T(8,128)(2,1)S(1)}, bf16[12,1024]{1,0:T(8,128)(2,1)S(1)}, u32[]{:S(2)}, u32[]{:S(2)}) %collective-permute-start.24) | collective-permute-done | bytes 24608 | tf_op jit(solution)/shard_map/ppermute | solution.py:37
  226.2 3.9 %shard_map.107 = bf16[128,8192]{1,0:T(8,128)(2,1)} custom-call(s32[1]{0:T(128)} %bitcast.z, bf16[8,128,256]{2,1,0:T(8,128)(2,1)} %copy-done.2, bf16[8,128,256]{2,1,0:T(8,128)(2,1)} %copy-done.3, bf16[8,128,512]{2,1,0:T(8,128)(2,1)} %copy-done.1), custom_call_target="tpu_custom_call" | custom-call | bytes 4194304 | tf_op jit(solution)/shard_map/pallas_call | solution.py:122
  (82 shorter events, 14.9 us)
Async XLA Ops:
  8.0 28.4 %collective-permute-start.1 = (bf16[16,1024]{1,0:T(8,128)(2,1)S(1)}, bf16[16,1024]{1,0:T(8,128)(2,1)S(1)}, u32[]{:S(2)}, u32[]{:S(2)}) collective-permute-start(bf16[16,1024]{1,0:T(8,128)(2,1)S(1)} %fusion.10), channel_id=1, source_target_pairs={{0,4},{1,5},{2,6},{3,7},{4,0},{5,1},{6,2},{7,3},{8,12},{9,13},{10,... | collective-permute-start | bytes 98312 | tf_op jit(solution)/shard_map/ppermute | solution.py:37
  15.3 21.2 %collective-permute-start.2 = (bf16[16,1024]{1,0:T(8,128)(2,1)S(1)}, bf16[16,1024]{1,0:T(8,128)(2,1)S(1)}, u32[]{:S(2)}, u32[]{:S(2)}) collective-permute-start(bf16[16,1024]{1,0:T(8,128)(2,1)S(1)} %fusion.10), channel_id=1, source_target_pairs={{0,2},{1,3},{2,4},{3,5},{4,6},{5,7},{6,0},{7,1},{8,10},{9,11},{10,... | collective-permute-start | bytes 98312 | tf_op jit(solution)/shard_map/ppermute | solution.py:37
  16.8 19.7 %collective-permute-start = (bf16[16,1024]{1,0:T(8,128)(2,1)S(1)}, bf16[16,1024]{1,0:T(8,128)(2,1)S(1)}, u32[]{:S(2)}, u32[]{:S(2)}) collective-permute-start(bf16[16,1024]{1,0:T(8,128)(2,1)S(1)} %fusion.10), channel_id=1, source_target_pairs={{0,6},{1,7},{2,0},{3,1},{4,2},{5,3},{6,4},{7,5},{8,14},{9,15},{10,... | collective-permute-start | bytes 98312 | tf_op jit(solution)/shard_map/ppermute | solution.py:37
  25.0 4.6 %copy-start.6 = (bf16[128,256]{1,0:T(8,128)(2,1)S(1)}, bf16[128,256]{1,0:T(8,128)(2,1)}, u32[]{:S(2)}) copy-start(bf16[128,256]{1,0:T(8,128)(2,1)} %param.10) | copy-start | bytes 196612
  25.1 4.6 %copy-start.7 = (bf16[128,256]{1,0:T(8,128)(2,1)S(1)}, bf16[128,256]{1,0:T(8,128)(2,1)}, u32[]{:S(2)}) copy-start(bf16[128,256]{1,0:T(8,128)(2,1)} %param.11) | copy-start | bytes 196612
  25.1 43.8 %all-to-all-start = ((bf16[8,2,128,512]{3,2,1,0:T(8,128)(2,1)}), bf16[8,2,128,512]{3,2,1,0:T(8,128)(2,1)S(1)}, u32[]{:S(2)}, u32[]{:S(2)}) async-start(bf16[8,2,128,512]{3,2,1,0:T(8,128)(2,1)} %shard_map.103), calls=%async_computation | async-start | bytes 4194304 | tf_op jit(solution)/shard_map/all_to_all | solution.py:248
  29.7 13.7 %collective-permute-start.7 = (bf16[128,512]{1,0:T(8,128)(2,1)S(1)}, bf16[128,512]{1,0:T(8,128)(2,1)S(1)}, u32[]{:S(2)}, u32[]{:S(2)}) collective-permute-start(bf16[128,512]{1,0:T(8,128)(2,1)S(1)} %constant_dynamic-update-slice_fusion), channel_id=1, source_target_pairs={{0,32},{32,0},{64,96},{96,64},{128,160},{160,128},{192,224},{224,1... | collective-permute-start | bytes 393224 | tf_op jit(solution)/shard_map/ppermute | solution.py:223
  30.8 5.7 %copy-start.5 = (bf16[12,1024]{1,0:T(8,128)(2,1)S(1)}, bf16[12,1024]{1,0:T(8,128)(2,1)}, u32[]{:S(2)}) copy-start(bf16[12,1024]{1,0:T(8,128)(2,1)} %param.9) | copy-start | bytes 73732
  36.6 23.6 %collective-permute-start.4 = (bf16[4,16,1024]{2,1,0:T(8,128)(2,1)S(1)}, bf16[4,16,1024]{2,1,0:T(8,128)(2,1)S(1)}, u32[]{:S(2)}, u32[]{:S(2)}) collective-permute-start(bf16[4,16,1024]{2,1,0:T(8,128)(2,1)S(1)} %pad_maximum_fusion.8), channel_id=1, source_target_pairs={{0,16},{1,17},{2,18},{3,19},{4,20},{5,21},{6,22},{7,23},{8,24},{9,... | collective-permute-start | bytes 393224 | tf_op jit(solution)/shard_map/ppermute | solution.py:37
  40.2 22.0 %collective-permute-start.5 = (bf16[4,16,1024]{2,1,0:T(8,128)(2,1)S(1)}, bf16[4,16,1024]{2,1,0:T(8,128)(2,1)S(1)}, u32[]{:S(2)}, u32[]{:S(2)}) collective-permute-start(bf16[4,16,1024]{2,1,0:T(8,128)(2,1)S(1)} %pad_maximum_fusion.8), channel_id=1, source_target_pairs={{0,8},{1,9},{2,10},{3,11},{4,12},{5,13},{6,14},{7,15},{8,16},{9,17... | collective-permute-start | bytes 393224 | tf_op jit(solution)/shard_map/ppermute | solution.py:37
  40.7 21.4 %collective-permute-start.3 = (bf16[4,16,1024]{2,1,0:T(8,128)(2,1)S(1)}, bf16[4,16,1024]{2,1,0:T(8,128)(2,1)S(1)}, u32[]{:S(2)}, u32[]{:S(2)}) collective-permute-start(bf16[4,16,1024]{2,1,0:T(8,128)(2,1)S(1)} %pad_maximum_fusion.8), channel_id=1, source_target_pairs={{0,24},{1,25},{2,26},{3,27},{4,28},{5,29},{6,30},{7,31},{8,0},{9,1... | collective-permute-start | bytes 393224 | tf_op jit(solution)/shard_map/ppermute | solution.py:37
  43.5 19.7 %collective-permute-start.9 = (bf16[2,128,512]{2,1,0:T(8,128)(2,1)S(1)}, bf16[2,128,512]{2,1,0:T(8,128)(2,1)S(1)}, u32[]{:S(2)}, u32[]{:S(2)}) collective-permute-start(bf16[2,128,512]{2,1,0:T(8,128)(2,1)S(1)} %pad_maximum_fusion.7), channel_id=1, source_target_pairs={{0,128},{32,160},{64,192},{96,224},{128,0},{160,32},{192,64},{224,... | collective-permute-start | bytes 786440 | tf_op jit(solution)/shard_map/ppermute | solution.py:223
  45.7 17.5 %collective-permute-start.10 = (bf16[2,128,512]{2,1,0:T(8,128)(2,1)S(1)}, bf16[2,128,512]{2,1,0:T(8,128)(2,1)S(1)}, u32[]{:S(2)}, u32[]{:S(2)}) collective-permute-start(bf16[2,128,512]{2,1,0:T(8,128)(2,1)S(1)} %pad_maximum_fusion.7), channel_id=1, source_target_pairs={{0,64},{32,96},{64,128},{96,160},{128,192},{160,224},{192,0},{224,... | collective-permute-start | bytes 786440 | tf_op jit(solution)/shard_map/ppermute | solution.py:223
  60.2 7.4 %collective-permute-start.8 = (bf16[2,128,512]{2,1,0:T(8,128)(2,1)S(1)}, bf16[2,128,512]{2,1,0:T(8,128)(2,1)S(1)}, u32[]{:S(2)}, u32[]{:S(2)}) collective-permute-start(bf16[2,128,512]{2,1,0:T(8,128)(2,1)S(1)} %pad_maximum_fusion.7), channel_id=1, source_target_pairs={{0,192},{32,224},{64,0},{96,32},{128,64},{160,96},{192,128},{224,1... | collective-permute-start | bytes 786440 | tf_op jit(solution)/shard_map/ppermute | solution.py:223
  63.1 10.1 %collective-permute-start.6 = (bf16[4,4,16,1024]{3,2,1,0:T(8,128)(2,1)}, bf16[4,4,16,1024]{3,2,1,0:T(8,128)(2,1)S(1)}, u32[]{:S(2)}, u32[]{:S(2)}) collective-permute-start(bf16[4,4,16,1024]{3,2,1,0:T(8,128)(2,1)} %pad_maximum_fusion.2), channel_id=1, source_target_pairs={{0,1},{1,0},{2,3},{3,2},{4,5},{5,4},{6,7},{7,6},{8,9},{9,8},{10,11... | collective-permute-start | bytes 1572872 | tf_op jit(solution)/shard_map/ppermute | solution.py:37
  68.9 56.0 %all-to-all-start.3 = ((bf16[8,2,128,512]{3,2,1,0:T(8,128)(2,1)}), bf16[8,2,128,512]{3,2,1,0:T(8,128)(2,1)}, u32[]{:S(2)}, u32[]{:S(2)}) async-start(bf16[8,2,128,512]{3,2,1,0:T(8,128)(2,1)} %shard_map.102), calls=%async_computation.3 | async-start | bytes 4194304 | tf_op jit(solution)/shard_map/all_to_all | solution.py:251
  73.5 3.3 %copy-start = (bf16[4,4,2,16,1024]{4,3,2,1,0:T(8,128)(2,1)}, bf16[4,4,2,16,1024]{4,3,2,1,0:T(8,128)(2,1)S(1)}, u32[]{:S(2)}) copy-start(bf16[4,4,2,16,1024]{4,3,2,1,0:T(8,128)(2,1)S(1)} %pad_maximum_fusion) | copy-start | bytes 3145732
  76.8 20.8 %collective-permute-start.11 = (bf16[384,512]{1,0:T(8,128)(2,1)S(1)}, bf16[384,512]{1,0:T(8,128)(2,1)S(1)}, u32[]{:S(2)}, u32[]{:S(2)}) collective-permute-start(bf16[384,512]{1,0:T(8,128)(2,1)S(1)} %convolution_convert_fusion.2), channel_id=1, source_target_pairs={{0,6},{1,7},{2,0},{3,1},{4,2},{5,3},{6,4},{7,5},{8,14},{9,15},{10,... | collective-permute-start | bytes 1179656 | tf_op jit(solution)/shard_map/ppermute | solution.py:37
  76.9 22.6 %collective-permute-start.13 = (bf16[384,512]{1,0:T(8,128)(2,1)S(1)}, bf16[384,512]{1,0:T(8,128)(2,1)S(1)}, u32[]{:S(2)}, u32[]{:S(2)}) collective-permute-start(bf16[384,512]{1,0:T(8,128)(2,1)S(1)} %convolution_convert_fusion.2), channel_id=1, source_target_pairs={{0,2},{1,3},{2,4},{3,5},{4,6},{5,7},{6,0},{7,1},{8,10},{9,11},{10,... | collective-permute-start | bytes 1179656 | tf_op jit(solution)/shard_map/ppermute | solution.py:37
  97.6 7.9 %collective-permute-start.12 = (bf16[384,256]{1,0:T(8,128)(2,1)S(1)}, bf16[384,256]{1,0:T(8,128)(2,1)S(1)}, u32[]{:S(2)}, u32[]{:S(2)}) collective-permute-start(bf16[384,256]{1,0:T(8,128)(2,1)S(1)} %get-tuple-element.46), channel_id=1, source_target_pairs={{0,6},{1,7},{2,0},{3,1},{4,2},{5,3},{6,4},{7,5},{8,14},{9,15},{10,... | collective-permute-start | bytes 589832 | tf_op jit(solution)/shard_map/ppermute | solution.py:37
  100.2 12.1 %collective-permute-start.14 = (bf16[384,256]{1,0:T(8,128)(2,1)S(1)}, bf16[384,256]{1,0:T(8,128)(2,1)S(1)}, u32[]{:S(2)}, u32[]{:S(2)}) collective-permute-start(bf16[384,256]{1,0:T(8,128)(2,1)S(1)} %get-tuple-element.49), channel_id=1, source_target_pairs={{0,2},{1,3},{2,4},{3,5},{4,6},{5,7},{6,0},{7,1},{8,10},{9,11},{10,... | collective-permute-start | bytes 589832 | tf_op jit(solution)/shard_map/ppermute | solution.py:37
  118.6 26.3 %collective-permute-start.17 = (bf16[384,256]{1,0:T(8,128)(2,1)S(1)}, bf16[384,256]{1,0:T(8,128)(2,1)}, u32[]{:S(2)}, u32[]{:S(2)}) collective-permute-start(bf16[384,256]{1,0:T(8,128)(2,1)S(1)} %bitcast.101), channel_id=1, source_target_pairs={{0,6},{1,7},{2,0},{3,1},{4,2},{5,3},{6,4},{7,5},{8,14},{9,15},{10,... | collective-permute-start | bytes 589832 | tf_op jit(solution)/shard_map/ppermute | solution.py:37
  124.9 21.0 %all-to-all-start.1 = ((bf16[8,128,256]{2,1,0:T(8,128)(2,1)}), bf16[8,128,256]{2,1,0:T(8,128)(2,1)S(1)}, u32[]{:S(2)}, u32[]{:S(2)}) async-start(bf16[8,128,256]{2,1,0:T(8,128)(2,1)} %get-tuple-element.16), calls=%async_computation.1 | async-start | bytes 1048576 | tf_op jit(solution)/shard_map/all_to_all | solution.py:267
  130.2 35.2 %collective-permute-start.15 = (bf16[384,256]{1,0:T(8,128)(2,1)S(1)}, bf16[384,256]{1,0:T(8,128)(2,1)S(1)}, u32[]{:S(2)}, u32[]{:S(2)}) collective-permute-start(bf16[384,256]{1,0:T(8,128)(2,1)S(1)} %bitcast.100), channel_id=1, source_target_pairs={{0,2},{1,3},{2,4},{3,5},{4,6},{5,7},{6,0},{7,1},{8,10},{9,11},{10,... | collective-permute-start | bytes 589832 | tf_op jit(solution)/shard_map/ppermute | solution.py:37
  145.9 16.0 %copy-start.2 = (bf16[8,128,256]{2,1,0:T(8,128)(2,1)}, bf16[8,128,256]{2,1,0:T(8,128)(2,1)S(1)}, u32[]{:S(2)}) copy-start(bf16[8,128,256]{2,1,0:T(8,128)(2,1)S(1)} %all-to-all-done.1.refs_0_) | copy-start | bytes 1572868
  145.9 15.2 %all-to-all-start.2 = ((bf16[8,128,256]{2,1,0:T(8,128)(2,1)}), bf16[8,128,256]{2,1,0:T(8,128)(2,1)S(1)}, u32[]{:S(2)}, u32[]{:S(2)}) async-start(bf16[8,128,256]{2,1,0:T(8,128)(2,1)} %get-tuple-element.17), calls=%async_computation.2 | async-start | bytes 1048576 | tf_op jit(solution)/shard_map/all_to_all | solution.py:267
  150.8 16.1 %collective-permute-start.18 = (bf16[384,512]{1,0:T(8,128)(2,1)S(1)}, bf16[384,512]{1,0:T(8,128)(2,1)}, u32[]{:S(2)}, u32[]{:S(2)}) collective-permute-start(bf16[384,512]{1,0:T(8,128)(2,1)S(1)} %pad_maximum_fusion.6), channel_id=1, source_target_pairs={{0,6},{1,7},{2,0},{3,1},{4,2},{5,3},{6,4},{7,5},{8,14},{9,15},{10,... | collective-permute-start | bytes 1179656 | tf_op jit(solution)/shard_map/ppermute | solution.py:37
  161.0 0.8 copy-start.3
  161.8 29.0 %all-to-all-start.4 = ((bf16[8,128,512]{2,1,0:T(8,128)(2,1)}), bf16[8,128,512]{2,1,0:T(8,128)(2,1)S(1)}, u32[]{:S(2)}, u32[]{:S(2)}) async-start(bf16[8,128,512]{2,1,0:T(8,128)(2,1)} %get-tuple-element.19), calls=%async_computation.4 | async-start | bytes 2097152 | tf_op jit(solution)/shard_map/all_to_all | solution.py:267
  165.5 22.1 %collective-permute-start.16 = (bf16[384,512]{1,0:T(8,128)(2,1)S(1)}, bf16[384,512]{1,0:T(8,128)(2,1)S(1)}, u32[]{:S(2)}, u32[]{:S(2)}) collective-permute-start(bf16[384,512]{1,0:T(8,128)(2,1)S(1)} %pad_maximum_fusion.5), channel_id=1, source_target_pairs={{0,2},{1,3},{2,4},{3,5},{4,6},{5,7},{6,0},{7,1},{8,10},{9,11},{10,... | collective-permute-start | bytes 1179656 | tf_op jit(solution)/shard_map/ppermute | solution.py:37
  187.7 3.2 %copy-start.8 = (bf16[384,512]{1,0:T(8,128)(2,1)}, bf16[384,512]{1,0:T(8,128)(2,1)S(1)}, u32[]{:S(2)}) copy-start(bf16[384,512]{1,0:T(8,128)(2,1)S(1)} %collective-permute-done.16) | copy-start | bytes 1179652
  187.7 9.0 %copy-start.4 = (bf16[4,2,128,512]{3,2,1,0:T(8,128)(2,1)S(1)}, bf16[4,2,128,512]{3,2,1,0:T(8,128)(2,1)}, u32[]{:S(2)}) copy-start(bf16[4,2,128,512]{3,2,1,0:T(8,128)(2,1)} %pad_maximum_fusion.1) | copy-start | bytes 3145732
  190.9 8.4 %copy-start.1 = (bf16[8,128,512]{2,1,0:T(8,128)(2,1)}, bf16[8,128,512]{2,1,0:T(8,128)(2,1)S(1)}, u32[]{:S(2)}) copy-start(bf16[8,128,512]{2,1,0:T(8,128)(2,1)S(1)} %all-to-all-done.4.refs_2_) | copy-start | bytes 3145732
  190.9 39.2 %all-to-all-start.5 = ((bf16[8,128,512]{2,1,0:T(8,128)(2,1)}), bf16[8,128,512]{2,1,0:T(8,128)(2,1)S(1)}, u32[]{:S(2)}, u32[]{:S(2)}) async-start(bf16[8,128,512]{2,1,0:T(8,128)(2,1)} %bitcast.112), calls=%async_computation.5 | async-start | bytes 2097152 | tf_op jit(solution)/shard_map/all_to_all | solution.py:284
  200.6 2.0 collective-permute-start.19
  202.8 8.9 %collective-permute-start.22 = (bf16[4,12,1024]{2,1,0:T(8,128)(2,1)S(1)}, bf16[4,12,1024]{2,1,0:T(8,128)(2,1)S(1)}, u32[]{:S(2)}, u32[]{:S(2)}) collective-permute-start(bf16[4,12,1024]{2,1,0:T(8,128)(2,1)S(1)} %get-tuple-element.38), channel_id=1, source_target_pairs={{0,24},{1,25},{2,26},{3,27},{4,28},{5,29},{6,30},{7,31},{8,0},{9,1... | collective-permute-start | bytes 294920 | tf_op jit(solution)/shard_map/ppermute | solution.py:37
  205.8 7.9 %collective-permute-start.21 = (bf16[4,12,1024]{2,1,0:T(8,128)(2,1)S(1)}, bf16[4,12,1024]{2,1,0:T(8,128)(2,1)S(1)}, u32[]{:S(2)}, u32[]{:S(2)}) collective-permute-start(bf16[4,12,1024]{2,1,0:T(8,128)(2,1)S(1)} %get-tuple-element.39), channel_id=1, source_target_pairs={{0,16},{1,17},{2,18},{3,19},{4,20},{5,21},{6,22},{7,23},{8,24},{9,... | collective-permute-start | bytes 294920 | tf_op jit(solution)/shard_map/ppermute | solution.py:37
  206.6 8.7 %collective-permute-start.20 = (bf16[4,12,1024]{2,1,0:T(8,128)(2,1)S(1)}, bf16[4,12,1024]{2,1,0:T(8,128)(2,1)S(1)}, u32[]{:S(2)}, u32[]{:S(2)}) collective-permute-start(bf16[4,12,1024]{2,1,0:T(8,128)(2,1)S(1)} %get-tuple-element.37), channel_id=1, source_target_pairs={{0,8},{1,9},{2,10},{3,11},{4,12},{5,13},{6,14},{7,15},{8,16},{9,17... | collective-permute-start | bytes 294920 | tf_op jit(solution)/shard_map/ppermute | solution.py:37
  215.5 5.4 %collective-permute-start.25 = (bf16[12,1024]{1,0:T(8,128)(2,1)S(1)}, bf16[12,1024]{1,0:T(8,128)(2,1)S(1)}, u32[]{:S(2)}, u32[]{:S(2)}) collective-permute-start(bf16[12,1024]{1,0:T(8,128)(2,1)S(1)} %get-tuple-element.57), channel_id=1, source_target_pairs={{0,6},{1,7},{2,0},{3,1},{4,2},{5,3},{6,4},{7,5},{8,14},{9,15},{10,... | collective-permute-start | bytes 73736 | tf_op jit(solution)/shard_map/ppermute | solution.py:37
  216.6 8.4 %collective-permute-start.24 = (bf16[12,1024]{1,0:T(8,128)(2,1)S(1)}, bf16[12,1024]{1,0:T(8,128)(2,1)S(1)}, u32[]{:S(2)}, u32[]{:S(2)}) collective-permute-start(bf16[12,1024]{1,0:T(8,128)(2,1)S(1)} %get-tuple-element.58), channel_id=1, source_target_pairs={{0,4},{1,5},{2,6},{3,7},{4,0},{5,1},{6,2},{7,3},{8,12},{9,13},{10,... | collective-permute-start | bytes 73736 | tf_op jit(solution)/shard_map/ppermute | solution.py:37
  219.3 6.3 %collective-permute-start.23 = (bf16[12,1024]{1,0:T(8,128)(2,1)S(1)}, bf16[12,1024]{1,0:T(8,128)(2,1)S(1)}, u32[]{:S(2)}, u32[]{:S(2)}) collective-permute-start(bf16[12,1024]{1,0:T(8,128)(2,1)S(1)} %get-tuple-element.56), channel_id=1, source_target_pairs={{0,2},{1,3},{2,4},{3,5},{4,6},{5,7},{6,0},{7,1},{8,10},{9,11},{10,... | collective-permute-start | bytes 73736 | tf_op jit(solution)/shard_map/ppermute | solution.py:37

commit v3 on v2

--- a/solution.py
+++ b/solution.py
@@ -18,7 +18,7 @@
 FEATURES = 256
 SHARED_Z = [[(y * NZ + z) * NC + c for y in range(NY) for c in range(NC)] for z in range(NZ)]
 GROUPS = ((0, 2), (1, 3))
-RETURNS = ((0,), (2,), (1, 3))
+
 BF16, F32 = jnp.bfloat16, jnp.float32
 
 
@@ -46,17 +46,19 @@
     return jnp.stack([lax.select_n((owner - me) & (n - 1), *blocks) for owner in range(n)])
 
 
-def gather_encoder(block):
+def gather_encoder(block, later):
     y, z, c = place()
-    along_z = by_owner(block, [shift(block, dz=-d) for d in range(1, NZ)], z)
-    along_y = by_owner(along_z, [shift(along_z, dy=-d) for d in range(1, NY)], y)
-    other = shift(along_y, dc=1)
+    along_y = by_owner(block, [shift(block, dy=-d) for d in range(1, NY)], y)
+    along_y, later = lax.optimization_barrier((along_y, later))
+    along_z = by_owner(along_y, [shift(along_y, dz=-d) for d in range(1, NZ)], z)
+    other = shift(along_z, dc=1)
     first = c == 0
-    both = jnp.stack([jnp.where(first, along_y, other), jnp.where(first, other, along_y)], axis=2)
-    return both.reshape(NY * NZ * NC, *block.shape)
-
-
-def sum_encoder(part):
+    both = [jnp.where(first, along_z, other), jnp.where(first, other, along_z)]
+    gathered = jnp.stack(both, axis=2).swapaxes(0, 1)
+    return gathered.reshape(NY * NZ * NC, *block.shape), later
+
+
+def sum_encoder(part, later):
     y, z, c = place()
 
     def at(value, index, axis):
@@ -65,30 +67,28 @@
         size = [1 if i == axis else n for i, n in enumerate(value.shape)]
         return lax.dynamic_slice(value, start, size, allow_negative_indices=False).squeeze(axis)
 
-    arrived = shift(at(part, 1 - c, 2), dc=1)
+    sent, later = lax.optimization_barrier((at(part, 1 - c, 2), later))
+    arrived = shift(sent, dc=1)
     total = (at(part, c, 2).astype(F32) + arrived.astype(F32)).astype(BF16)
     arrived = [shift(at(total, (y + d) & 3, 0), dy=d) for d in range(1, NY)]
     total = sum((a.astype(F32) for a in arrived), at(total, y, 0).astype(F32)).astype(BF16)
     arrived = [shift(at(total, (z + d) & 3, 0), dz=d) for d in range(1, NZ)]
-    return sum((a.astype(F32) for a in arrived), at(total, z, 0).astype(F32)).astype(BF16)
-
-
-def column_block(peer, distance, z):
-    owner_y, owner_c = lax.div(peer, NC), lax.rem(peer, NC)
-    return (owner_y * NZ + lax.rem(z + distance, NZ)) * NC + owner_c
+    return sum((a.astype(F32) for a in arrived), at(total, z, 0).astype(F32)).astype(BF16), later
 
 
 def pack_kernel(z, *refs):
     sources, out = refs[:-1], refs[-1]
     for i in range(len(sources) // 2):
         for which in range(2):
-            out[0, which, :, pl.ds(i * FEATURES, FEATURES)] = sources[2 * i + which][...]
+            for c in range(NC):
+                block = sources[2 * i + which][:, pl.ds(c * FEATURES, FEATURES)]
+                out[c, which, :, pl.ds(i * FEATURES, FEATURES)] = block
 
 
 def pack(group, z, queries, grads):
     shape = (2, ROWS, len(group) * FEATURES)
     columns = [
-        pl.BlockSpec((ROWS, FEATURES), lambda p, z, d=d: (0, column_block(p, d, z[0])))
+        pl.BlockSpec((ROWS, NC * FEATURES), lambda y, z, d=d: (0, y * NZ + lax.rem(z[0] + d, NZ)))
         for d in group
         for _ in range(2)
     ]
@@ -97,9 +97,9 @@
         out_shape=jax.ShapeDtypeStruct((PEERS, *shape), BF16),
         grid_spec=pltpu.PrefetchScalarGridSpec(
             num_scalar_prefetch=1,
-            grid=(PEERS,),
+            grid=(NY,),
             in_specs=columns,
-            out_specs=pl.BlockSpec((1, *shape), lambda p, z: (p, 0, 0, 0)),
+            out_specs=pl.BlockSpec((NC, *shape), lambda y, z: (y, 0, 0, 0)),
         ),
         cost_estimate=pl.CostEstimate(
             flops=0, bytes_accessed=4 * PEERS * math.prod(shape), transcendentals=0
@@ -109,7 +109,7 @@
 
 def unpack_kernel(z, *refs):
     sources, out = refs[:-1], refs[-1]
-    for group, source in zip(RETURNS, sources, strict=True):
+    for group, source in zip(GROUPS, sources, strict=True):
         for i, distance in enumerate(group):
             for c in range(NC):
                 at = (lax.rem(z[0] + distance, NZ) * NC + c) * FEATURES
@@ -136,7 +136,8 @@
     )(z, *arrived)
 
 
-def attend_kernel(ends, rows, key, value, query_grad, key_grad, value_grad, bias):
+def attend_kernel(ends, rows, key, value, *refs):
+    query_grad, key_grad, value_grad, bias = refs[-4:]
     tile = NC * ROWS
 
     @pl.when(pl.program_id(0) == 0)
@@ -178,16 +179,17 @@
     value_grad[0] = value_total.astype(BF16)
 
 
-def attend(ends, rows, first, keys, values):
+def attend(ends, rows, first, keys, values, into=None):
     count = keys.shape[0]
     heads = FEATURES // HEAD_DIM
+    given = [] if into is None else [into]
     elements = count * heads * PEERS * ROWS * KEYS
     block = (1, KEYS, HEAD_DIM)
     in_block = lambda h, ends: (h // heads, 0, h % heads)
     grads = jax.ShapeDtypeStruct((count, KEYS, FEATURES), BF16)
     return pl.pallas_call(
         attend_kernel,
-        out_shape=(jax.ShapeDtypeStruct((PEERS, ROWS, count * FEATURES), BF16), grads, grads),
+        out_shape=(jax.ShapeDtypeStruct((PEERS, ROWS, rows.shape[3]), BF16), grads, grads),
         grid_spec=pltpu.PrefetchScalarGridSpec(
             num_scalar_prefetch=1,
             grid=(count * heads,),
@@ -197,9 +199,10 @@
                 ),
                 pl.BlockSpec(block, in_block),
                 pl.BlockSpec(block, in_block),
+                *[pl.BlockSpec(memory_space=pl.ANY) for _ in given],
             ],
             out_specs=(
-                pl.BlockSpec((PEERS, ROWS, HEAD_DIM), lambda h, ends: (0, 0, h)),
+                pl.BlockSpec((PEERS, ROWS, HEAD_DIM), lambda h, ends: (0, 0, first * heads + h)),
                 pl.BlockSpec(block, in_block),
                 pl.BlockSpec(block, in_block),
             ),
@@ -209,32 +212,31 @@
         cost_estimate=pl.CostEstimate(
             flops=elements * HEAD_DIM * 10, bytes_accessed=6 * 2**20, transcendentals=elements
         ),
-    )(ends, rows, keys, values)
+        input_output_aliases={4: 0} if given else {},
+    )(ends, rows, keys, values, *given)
 
 
 def gather_weights(block):
     me = lax.axis_index("dp")
-    x, low = me >> 1, me & 1
-
-    def ahead(value, dx, dl):
-        pairs = [
-            (a * NL + b, (a - dx) % NX * NL + (b - dl) % NL) for a in range(NX) for b in range(NL)
-        ]
-        return lax.ppermute(value, "dp", pairs)
-
-    pair = by_owner(block, [ahead(block, 0, 1)], low)
-    return by_owner(pair, [ahead(pair, d, 0) for d in range(1, NX)], x).reshape(-1, block.shape[1])
+    held = block[None]
+    for bit in (1, 2, 4):
+        other = lax.ppermute(held, "dp", [(d, d ^ bit) for d in range(NX * NL)])
+        first = (me & bit) == 0
+        held = jnp.concatenate([jnp.where(first, held, other), jnp.where(first, other, held)])
+    return held.reshape(-1, block.shape[1])
 
 
 def body(queries, out_grad, enc_states, w_key, w_value, dec_segments, enc_segments):
     z = place()[1]
     z_index = z.reshape(1)
-    below = [jnp.sum(ids < d) for ids in (enc_segments, dec_segments) for d in range(1, 4)]
-    counts = jnp.stack(below).astype(BF16)
-    last_rows = jnp.pad(counts[None], ((0, 3), (0, enc_states.shape[1] - 6)))
-    gathered = gather_encoder(jnp.concatenate([enc_states, last_rows], axis=0))
+    width = enc_states.shape[1]
+    ids = [jnp.pad(i.astype(BF16)[None], ((0, 0), (0, width - i.size))) for i in (enc_segments, dec_segments)]
+    block = jnp.concatenate([enc_states, *ids, jnp.zeros((2, width), BF16)], axis=0)
+    gathered, z_later = gather_encoder(block, z_index)
     encoder = gathered[:, :ENC_ROWS].reshape(KEYS, -1)
-    ends = jnp.sum(gathered[:, ENC_ROWS, :6].astype(jnp.int32), axis=0)
+    all_ids = (gathered[:, ENC_ROWS, :ENC_ROWS], gathered[:, ENC_ROWS + 1, :ROWS])
+    first_of = jnp.arange(1, 4, dtype=BF16)[:, None, None]
+    ends = jnp.concatenate([jnp.sum((i[None] < first_of).astype(jnp.int32), axis=(1, 2)) for i in all_ids])
     weight = gather_weights(jnp.concatenate([w_key, w_value], axis=1))
 
     swap = functools.partial(
@@ -247,7 +249,7 @@
     )
     near = swap(pack(GROUPS[0], z_index, queries, out_grad))
     own = jnp.dot(encoder, weight, preferred_element_type=F32).astype(BF16)
-    far_packed, near = lax.optimization_barrier((pack(GROUPS[1], z_index, queries, out_grad), near))
+    far_packed, near = lax.optimization_barrier((pack(GROUPS[1], z_later, queries, out_grad), near))
     far = swap(far_packed)
 
     ahead, behind = shift(own, dz=-1), shift(own, dz=1)
@@ -255,29 +257,35 @@
     value_of = lambda block: block[:, FEATURES:]
     key_opposite, value_opposite = shift(key_of(ahead), dz=-1), shift(value_of(behind), dz=1)
 
-    back_0, key_0, value_0 = attend(ends, near, 0, key_of(own)[None], value_of(own)[None])
-    back_2, key_2, value_2 = attend(ends, near, 1, key_opposite[None], value_opposite[None])
-    back_1, key_1, value_1 = attend(
+    back, key_0, value_0 = attend(ends, near, 0, key_of(own)[None], value_of(own)[None])
+    back, key_2, value_2 = attend(ends, near, 1, key_opposite[None], value_opposite[None], back)
+    back_near = swap(back)
+    back, key_1, value_1 = attend(
         ends,
         far,
         0,
         jnp.stack([key_of(ahead), key_of(behind)]),
         jnp.stack([value_of(ahead), value_of(behind)]),
     )
-    query_grad = unpack(z_index, [swap(back_0), swap(back_2), swap(back_1)])
 
     def joined(a, b):
         return (a.astype(F32) + b.astype(F32)).astype(BF16)
 
     key_ahead = joined(key_1[0], shift(key_2[0], dz=1))
     value_behind = joined(value_1[1], shift(value_2[0], dz=-1))
+    for_ahead = jnp.concatenate([key_ahead, value_1[0]], axis=1)
+    for_behind = jnp.concatenate([key_1[1], value_behind], axis=1)
+    for_ahead, for_behind, back = lax.optimization_barrier((for_ahead, for_behind, back))
     total = jnp.concatenate([key_0[0], value_0[0]], axis=1).astype(F32)
-    total += shift(jnp.concatenate([key_ahead, value_1[0]], axis=1), dz=1).astype(F32)
-    total += shift(jnp.concatenate([key_1[1], value_behind], axis=1), dz=-1).astype(F32)
+    total += shift(for_ahead, dz=1).astype(F32) + shift(for_behind, dz=-1).astype(F32)
+
+    query_grad = unpack(z_index, [back_near, swap(back)])
+    total, query_grad = lax.optimization_barrier((total, query_grad))
 
     rounded = total.astype(BF16)
     part = lax.dot_general(rounded, weight, (((1,), (1,)), ((), ())), preferred_element_type=F32)
-    enc_grad = sum_encoder(part.astype(BF16).reshape(NY, NZ, NC, ENC_ROWS, -1))
+    part = part.astype(BF16).reshape(NY, NZ, NC, ENC_ROWS, -1)
+    enc_grad, encoder = sum_encoder(part, encoder)
 
     term = lax.dot_general(encoder, rounded, (((0,), (0,)), ((), ())), preferred_element_type=F32)
     pieces = term.astype(BF16).reshape(NX * NL, -1, 2 * FEATURES)

time: 233 us -> 202 us (0.87)
  waiting for transfers between devices: 93.3 us -> 71.8 us
  between operations: 4.81 us -> 0.97 us
  Pallas kernels: 39.4 us -> 35.8 us
  matrix products: 7.83 us -> 4.58 us
  starting transfers between devices: 70.6 us -> 67.5 us
  local copies, waits for them, and re-layouts: 5.08 us -> 8.05 us
    ppermute x22, waiting for transfers between devices: 79.8 us -> 59.8 us  [shift(): return lax.ppermute(value, 'ctx', pairs)]
    all_to_all x3 -> x2, waiting for transfers between devices: 9 us -> 4.11 us  [the longest x1 4.11 us: body(): back_near = swap(back)]
    all_to_all x3 -> x2, starting transfers between devices: 12.7 us -> 7.92 us  [the longest x1 4.37 us: body(): back_near = swap(back)]
    pallas_call x2, Pallas kernels: 11.3 us -> 7.65 us  [pack(): pl.pallas_call(pack_kernel, out_shape=jax.ShapeDtypeStruct((PEERS, *shape...]
    ppermute x4 -> x3, waiting for transfers between devices: 4.42 us -> 7.87 us  [gather_weights(): other = lax.ppermute(held, 'dp', [(d, d ^ bit) for d in range(NX * NL)])]
    reduce_sum x3 -> x2, other arithmetic: 3.56 us -> 0.47 us  [body(): jnp.sum((i[None] < first_of).astype(jnp.int32), axis=(1, 2))]
    ppermute x22, starting transfers between devices: 39.3 us -> 41.8 us  [shift(): return lax.ppermute(value, 'ctx', pairs)]
    concatenate x3 -> x7, other arithmetic: 0.82 us -> 3.21 us  [the longest x3 2.24 us: gather_weights(): jnp.concatenate([jnp.where(first, held, other), jnp.where(first, other, h...]
  transfers between devices with their start and end apart: 32 -> 30, of which waited for: 15 -> 14; matrix products, arithmetic and copies ran while one was open for 8% -> 7% of each run, Pallas kernels for 17% -> 16%
where the time goes in v3:
time: 202 us; the launch traced here: 201 us
  waiting for transfers between devices  71.8 us (36%)
  starting transfers between devices  67.5 us (33%)
  Pallas kernels  35.8 us (18%)
  other arithmetic  11.9 us (6%)
  local copies, waits for them, and re-layouts  8.05 us (4%)
  matrix products  4.58 us (2%)
    ppermute x22, waiting for transfers between devices, shift(): return lax.ppermute(value, 'ctx', pairs)  59.8 us
    ppermute x22, starting transfers between devices, shift(): return lax.ppermute(value, 'ctx', pairs)  41.8 us
    pallas_call x3, Pallas kernels, attend(): pl.pallas_call(attend_kernel, out_shape=(jax.ShapeDtypeStruct((PEERS, ROW...  24.3 us
    ppermute x3, waiting for transfers between devices, gather_weights(): other = lax.ppermute(held, 'dp', [(d, d ^ bit) for d in range(NX * NL)])  7.87 us
    pallas_call x2, Pallas kernels, pack(): pl.pallas_call(pack_kernel, out_shape=jax.ShapeDtypeStruct((PEERS, *shape...  7.65 us
    all_to_all x1, starting transfers between devices, body(): pieces = lax.all_to_all(pieces, 'dp', 0, 0, tiled=True)  4.82 us
    ppermute x3, starting transfers between devices, gather_weights(): other = lax.ppermute(held, 'dp', [(d, d ^ bit) for d in range(NX * NL)])  4.78 us
    all_to_all x1, starting transfers between devices, body(): far = swap(far_packed)  4.47 us
  transfers between devices with their start and end apart: 30, of which 14 were waited for; matrix products, arithmetic and copies ran while one was open for 7% of the time, Pallas kernels for 16%

profile of v3, /device:TPU:2, one launch (start us, length us, event | category | flops | bytes accessed | tf_op | source)
XLA Modules:
  0.0 200.6 jit_solution(2322348000566427621)
XLA Ops:
  2.9 3.2 %collective-permute-start.1 = (bf16[16,1024]{1,0:T(8,128)(2,1)S(1)}, bf16[16,1024]{1,0:T(8,128)(2,1)S(1)}, u32[]{:S(2)}, u32[]{:S(2)}) collective-permute-start(bf16[16,1024]{1,0:T(8,128)(2,1)S(1)} %fusion.16), channel_id=1, source_target_pairs={{0,16},{1,17},{2,18},{3,19},{4,20},{5,21},{6,22},{7,23},{8,24},{9,... | collective-permute-start | bytes 98312 | tf_op jit(solution)/shard_map/ppermute | solution.py:37
  6.8 2.6 %collective-permute-start = (bf16[16,1024]{1,0:T(8,128)(2,1)S(1)}, bf16[16,1024]{1,0:T(8,128)(2,1)S(1)}, u32[]{:S(2)}, u32[]{:S(2)}) collective-permute-start(bf16[16,1024]{1,0:T(8,128)(2,1)S(1)} %fusion.16), channel_id=1, source_target_pairs={{0,24},{1,25},{2,26},{3,27},{4,28},{5,29},{6,30},{7,31},{8,0},{9,1... | collective-permute-start | bytes 98312 | tf_op jit(solution)/shard_map/ppermute | solution.py:37
  9.3 3.8 %shard_map.103 = bf16[8,2,128,512]{3,2,1,0:T(8,128)(2,1)} custom-call(s32[1]{0:T(128)} %bitcast.6.z, bf16[128,8192]{1,0:T(8,128)(2,1)} %refs_2_.3, bf16[128,8192]{1,0:T(8,128)(2,1)} %refs_3_.3, bf16[128,8192]{1,0:T(8,128)(2,1)} %refs_2_.3, bf16[128,8192]{1,0:T(8,128)(2,1)} %refs_3_.3), custom_call_target="tpu_custom_call" | custom-call | bytes 4194304 | tf_op jit(solution)/shard_map/pallas_call | solution.py:95
  13.2 3.7 %all-to-all-start = ((bf16[8,2,128,512]{3,2,1,0:T(8,128)(2,1)}), bf16[8,2,128,512]{3,2,1,0:T(8,128)(2,1)S(1)}, u32[]{:S(2)}, u32[]{:S(2)}) async-start(bf16[8,2,128,512]{3,2,1,0:T(8,128)(2,1)} %shard_map.103), calls=%async_computation | async-start | bytes 4194304 | tf_op jit(solution)/shard_map/all_to_all | solution.py:250
  17.0 2.0 %collective-permute-start.7 = (bf16[1,128,512]{2,1,0:T(8,128)(2,1)S(1)}, bf16[1,128,512]{2,1,0:T(8,128)(2,1)S(1)}, u32[]{:S(2)}, u32[]{:S(2)}) collective-permute-start(bf16[1,128,512]{2,1,0:T(8,128)(2,1)S(1)} %maximum_bitcast_fusion), channel_id=1, source_target_pairs={{0,32},{32,0},{64,96},{96,64},{128,160},{160,128},{192,224},{224,1... | collective-permute-start | bytes 393224 | tf_op jit(solution)/shard_map/ppermute | solution.py:223
  19.1 6.4 %collective-permute-start.4 = (bf16[4,16,1024]{2,1,0:T(8,128)(2,1)S(1)}, bf16[4,16,1024]{2,1,0:T(8,128)(2,1)S(1)}, u32[]{:S(2)}, u32[]{:S(2)}) collective-permute-start(bf16[4,16,1024]{2,1,0:T(8,128)(2,1)S(1)} %pad_maximum_fusion.9), channel_id=1, source_target_pairs={{0,4},{1,5},{2,6},{3,7},{4,0},{5,1},{6,2},{7,3},{8,12},{9,13},{10,... | collective-permute-start | bytes 393224 | tf_op jit(solution)/shard_map/ppermute | solution.py:37
  25.5 1.5 collective-permute-start.5
  27.0 2.7 %collective-permute-start.3 = (bf16[4,16,1024]{2,1,0:T(8,128)(2,1)S(1)}, bf16[4,16,1024]{2,1,0:T(8,128)(2,1)S(1)}, u32[]{:S(2)}, u32[]{:S(2)}) collective-permute-start(bf16[4,16,1024]{2,1,0:T(8,128)(2,1)S(1)} %pad_maximum_fusion.9), channel_id=1, source_target_pairs={{0,6},{1,7},{2,0},{3,1},{4,2},{5,3},{6,4},{7,5},{8,14},{9,15},{10,... | collective-permute-start | bytes 393224 | tf_op jit(solution)/shard_map/ppermute | solution.py:37
  30.4 3.8 %collective-permute-done.4 = bf16[4,16,1024]{2,1,0:T(8,128)(2,1)S(1)} collective-permute-done((bf16[4,16,1024]{2,1,0:T(8,128)(2,1)S(1)}, bf16[4,16,1024]{2,1,0:T(8,128)(2,1)S(1)}, u32[]{:S(2)}, u32[]{:S(2)}) %collective-permute-start.4) | collective-permute-done | bytes 131104 | tf_op jit(solution)/shard_map/ppermute | solution.py:37
  34.2 5.2 %collective-permute-done.5 = bf16[4,16,1024]{2,1,0:T(8,128)(2,1)S(1)} collective-permute-done((bf16[4,16,1024]{2,1,0:T(8,128)(2,1)S(1)}, bf16[4,16,1024]{2,1,0:T(8,128)(2,1)S(1)}, u32[]{:S(2)}, u32[]{:S(2)}) %collective-permute-start.5) | collective-permute-done | bytes 131104 | tf_op jit(solution)/shard_map/ppermute | solution.py:37
  41.9 2.1 %collective-permute-start.9 = (bf16[4,128,512]{2,1,0:T(8,128)(2,1)}, bf16[4,128,512]{2,1,0:T(8,128)(2,1)}, u32[]{:S(2)}, u32[]{:S(2)}) collective-permute-start(bf16[4,128,512]{2,1,0:T(8,128)(2,1)} %pad_maximum_fusion.3), channel_id=1, source_target_pairs={{0,128},{32,160},{64,192},{96,224},{128,0},{160,32},{192,64},{224,... | collective-permute-start | bytes 1572872 | tf_op jit(solution)/shard_map/ppermute | solution.py:223
  44.0 3.8 %shard_map.102 = bf16[8,2,128,512]{3,2,1,0:T(8,128)(2,1)} custom-call(s32[1]{0:T(128)} %bitcast.6.z, bf16[128,8192]{1,0:T(8,128)(2,1)} %refs_2_.3, bf16[128,8192]{1,0:T(8,128)(2,1)} %refs_3_.3, bf16[128,8192]{1,0:T(8,128)(2,1)} %refs_2_.3, bf16[128,8192]{1,0:T(8,128)(2,1)} %refs_3_.3), custom_call_target="tpu_custom_call" | custom-call | bytes 4194304 | tf_op jit(solution)/shard_map/pallas_call | solution.py:95
  50.2 7.9 %collective-permute-done.9 = bf16[4,128,512]{2,1,0:T(8,128)(2,1)} collective-permute-done((bf16[4,128,512]{2,1,0:T(8,128)(2,1)}, bf16[4,128,512]{2,1,0:T(8,128)(2,1)}, u32[]{:S(2)}, u32[]{:S(2)}) %collective-permute-start.9) | collective-permute-done | bytes 524320 | tf_op jit(solution)/shard_map/ppermute | solution.py:223
  58.1 2.2 %broadcast_select_fusion.1 = (bf16[4,128,512]{2,1,0:T(8,128)(2,1)}, bf16[4,128,512]{2,1,0:T(8,128)(2,1)}) fusion(bf16[4,128,512]{2,1,0:T(8,128)(2,1)} %collective-permute-done.9, pred[]{:T(512)S(6)} %eq.13, bf16[2,128,512]{2,1,0:T(8,128)(2,1)} %copy-done.1, bf16[2,128,512]{2,1,0:T(8,128)(2,1)S(1)} %get-tuple-element.51), kind=kLoop, calls=%fused_computation.15 | loop fusion | flops 786432 | bytes 2097153 | tf_op jit(solution)/shard_map/jit(_where)/select_n | solution.py:225
  60.2 4.5 %all-to-all-start.1 = ((bf16[8,2,128,512]{3,2,1,0:T(8,128)(2,1)}), bf16[8,2,128,512]{3,2,1,0:T(8,128)(2,1)}, u32[]{:S(2)}, u32[]{:S(2)}) async-start(bf16[8,2,128,512]{3,2,1,0:T(8,128)(2,1)} %shard_map.102), calls=%async_computation.1 | async-start | bytes 4194304 | tf_op jit(solution)/shard_map/all_to_all | solution.py:253
  64.7 1.4 pad_maximum_fusion.1
  66.2 1.3 convolution_convert_fusion.2
  67.5 2.6 %collective-permute-start.10 = (bf16[384,512]{1,0:T(8,128)(2,1)}, bf16[384,512]{1,0:T(8,128)(2,1)}, u32[]{:S(2)}, u32[]{:S(2)}) collective-permute-start(bf16[384,512]{1,0:T(8,128)(2,1)} %convolution_convert_fusion.2), channel_id=1, source_target_pairs={{0,6},{1,7},{2,0},{3,1},{4,2},{5,3},{6,4},{7,5},{8,14},{9,15},{10,... | collective-permute-start | bytes 1179656 | tf_op jit(solution)/shard_map/ppermute | solution.py:37
  71.2 17.5 %collective-permute-done.10 = bf16[384,512]{1,0:T(8,128)(2,1)} collective-permute-done((bf16[384,512]{1,0:T(8,128)(2,1)}, bf16[384,512]{1,0:T(8,128)(2,1)}, u32[]{:S(2)}, u32[]{:S(2)}) %collective-permute-start.10) | collective-permute-done | bytes 393248 | tf_op jit(solution)/shard_map/ppermute | solution.py:37
  89.8 3.3 %collective-permute-start.12 = (bf16[384,256]{1,0:T(8,128)(2,1)S(1)}, bf16[384,256]{1,0:T(8,128)(2,1)S(1)}, u32[]{:S(2)}, u32[]{:S(2)}) collective-permute-start(bf16[384,256]{1,0:T(8,128)(2,1)S(1)} %get-tuple-element.62), channel_id=1, source_target_pairs={{0,6},{1,7},{2,0},{3,1},{4,2},{5,3},{6,4},{7,5},{8,14},{9,15},{10,... | collective-permute-start | bytes 589832 | tf_op jit(solution)/shard_map/ppermute | solution.py:37
  94.4 6.3 %shard_map.104 = (bf16[8,128,512]{2,1,0:T(8,128)(2,1)}, bf16[1,384,256]{2,1,0:T(8,128)(2,1)S(1)}, bf16[1,384,256]{2,1,0:T(8,128)(2,1)S(1)}) custom-call(s32[6]{0:T(128)S(1)} %pad_add_fusion.ends, bf16[8,2,128,512]{3,2,1,0:T(8,128)(2,1)S(1)} %all-to-all-done.rows, bf16[1,384,256]{2,1,0:T(8,128)(2,1)S(1)} %get-tuple-element.58.key, ...), custom_call_target="tpu_custom_call" | custom-call | flops 1006632960 | bytes 6291456 | tf_op jit(solution)/shard_map/pallas_call | solution.py:190
  100.7 2.0 collective-permute-done.13
  102.7 6.3 %shard_map.106 = (bf16[8,128,512]{2,1,0:T(8,128)(2,1)}, bf16[1,384,256]{2,1,0:T(8,128)(2,1)S(1)}, bf16[1,384,256]{2,1,0:T(8,128)(2,1)S(1)}) custom-call(s32[6]{0:T(128)S(1)} %pad_add_fusion.ends, bf16[8,2,128,512]{3,2,1,0:T(8,128)(2,1)S(1)} %all-to-all-done.rows, bf16[1,384,256]{2,1,0:T(8,128)(2,1)S(1)} %bitcast.110, ...), custom_call_target="tpu_custom_call", output_to_operand_aliasing={{0}: (4, {})} | custom-call | flops 1006632960 | bytes 6291456 | tf_op jit(solution)/shard_map/pallas_call | solution.py:190
  109.0 2.1 %collective-permute-start.14 = (bf16[384,256]{1,0:T(8,128)(2,1)S(1)}, bf16[384,256]{1,0:T(8,128)(2,1)S(1)}, u32[]{:S(2)}, u32[]{:S(2)}) collective-permute-start(bf16[384,256]{1,0:T(8,128)(2,1)S(1)} %bitcast.109), channel_id=1, source_target_pairs={{0,2},{1,3},{2,4},{3,5},{4,6},{5,7},{6,0},{7,1},{8,10},{9,11},{10,... | collective-permute-start | bytes 589832 | tf_op jit(solution)/shard_map/ppermute | solution.py:37
  111.1 2.1 %collective-permute-start.15 = (bf16[384,256]{1,0:T(8,128)(2,1)S(1)}, bf16[384,256]{1,0:T(8,128)(2,1)S(1)}, u32[]{:S(2)}, u32[]{:S(2)}) collective-permute-start(bf16[384,256]{1,0:T(8,128)(2,1)S(1)} %bitcast.108), channel_id=1, source_target_pairs={{0,6},{1,7},{2,0},{3,1},{4,2},{5,3},{6,4},{7,5},{8,14},{9,15},{10,... | collective-permute-start | bytes 589832 | tf_op jit(solution)/shard_map/ppermute | solution.py:37
  113.3 4.4 %all-to-all-start.2 = ((bf16[8,128,512]{2,1,0:T(8,128)(2,1)}), bf16[8,128,512]{2,1,0:T(8,128)(2,1)}, u32[]{:S(2)}, u32[]{:S(2)}) async-start(bf16[8,128,512]{2,1,0:T(8,128)(2,1)} %get-tuple-element.38), calls=%async_computation.2 | async-start | bytes 2097152 | tf_op jit(solution)/shard_map/all_to_all | solution.py:262
  117.7 11.7 %shard_map.105 = (bf16[8,128,512]{2,1,0:T(8,128)(2,1)}, bf16[2,384,256]{2,1,0:T(8,128)(2,1)S(1)}, bf16[2,384,256]{2,1,0:T(8,128)(2,1)S(1)}) custom-call(s32[6]{0:T(128)S(1)} %pad_add_fusion.ends, bf16[8,2,128,512]{3,2,1,0:T(8,128)(2,1)} %all-to-all-done.1.rows, bf16[2,384,256]{2,1,0:T(8,128)(2,1)S(1)} %get-tuple-element.76.key, ...), custom_call_target="tpu_custom_call" | custom-call | flops 2013265920 | bytes 6291456 | tf_op jit(solution)/shard_map/pallas_call | solution.py:190
  129.6 4.1 %all-to-all-done.2.refs_0_ = bf16[8,128,512]{2,1,0:T(8,128)(2,1)} async-done(((bf16[8,128,512]{2,1,0:T(8,128)(2,1)}), bf16[8,128,512]{2,1,0:T(8,128)(2,1)}, u32[]{:S(2)}, u32[]{:S(2)}) %all-to-all-start.2) | async-done | bytes 1048608 | tf_op jit(solution)/shard_map/all_to_all | solution.py:262
  133.7 3.6 %all-to-all-start.3 = ((bf16[8,128,512]{2,1,0:T(8,128)(2,1)}), bf16[8,128,512]{2,1,0:T(8,128)(2,1)S(1)}, u32[]{:S(2)}, u32[]{:S(2)}) async-start(bf16[8,128,512]{2,1,0:T(8,128)(2,1)} %get-tuple-element.39), calls=%async_computation.3 | async-start | bytes 2097152 | tf_op jit(solution)/shard_map/all_to_all | solution.py:282
  138.4 1.9 collective-permute-start.16
  140.3 14.9 %collective-permute-done.17 = bf16[384,512]{1,0:T(8,128)(2,1)S(1)} collective-permute-done((bf16[384,512]{1,0:T(8,128)(2,1)S(1)}, bf16[384,512]{1,0:T(8,128)(2,1)S(1)}, u32[]{:S(2)}, u32[]{:S(2)}) %collective-permute-start.17) | collective-permute-done | bytes 393248 | tf_op jit(solution)/shard_map/ppermute | solution.py:37
  155.2 1.4 collective-permute-done.16
  157.4 1.1 add_add_fusion
  159.5 3.8 %shard_map.107 = bf16[128,8192]{1,0:T(8,128)(2,1)} custom-call(s32[1]{0:T(128)} %bitcast.6.z, bf16[8,128,512]{2,1,0:T(8,128)(2,1)} %all-to-all-done.2.refs_0_, bf16[8,128,512]{2,1,0:T(8,128)(2,1)} %copy-done), custom_call_target="tpu_custom_call" | custom-call | bytes 4194304 | tf_op jit(solution)/shard_map/pallas_call | solution.py:122
  163.3 1.5 convolution_convert_fusion.1
  164.8 1.2 reshape.46
  166.2 1.8 convolution_convert_fusion
  167.9 4.8 %all-to-all-start.4 = ((bf16[8,128,512]{2,1,0:T(8,128)(2,1)}), bf16[8,128,512]{2,1,0:T(8,128)(2,1)S(1)}, u32[]{:S(2)}, u32[]{:S(2)}) async-start(bf16[8,128,512]{2,1,0:T(8,128)(2,1)} %bitcast.49), calls=%async_computation.4 | async-start | bytes 2097152 | tf_op jit(solution)/shard_map/all_to_all | solution.py:292
  172.7 1.9 collective-permute-done.18
  174.9 3.0 %collective-permute-start.21 = (bf16[4,12,1024]{2,1,0:T(8,128)(2,1)S(1)}, bf16[4,12,1024]{2,1,0:T(8,128)(2,1)S(1)}, u32[]{:S(2)}, u32[]{:S(2)}) collective-permute-start(bf16[4,12,1024]{2,1,0:T(8,128)(2,1)S(1)} %get-tuple-element.49), channel_id=1, source_target_pairs={{0,24},{1,25},{2,26},{3,27},{4,28},{5,29},{6,30},{7,31},{8,0},{9,1... | collective-permute-start | bytes 294920 | tf_op jit(solution)/shard_map/ppermute | solution.py:37
  179.6 4.2 %collective-permute-done.21 = bf16[4,12,1024]{2,1,0:T(8,128)(2,1)S(1)} collective-permute-done((bf16[4,12,1024]{2,1,0:T(8,128)(2,1)S(1)}, bf16[4,12,1024]{2,1,0:T(8,128)(2,1)S(1)}, u32[]{:S(2)}, u32[]{:S(2)}) %collective-permute-start.21) | collective-permute-done | bytes 98336 | tf_op jit(solution)/shard_map/ppermute | solution.py:37
  183.8 2.0 %collective-permute-done.20 = bf16[4,12,1024]{2,1,0:T(8,128)(2,1)S(1)} collective-permute-done((bf16[4,12,1024]{2,1,0:T(8,128)(2,1)S(1)}, bf16[4,12,1024]{2,1,0:T(8,128)(2,1)S(1)}, u32[]{:S(2)}, u32[]{:S(2)}) %collective-permute-start.20) | collective-permute-done | bytes 98336 | tf_op jit(solution)/shard_map/ppermute | solution.py:37
  185.8 1.7 collective-permute-done.19
  187.6 2.1 %collective-permute-start.24 = (bf16[12,1024]{1,0:T(8,128)(2,1)S(1)}, bf16[12,1024]{1,0:T(8,128)(2,1)S(1)}, u32[]{:S(2)}, u32[]{:S(2)}) collective-permute-start(bf16[12,1024]{1,0:T(8,128)(2,1)S(1)} %get-tuple-element.70), channel_id=1, source_target_pairs={{0,6},{1,7},{2,0},{3,1},{4,2},{5,3},{6,4},{7,5},{8,14},{9,15},{10,... | collective-permute-start | bytes 73736 | tf_op jit(solution)/shard_map/ppermute | solution.py:37
  189.7 3.0 %collective-permute-start.23 = (bf16[12,1024]{1,0:T(8,128)(2,1)S(1)}, bf16[12,1024]{1,0:T(8,128)(2,1)S(1)}, u32[]{:S(2)}, u32[]{:S(2)}) collective-permute-start(bf16[12,1024]{1,0:T(8,128)(2,1)S(1)} %get-tuple-element.71), channel_id=1, source_target_pairs={{0,4},{1,5},{2,6},{3,7},{4,0},{5,1},{6,2},{7,3},{8,12},{9,13},{10,... | collective-permute-start | bytes 73736 | tf_op jit(solution)/shard_map/ppermute | solution.py:37
  192.7 1.2 collective-permute-start.22
  193.9 3.9 %collective-permute-done.23 = bf16[12,1024]{1,0:T(8,128)(2,1)S(1)} collective-permute-done((bf16[12,1024]{1,0:T(8,128)(2,1)S(1)}, bf16[12,1024]{1,0:T(8,128)(2,1)S(1)}, u32[]{:S(2)}, u32[]{:S(2)}) %collective-permute-start.23) | collective-permute-done | bytes 24608 | tf_op jit(solution)/shard_map/ppermute | solution.py:37
  197.9 1.2 collective-permute-done.22
  (88 shorter events, 18.8 us)
Async XLA Ops:
  2.9 16.1 %collective-permute-start.1 = (bf16[16,1024]{1,0:T(8,128)(2,1)S(1)}, bf16[16,1024]{1,0:T(8,128)(2,1)S(1)}, u32[]{:S(2)}, u32[]{:S(2)}) collective-permute-start(bf16[16,1024]{1,0:T(8,128)(2,1)S(1)} %fusion.16), channel_id=1, source_target_pairs={{0,16},{1,17},{2,18},{3,19},{4,20},{5,21},{6,22},{7,23},{8,24},{9,... | collective-permute-start | bytes 98312 | tf_op jit(solution)/shard_map/ppermute | solution.py:37
  6.1 12.9 %collective-permute-start.2 = (bf16[16,1024]{1,0:T(8,128)(2,1)S(1)}, bf16[16,1024]{1,0:T(8,128)(2,1)S(1)}, u32[]{:S(2)}, u32[]{:S(2)}) collective-permute-start(bf16[16,1024]{1,0:T(8,128)(2,1)S(1)} %fusion.16), channel_id=1, source_target_pairs={{0,8},{1,9},{2,10},{3,11},{4,12},{5,13},{6,14},{7,15},{8,16},{9,17... | collective-permute-start | bytes 98312 | tf_op jit(solution)/shard_map/ppermute | solution.py:37
  6.8 12.2 %collective-permute-start = (bf16[16,1024]{1,0:T(8,128)(2,1)S(1)}, bf16[16,1024]{1,0:T(8,128)(2,1)S(1)}, u32[]{:S(2)}, u32[]{:S(2)}) collective-permute-start(bf16[16,1024]{1,0:T(8,128)(2,1)S(1)} %fusion.16), channel_id=1, source_target_pairs={{0,24},{1,25},{2,26},{3,27},{4,28},{5,29},{6,30},{7,31},{8,0},{9,1... | collective-permute-start | bytes 98312 | tf_op jit(solution)/shard_map/ppermute | solution.py:37
  13.1 3.8 %copy-start.7 = (bf16[128,256]{1,0:T(8,128)(2,1)S(1)}, bf16[128,256]{1,0:T(8,128)(2,1)}, u32[]{:S(2)}) copy-start(bf16[128,256]{1,0:T(8,128)(2,1)} %param.11) | copy-start | bytes 196612
  13.2 3.8 %copy-start.8 = (bf16[128,256]{1,0:T(8,128)(2,1)S(1)}, bf16[128,256]{1,0:T(8,128)(2,1)}, u32[]{:S(2)}) copy-start(bf16[128,256]{1,0:T(8,128)(2,1)} %param.10) | copy-start | bytes 196612
  13.2 5.9 %copy-start.9 = (bf16[12,1024]{1,0:T(8,128)(2,1)S(1)}, bf16[12,1024]{1,0:T(8,128)(2,1)}, u32[]{:S(2)}) copy-start(bf16[12,1024]{1,0:T(8,128)(2,1)} %param.9) | copy-start | bytes 73732
  13.2 47.1 %all-to-all-start = ((bf16[8,2,128,512]{3,2,1,0:T(8,128)(2,1)}), bf16[8,2,128,512]{3,2,1,0:T(8,128)(2,1)S(1)}, u32[]{:S(2)}, u32[]{:S(2)}) async-start(bf16[8,2,128,512]{3,2,1,0:T(8,128)(2,1)} %shard_map.103), calls=%async_computation | async-start | bytes 4194304 | tf_op jit(solution)/shard_map/all_to_all | solution.py:250
  17.0 12.7 %collective-permute-start.7 = (bf16[1,128,512]{2,1,0:T(8,128)(2,1)S(1)}, bf16[1,128,512]{2,1,0:T(8,128)(2,1)S(1)}, u32[]{:S(2)}, u32[]{:S(2)}) collective-permute-start(bf16[1,128,512]{2,1,0:T(8,128)(2,1)S(1)} %maximum_bitcast_fusion), channel_id=1, source_target_pairs={{0,32},{32,0},{64,96},{96,64},{128,160},{160,128},{192,224},{224,1... | collective-permute-start | bytes 393224 | tf_op jit(solution)/shard_map/ppermute | solution.py:223
  19.1 15.0 %collective-permute-start.4 = (bf16[4,16,1024]{2,1,0:T(8,128)(2,1)S(1)}, bf16[4,16,1024]{2,1,0:T(8,128)(2,1)S(1)}, u32[]{:S(2)}, u32[]{:S(2)}) collective-permute-start(bf16[4,16,1024]{2,1,0:T(8,128)(2,1)S(1)} %pad_maximum_fusion.9), channel_id=1, source_target_pairs={{0,4},{1,5},{2,6},{3,7},{4,0},{5,1},{6,2},{7,3},{8,12},{9,13},{10,... | collective-permute-start | bytes 393224 | tf_op jit(solution)/shard_map/ppermute | solution.py:37
  25.5 13.8 %collective-permute-start.5 = (bf16[4,16,1024]{2,1,0:T(8,128)(2,1)S(1)}, bf16[4,16,1024]{2,1,0:T(8,128)(2,1)S(1)}, u32[]{:S(2)}, u32[]{:S(2)}) collective-permute-start(bf16[4,16,1024]{2,1,0:T(8,128)(2,1)S(1)} %pad_maximum_fusion.9), channel_id=1, source_target_pairs={{0,2},{1,3},{2,4},{3,5},{4,6},{5,7},{6,0},{7,1},{8,10},{9,11},{10,... | collective-permute-start | bytes 393224 | tf_op jit(solution)/shard_map/ppermute | solution.py:37
  27.0 12.4 %collective-permute-start.3 = (bf16[4,16,1024]{2,1,0:T(8,128)(2,1)S(1)}, bf16[4,16,1024]{2,1,0:T(8,128)(2,1)S(1)}, u32[]{:S(2)}, u32[]{:S(2)}) collective-permute-start(bf16[4,16,1024]{2,1,0:T(8,128)(2,1)S(1)} %pad_maximum_fusion.9), channel_id=1, source_target_pairs={{0,6},{1,7},{2,0},{3,1},{4,2},{5,3},{6,4},{7,5},{8,14},{9,15},{10,... | collective-permute-start | bytes 393224 | tf_op jit(solution)/shard_map/ppermute | solution.py:37
  29.7 10.6 %collective-permute-start.8 = (bf16[2,128,512]{2,1,0:T(8,128)(2,1)S(1)}, bf16[2,128,512]{2,1,0:T(8,128)(2,1)S(1)}, u32[]{:S(2)}, u32[]{:S(2)}) collective-permute-start(bf16[2,128,512]{2,1,0:T(8,128)(2,1)S(1)} %pad_maximum_fusion.8), channel_id=1, source_target_pairs={{0,64},{32,96},{64,0},{96,32},{128,192},{160,224},{192,128},{224,1... | collective-permute-start | bytes 786440 | tf_op jit(solution)/shard_map/ppermute | solution.py:223
  40.3 7.6 %collective-permute-start.6 = (bf16[4,4,16,1024]{3,2,0,1:T(8,128)(2,1)}, bf16[4,4,16,1024]{3,2,0,1:T(8,128)(2,1)}, u32[]{:S(2)}, u32[]{:S(2)}) collective-permute-start(bf16[4,4,16,1024]{3,2,0,1:T(8,128)(2,1)} %pad_maximum_fusion.2), channel_id=1, source_target_pairs={{0,1},{1,0},{2,3},{3,2},{4,5},{5,4},{6,7},{7,6},{8,9},{9,8},{10,11... | collective-permute-start | bytes 1572872 | tf_op jit(solution)/shard_map/ppermute | solution.py:37
  40.4 0.7 copy-start.1
  41.9 16.2 %collective-permute-start.9 = (bf16[4,128,512]{2,1,0:T(8,128)(2,1)}, bf16[4,128,512]{2,1,0:T(8,128)(2,1)}, u32[]{:S(2)}, u32[]{:S(2)}) collective-permute-start(bf16[4,128,512]{2,1,0:T(8,128)(2,1)} %pad_maximum_fusion.3), channel_id=1, source_target_pairs={{0,128},{32,160},{64,192},{96,224},{128,0},{160,32},{192,64},{224,... | collective-permute-start | bytes 1572872 | tf_op jit(solution)/shard_map/ppermute | solution.py:223
  60.2 53.0 %all-to-all-start.1 = ((bf16[8,2,128,512]{3,2,1,0:T(8,128)(2,1)}), bf16[8,2,128,512]{3,2,1,0:T(8,128)(2,1)}, u32[]{:S(2)}, u32[]{:S(2)}) async-start(bf16[8,2,128,512]{3,2,1,0:T(8,128)(2,1)} %shard_map.102), calls=%async_computation.1 | async-start | bytes 4194304 | tf_op jit(solution)/shard_map/all_to_all | solution.py:253
  64.7 1.4 copy-start.4
  66.1 4.1 %copy-start.2 = (bf16[8,128,512]{2,1,0:T(8,128)(2,1)}, bf16[8,128,512]{2,1,0:T(8,128)(2,1)S(1)}, u32[]{:S(2)}) copy-start(bf16[8,128,512]{2,1,0:T(8,128)(2,1)S(1)} %pad_maximum_fusion.1) | copy-start | bytes 3145732
  67.5 21.2 %collective-permute-start.10 = (bf16[384,512]{1,0:T(8,128)(2,1)}, bf16[384,512]{1,0:T(8,128)(2,1)}, u32[]{:S(2)}, u32[]{:S(2)}) collective-permute-start(bf16[384,512]{1,0:T(8,128)(2,1)} %convolution_convert_fusion.2), channel_id=1, source_target_pairs={{0,6},{1,7},{2,0},{3,1},{4,2},{5,3},{6,4},{7,5},{8,14},{9,15},{10,... | collective-permute-start | bytes 1179656 | tf_op jit(solution)/shard_map/ppermute | solution.py:37
  70.5 22.5 %collective-permute-start.11 = (bf16[384,512]{1,0:T(8,128)(2,1)}, bf16[384,512]{1,0:T(8,128)(2,1)S(1)}, u32[]{:S(2)}, u32[]{:S(2)}) collective-permute-start(bf16[384,512]{1,0:T(8,128)(2,1)} %convolution_convert_fusion.2), channel_id=1, source_target_pairs={{0,2},{1,3},{2,4},{3,5},{4,6},{5,7},{6,0},{7,1},{8,10},{9,11},{10,... | collective-permute-start | bytes 1179656 | tf_op jit(solution)/shard_map/ppermute | solution.py:37
  89.8 11.0 %collective-permute-start.12 = (bf16[384,256]{1,0:T(8,128)(2,1)S(1)}, bf16[384,256]{1,0:T(8,128)(2,1)S(1)}, u32[]{:S(2)}, u32[]{:S(2)}) collective-permute-start(bf16[384,256]{1,0:T(8,128)(2,1)S(1)} %get-tuple-element.62), channel_id=1, source_target_pairs={{0,6},{1,7},{2,0},{3,1},{4,2},{5,3},{6,4},{7,5},{8,14},{9,15},{10,... | collective-permute-start | bytes 589832 | tf_op jit(solution)/shard_map/ppermute | solution.py:37
  93.1 9.6 %collective-permute-start.13 = (bf16[384,256]{1,0:T(8,128)(2,1)S(1)}, bf16[384,256]{1,0:T(8,128)(2,1)S(1)}, u32[]{:S(2)}, u32[]{:S(2)}) collective-permute-start(bf16[384,256]{1,0:T(8,128)(2,1)S(1)} %get-tuple-element.59), channel_id=1, source_target_pairs={{0,2},{1,3},{2,4},{3,5},{4,6},{5,7},{6,0},{7,1},{8,10},{9,11},{10,... | collective-permute-start | bytes 589832 | tf_op jit(solution)/shard_map/ppermute | solution.py:37
  109.0 20.4 %collective-permute-start.14 = (bf16[384,256]{1,0:T(8,128)(2,1)S(1)}, bf16[384,256]{1,0:T(8,128)(2,1)S(1)}, u32[]{:S(2)}, u32[]{:S(2)}) collective-permute-start(bf16[384,256]{1,0:T(8,128)(2,1)S(1)} %bitcast.109), channel_id=1, source_target_pairs={{0,2},{1,3},{2,4},{3,5},{4,6},{5,7},{6,0},{7,1},{8,10},{9,11},{10,... | collective-permute-start | bytes 589832 | tf_op jit(solution)/shard_map/ppermute | solution.py:37
  111.1 18.4 %collective-permute-start.15 = (bf16[384,256]{1,0:T(8,128)(2,1)S(1)}, bf16[384,256]{1,0:T(8,128)(2,1)S(1)}, u32[]{:S(2)}, u32[]{:S(2)}) collective-permute-start(bf16[384,256]{1,0:T(8,128)(2,1)S(1)} %bitcast.108), channel_id=1, source_target_pairs={{0,6},{1,7},{2,0},{3,1},{4,2},{5,3},{6,4},{7,5},{8,14},{9,15},{10,... | collective-permute-start | bytes 589832 | tf_op jit(solution)/shard_map/ppermute | solution.py:37
  113.3 20.4 %all-to-all-start.2 = ((bf16[8,128,512]{2,1,0:T(8,128)(2,1)}), bf16[8,128,512]{2,1,0:T(8,128)(2,1)}, u32[]{:S(2)}, u32[]{:S(2)}) async-start(bf16[8,128,512]{2,1,0:T(8,128)(2,1)} %get-tuple-element.38), calls=%async_computation.2 | async-start | bytes 2097152 | tf_op jit(solution)/shard_map/all_to_all | solution.py:262
  133.7 24.8 %all-to-all-start.3 = ((bf16[8,128,512]{2,1,0:T(8,128)(2,1)}), bf16[8,128,512]{2,1,0:T(8,128)(2,1)S(1)}, u32[]{:S(2)}, u32[]{:S(2)}) async-start(bf16[8,128,512]{2,1,0:T(8,128)(2,1)} %get-tuple-element.39), calls=%async_computation.3 | async-start | bytes 2097152 | tf_op jit(solution)/shard_map/all_to_all | solution.py:282
  137.3 17.9 %collective-permute-start.17 = (bf16[384,512]{1,0:T(8,128)(2,1)S(1)}, bf16[384,512]{1,0:T(8,128)(2,1)S(1)}, u32[]{:S(2)}, u32[]{:S(2)}) collective-permute-start(bf16[384,512]{1,0:T(8,128)(2,1)S(1)} %pad_maximum_fusion.7), channel_id=1, source_target_pairs={{0,6},{1,7},{2,0},{3,1},{4,2},{5,3},{6,4},{7,5},{8,14},{9,15},{10,... | collective-permute-start | bytes 1179656 | tf_op jit(solution)/shard_map/ppermute | solution.py:37
  138.4 18.2 %collective-permute-start.16 = (bf16[384,512]{1,0:T(8,128)(2,1)S(1)}, bf16[384,512]{1,0:T(8,128)(2,1)S(1)}, u32[]{:S(2)}, u32[]{:S(2)}) collective-permute-start(bf16[384,512]{1,0:T(8,128)(2,1)S(1)} %pad_maximum_fusion.6), channel_id=1, source_target_pairs={{0,2},{1,3},{2,4},{3,5},{4,6},{5,7},{6,0},{7,1},{8,10},{9,11},{10,... | collective-permute-start | bytes 1179656 | tf_op jit(solution)/shard_map/ppermute | solution.py:37
  156.6 0.7 copy-start.6
  158.5 4.8 %copy-start.3 = (bf16[8,128,512]{2,1,0:T(8,128)(2,1)S(1)}, bf16[8,128,512]{2,1,0:T(8,128)(2,1)}, u32[]{:S(2)}) copy-start(bf16[8,128,512]{2,1,0:T(8,128)(2,1)} %copy-done.2) | copy-start | bytes 3145732
  158.5 1.0 copy-start
  163.3 2.8 %copy-start.5 = (bf16[384,1024]{1,0:T(8,128)(2,1)S(1)}, bf16[384,1024]{1,0:T(8,128)(2,1)}, u32[]{:S(2)}) copy-start(bf16[384,1024]{1,0:T(8,128)(2,1)} %reshape.44) | copy-start | bytes 2359300
  167.9 31.8 %all-to-all-start.4 = ((bf16[8,128,512]{2,1,0:T(8,128)(2,1)}), bf16[8,128,512]{2,1,0:T(8,128)(2,1)S(1)}, u32[]{:S(2)}, u32[]{:S(2)}) async-start(bf16[8,128,512]{2,1,0:T(8,128)(2,1)} %bitcast.49), calls=%async_computation.4 | async-start | bytes 2097152 | tf_op jit(solution)/shard_map/all_to_all | solution.py:292
  172.7 1.9 collective-permute-start.18
  174.9 8.9 %collective-permute-start.21 = (bf16[4,12,1024]{2,1,0:T(8,128)(2,1)S(1)}, bf16[4,12,1024]{2,1,0:T(8,128)(2,1)S(1)}, u32[]{:S(2)}, u32[]{:S(2)}) collective-permute-start(bf16[4,12,1024]{2,1,0:T(8,128)(2,1)S(1)} %get-tuple-element.49), channel_id=1, source_target_pairs={{0,24},{1,25},{2,26},{3,27},{4,28},{5,29},{6,30},{7,31},{8,0},{9,1... | collective-permute-start | bytes 294920 | tf_op jit(solution)/shard_map/ppermute | solution.py:37
  177.9 7.9 %collective-permute-start.20 = (bf16[4,12,1024]{2,1,0:T(8,128)(2,1)S(1)}, bf16[4,12,1024]{2,1,0:T(8,128)(2,1)S(1)}, u32[]{:S(2)}, u32[]{:S(2)}) collective-permute-start(bf16[4,12,1024]{2,1,0:T(8,128)(2,1)S(1)} %get-tuple-element.50), channel_id=1, source_target_pairs={{0,16},{1,17},{2,18},{3,19},{4,20},{5,21},{6,22},{7,23},{8,24},{9,... | collective-permute-start | bytes 294920 | tf_op jit(solution)/shard_map/ppermute | solution.py:37
  178.7 8.7 %collective-permute-start.19 = (bf16[4,12,1024]{2,1,0:T(8,128)(2,1)S(1)}, bf16[4,12,1024]{2,1,0:T(8,128)(2,1)S(1)}, u32[]{:S(2)}, u32[]{:S(2)}) collective-permute-start(bf16[4,12,1024]{2,1,0:T(8,128)(2,1)S(1)} %get-tuple-element.48), channel_id=1, source_target_pairs={{0,8},{1,9},{2,10},{3,11},{4,12},{5,13},{6,14},{7,15},{8,16},{9,17... | collective-permute-start | bytes 294920 | tf_op jit(solution)/shard_map/ppermute | solution.py:37
  187.6 6.4 %collective-permute-start.24 = (bf16[12,1024]{1,0:T(8,128)(2,1)S(1)}, bf16[12,1024]{1,0:T(8,128)(2,1)S(1)}, u32[]{:S(2)}, u32[]{:S(2)}) collective-permute-start(bf16[12,1024]{1,0:T(8,128)(2,1)S(1)} %get-tuple-element.70), channel_id=1, source_target_pairs={{0,6},{1,7},{2,0},{3,1},{4,2},{5,3},{6,4},{7,5},{8,14},{9,15},{10,... | collective-permute-start | bytes 73736 | tf_op jit(solution)/shard_map/ppermute | solution.py:37
  189.7 8.2 %collective-permute-start.23 = (bf16[12,1024]{1,0:T(8,128)(2,1)S(1)}, bf16[12,1024]{1,0:T(8,128)(2,1)S(1)}, u32[]{:S(2)}, u32[]{:S(2)}) collective-permute-start(bf16[12,1024]{1,0:T(8,128)(2,1)S(1)} %get-tuple-element.71), channel_id=1, source_target_pairs={{0,4},{1,5},{2,6},{3,7},{4,0},{5,1},{6,2},{7,3},{8,12},{9,13},{10,... | collective-permute-start | bytes 73736 | tf_op jit(solution)/shard_map/ppermute | solution.py:37
  192.7 6.4 %collective-permute-start.22 = (bf16[12,1024]{1,0:T(8,128)(2,1)S(1)}, bf16[12,1024]{1,0:T(8,128)(2,1)S(1)}, u32[]{:S(2)}, u32[]{:S(2)}) collective-permute-start(bf16[12,1024]{1,0:T(8,128)(2,1)S(1)} %get-tuple-element.69), channel_id=1, source_target_pairs={{0,2},{1,3},{2,4},{3,5},{4,6},{5,7},{6,0},{7,1},{8,10},{9,11},{10,... | collective-permute-start | bytes 73736 | tf_op jit(solution)/shard_map/ppermute | solution.py:37

commit v4 on v3

--- a/solution.py
+++ b/solution.py
@@ -46,19 +46,38 @@
     return jnp.stack([lax.select_n((owner - me) & (n - 1), *blocks) for owner in range(n)])
 
 
-def gather_encoder(block, later):
+def double(held, bit):
+    other = lax.ppermute(held, "dp", [(d, d ^ bit) for d in range(NX * NL)])
+    first = (lax.axis_index("dp") & bit) == 0
+    return jnp.concatenate([jnp.where(first, held, other), jnp.where(first, other, held)])
+
+
+def along_x(pair):
+    x = lax.axis_index("dp") >> 1
+
+    def from_ahead(d):
+        pairs = [(a * NL + b, (a - d) % NX * NL + b) for a in range(NX) for b in range(NL)]
+        return lax.ppermute(pair, "dp", pairs)
+
+    return by_owner(pair, [from_ahead(d) for d in range(1, NX)], x).reshape(-1, *pair.shape[1:])
+
+
+def gather(block, weight, packed, later):
     y, z, c = place()
+    weight = double(weight[None], 1)
     along_y = by_owner(block, [shift(block, dy=-d) for d in range(1, NY)], y)
-    along_y, later = lax.optimization_barrier((along_y, later))
+    along_y, weight, packed = lax.optimization_barrier((along_y, weight, packed))
+    weight = along_x(weight)
     along_z = by_owner(along_y, [shift(along_y, dz=-d) for d in range(1, NZ)], z)
+    along_z, later = lax.optimization_barrier((along_z, later))
     other = shift(along_z, dc=1)
     first = c == 0
     both = [jnp.where(first, along_z, other), jnp.where(first, other, along_z)]
     gathered = jnp.stack(both, axis=2).swapaxes(0, 1)
-    return gathered.reshape(NY * NZ * NC, *block.shape), later
-
-
-def sum_encoder(part, later):
+    return gathered.reshape(NY * NZ * NC, *block.shape), weight.reshape(-1, weight.shape[2]), packed, later
+
+
+def sum_encoder(part, later, last):
     y, z, c = place()
 
     def at(value, index, axis):
@@ -72,8 +91,9 @@
     total = (at(part, c, 2).astype(F32) + arrived.astype(F32)).astype(BF16)
     arrived = [shift(at(total, (y + d) & 3, 0), dy=d) for d in range(1, NY)]
     total = sum((a.astype(F32) for a in arrived), at(total, y, 0).astype(F32)).astype(BF16)
+    total, last = lax.optimization_barrier((total, last))
     arrived = [shift(at(total, (z + d) & 3, 0), dz=d) for d in range(1, NZ)]
-    return sum((a.astype(F32) for a in arrived), at(total, z, 0).astype(F32)).astype(BF16), later
+    return sum((a.astype(F32) for a in arrived), at(total, z, 0).astype(F32)).astype(BF16), later, last
 
 
 def pack_kernel(z, *refs):
@@ -107,33 +127,35 @@
     )(z, *[queries, grads] * len(group))
 
 
-def unpack_kernel(z, *refs):
-    sources, out = refs[:-1], refs[-1]
-    for group, source in zip(GROUPS, sources, strict=True):
-        for i, distance in enumerate(group):
-            for c in range(NC):
-                at = (lax.rem(z[0] + distance, NZ) * NC + c) * FEATURES
-                columns = pl.ds(pl.multiple_of(at, FEATURES), FEATURES)
-                out[:, columns] = source[c, :, pl.ds(i * FEATURES, FEATURES)]
-
-
-def unpack(z, arrived):
-    width = NZ * NC * FEATURES
+def unpack_kernel(z, source, *refs):
+    out = refs[-1]
+    for c in range(NC):
+        out[:, pl.ds(c * FEATURES, FEATURES)] = source[c]
+
+
+def unpack(group, z, arrived, into=None):
+    assert group[1] == group[0] + 2
+    width = NC * FEATURES
+    given = [] if into is None else [into]
     return pl.pallas_call(
         unpack_kernel,
-        out_shape=jax.ShapeDtypeStruct((ROWS, NY * width), BF16),
+        out_shape=jax.ShapeDtypeStruct((ROWS, NY * NZ * width), BF16),
         grid_spec=pltpu.PrefetchScalarGridSpec(
             num_scalar_prefetch=1,
-            grid=(NY,),
+            grid=(NY, 2),
             in_specs=[
-                pl.BlockSpec((NC, ROWS, a.shape[2]), lambda y, z: (y, 0, 0)) for a in arrived
+                pl.BlockSpec((NC, ROWS, FEATURES), lambda y, i, z: (y, 0, i)),
+                *[pl.BlockSpec(memory_space=pl.ANY) for _ in given],
             ],
-            out_specs=pl.BlockSpec((ROWS, width), lambda y, z: (0, y)),
-        ),
+            out_specs=pl.BlockSpec(
+                (ROWS, width), lambda y, i, z: (0, y * NZ + lax.rem(z[0] + group[0] + 2 * i, NZ))
+            ),
+        ),
+        input_output_aliases={2: 0} if given else {},
         cost_estimate=pl.CostEstimate(
-            flops=0, bytes_accessed=4 * ROWS * NY * width, transcendentals=0
-        ),
-    )(z, *arrived)
+            flops=0, bytes_accessed=4 * ROWS * NY * 2 * width, transcendentals=0
+        ),
+    )(z, arrived, *given)
 
 
 def attend_kernel(ends, rows, key, value, *refs):
@@ -216,29 +238,22 @@
     )(ends, rows, keys, values, *given)
 
 
-def gather_weights(block):
-    me = lax.axis_index("dp")
-    held = block[None]
-    for bit in (1, 2, 4):
-        other = lax.ppermute(held, "dp", [(d, d ^ bit) for d in range(NX * NL)])
-        first = (me & bit) == 0
-        held = jnp.concatenate([jnp.where(first, held, other), jnp.where(first, other, held)])
-    return held.reshape(-1, block.shape[1])
-
-
 def body(queries, out_grad, enc_states, w_key, w_value, dec_segments, enc_segments):
     z = place()[1]
     z_index = z.reshape(1)
     width = enc_states.shape[1]
     ids = [jnp.pad(i.astype(BF16)[None], ((0, 0), (0, width - i.size))) for i in (enc_segments, dec_segments)]
     block = jnp.concatenate([enc_states, *ids, jnp.zeros((2, width), BF16)], axis=0)
-    gathered, z_later = gather_encoder(block, z_index)
+    gathered, weight, near_packed, z_later = gather(
+        block,
+        jnp.concatenate([w_key, w_value], axis=1),
+        pack(GROUPS[0], z_index, queries, out_grad),
+        z_index,
+    )
     encoder = gathered[:, :ENC_ROWS].reshape(KEYS, -1)
     all_ids = (gathered[:, ENC_ROWS, :ENC_ROWS], gathered[:, ENC_ROWS + 1, :ROWS])
     first_of = jnp.arange(1, 4, dtype=BF16)[:, None, None]
     ends = jnp.concatenate([jnp.sum((i[None] < first_of).astype(jnp.int32), axis=(1, 2)) for i in all_ids])
-    weight = gather_weights(jnp.concatenate([w_key, w_value], axis=1))
-
     swap = functools.partial(
         lax.all_to_all,
         axis_name="ctx",
@@ -247,45 +262,51 @@
         axis_index_groups=SHARED_Z,
         tiled=True,
     )
-    near = swap(pack(GROUPS[0], z_index, queries, out_grad))
+    near = swap(near_packed)
     own = jnp.dot(encoder, weight, preferred_element_type=F32).astype(BF16)
-    far_packed, near = lax.optimization_barrier((pack(GROUPS[1], z_later, queries, out_grad), near))
+    far_packed = pack(GROUPS[1], z_later, queries, out_grad)
+    far_packed, near, own = lax.optimization_barrier((far_packed, near, own))
     far = swap(far_packed)
 
-    ahead, behind = shift(own, dz=-1), shift(own, dz=1)
-    key_of = lambda block: block[:, :FEATURES]
-    value_of = lambda block: block[:, FEATURES:]
-    key_opposite, value_opposite = shift(key_of(ahead), dz=-1), shift(value_of(behind), dz=1)
-
-    back, key_0, value_0 = attend(ends, near, 0, key_of(own)[None], value_of(own)[None])
+    own_key, own_value = own[:, :FEATURES], own[:, FEATURES:]
+    key_ahead, value_behind = shift(own_key, dz=-1), shift(own_value, dz=1)
+    back, key_0, value_0 = attend(ends, near, 0, own_key[None], own_value[None])
+    key_ahead, value_behind, back = lax.optimization_barrier((key_ahead, value_behind, back))
+    key_opposite, value_opposite = shift(key_ahead, dz=-1), shift(value_behind, dz=1)
+    later_key, later_value, key_opposite, value_opposite = lax.optimization_barrier(
+        (own_key, own_value, key_opposite, value_opposite)
+    )
+    key_behind, value_ahead = shift(later_key, dz=1), shift(later_value, dz=-1)
+
     back, key_2, value_2 = attend(ends, near, 1, key_opposite[None], value_opposite[None], back)
     back_near = swap(back)
     back, key_1, value_1 = attend(
         ends,
         far,
         0,
-        jnp.stack([key_of(ahead), key_of(behind)]),
-        jnp.stack([value_of(ahead), value_of(behind)]),
+        jnp.stack([key_ahead, key_behind]),
+        jnp.stack([value_ahead, value_behind]),
     )
 
     def joined(a, b):
         return (a.astype(F32) + b.astype(F32)).astype(BF16)
 
-    key_ahead = joined(key_1[0], shift(key_2[0], dz=1))
-    value_behind = joined(value_1[1], shift(value_2[0], dz=-1))
-    for_ahead = jnp.concatenate([key_ahead, value_1[0]], axis=1)
-    for_behind = jnp.concatenate([key_1[1], value_behind], axis=1)
+    key_sum = joined(key_1[0], shift(key_2[0], dz=1))
+    value_sum = joined(value_1[1], shift(value_2[0], dz=-1))
+    for_ahead = jnp.concatenate([key_sum, value_1[0]], axis=1)
+    for_behind = jnp.concatenate([key_1[1], value_sum], axis=1)
     for_ahead, for_behind, back = lax.optimization_barrier((for_ahead, for_behind, back))
     total = jnp.concatenate([key_0[0], value_0[0]], axis=1).astype(F32)
     total += shift(for_ahead, dz=1).astype(F32) + shift(for_behind, dz=-1).astype(F32)
 
-    query_grad = unpack(z_index, [back_near, swap(back)])
+    query_grad = unpack(GROUPS[0], z_index, back_near)
     total, query_grad = lax.optimization_barrier((total, query_grad))
-
+    back = swap(back)
     rounded = total.astype(BF16)
     part = lax.dot_general(rounded, weight, (((1,), (1,)), ((), ())), preferred_element_type=F32)
     part = part.astype(BF16).reshape(NY, NZ, NC, ENC_ROWS, -1)
-    enc_grad, encoder = sum_encoder(part, encoder)
+    enc_grad, encoder, back = sum_encoder(part, encoder, back)
+    query_grad = unpack(GROUPS[1], z_index, back, query_grad)
 
     term = lax.dot_general(encoder, rounded, (((0,), (0,)), ((), ())), preferred_element_type=F32)
     pieces = term.astype(BF16).reshape(NX * NL, -1, 2 * FEATURES)

time: 202 us -> 180 us (0.89)
  waiting for transfers between devices: 71.8 us -> 41.4 us
  Pallas kernels: 35.8 us -> 42.5 us
  starting transfers between devices: 67.5 us -> 71 us
  local copies, waits for them, and re-layouts: 8.05 us -> 5.06 us
    ppermute x22 -> x24, waiting for transfers between devices: 59.8 us -> 39.2 us  [shift(): return lax.ppermute(value, 'ctx', pairs)]
    ppermute x3 -> x4, waiting for transfers between devices: 7.87 us -> 1.12 us  [the longest x3 1.12 us: from_ahead(): return lax.ppermute(pair, 'dp', pairs)]
    pallas_call x1 -> x2, Pallas kernels: 3.82 us -> 10.4 us  [unpack(): pl.pallas_call(unpack_kernel, out_shape=jax.ShapeDtypeStruct((ROWS, NY *...]
    all_to_all x1, waiting for transfers between devices: 4.11 us -> 0.01 us  [body(): back_near = swap(back)]
    select_n x3 -> x1, other arithmetic: 2.27 us -> 0.05 us  [double(): jnp.where(first, held, other)]
    concatenate x5 -> x3, other arithmetic: 2.3 us -> 0.08 us  [the longest x1 0.03 us: body(): for_behind = jnp.concatenate([key_1[1], value_sum], axis=1)]
    ppermute x3 -> x4, starting transfers between devices: 4.78 us -> 6.15 us  [the longest x3 4.15 us: from_ahead(): return lax.ppermute(pair, 'dp', pairs)]
    ppermute x22 -> x24, starting transfers between devices: 41.8 us -> 41.6 us  [shift(): return lax.ppermute(value, 'ctx', pairs)]
  transfers between devices with their start and end apart: 30 -> 33, of which waited for: 14 -> 11; matrix products, arithmetic and copies ran while one was open for 7% -> 11% of each run, Pallas kernels for 16% -> 24%
where the time goes in v4:
time: 180 us; the launch traced here: 179 us
  starting transfers between devices  71 us (39%)
  Pallas kernels  42.5 us (24%)
  waiting for transfers between devices  41.4 us (23%)
  other arithmetic  12.7 us (7%)
  matrix products  5.3 us (3%)
  local copies, waits for them, and re-layouts  5.06 us (3%)
    ppermute x24, starting transfers between devices, shift(): return lax.ppermute(value, 'ctx', pairs)  41.6 us
    ppermute x24, waiting for transfers between devices, shift(): return lax.ppermute(value, 'ctx', pairs)  39.2 us
    pallas_call x3, Pallas kernels, attend(): pl.pallas_call(attend_kernel, out_shape=(jax.ShapeDtypeStruct((PEERS, ROW...  24.3 us
    pallas_call x2, Pallas kernels, unpack(): pl.pallas_call(unpack_kernel, out_shape=jax.ShapeDtypeStruct((ROWS, NY *...  10.4 us
    pallas_call x2, Pallas kernels, pack(): pl.pallas_call(pack_kernel, out_shape=jax.ShapeDtypeStruct((PEERS, *shape...  7.79 us
    all_to_all x1, starting transfers between devices, body(): pieces = lax.all_to_all(pieces, 'dp', 0, 0, tiled=True)  5.52 us
    all_to_all x1, starting transfers between devices, body(): back = swap(back)  4.94 us
    all_to_all x1, starting transfers between devices, body(): back_near = swap(back)  4.76 us
  transfers between devices with their start and end apart: 33, of which 11 were waited for; matrix products, arithmetic and copies ran while one was open for 11% of the time, Pallas kernels for 24%

profile of v4, /device:TPU:2, one launch (start us, length us, event | category | flops | bytes accessed | tf_op | source)
XLA Modules:
  0.0 179.0 jit_solution(16929259281248904217)
XLA Ops:
  2.9 3.0 %collective-permute-start = (bf16[16,1024]{1,0:T(8,128)(2,1)S(1)}, bf16[16,1024]{1,0:T(8,128)(2,1)S(1)}, u32[]{:S(2)}, u32[]{:S(2)}) collective-permute-start(bf16[16,1024]{1,0:T(8,128)(2,1)S(1)} %fusion.16), channel_id=1, source_target_pairs={{0,24},{1,25},{2,26},{3,27},{4,28},{5,29},{6,30},{7,31},{8,0},{9,1... | collective-permute-start | bytes 98312 | tf_op jit(solution)/shard_map/ppermute | solution.py:37
  8.4 2.0 %collective-permute-start.3 = (bf16[1,128,512]{2,1,0:T(8,128)(2,1)S(1)}, bf16[1,128,512]{2,1,0:T(8,128)(2,1)S(1)}, u32[]{:S(2)}, u32[]{:S(2)}) collective-permute-start(bf16[1,128,512]{2,1,0:T(8,128)(2,1)S(1)} %maximum_bitcast_fusion), channel_id=1, source_target_pairs={{0,32},{32,0},{64,96},{96,64},{128,160},{160,128},{192,224},{224,1... | collective-permute-start | bytes 393224 | tf_op jit(solution)/shard_map/ppermute | solution.py:50
  10.4 3.9 %shard_map.102 = bf16[8,2,128,512]{3,2,1,0:T(8,128)(2,1)} custom-call(s32[1]{0:T(128)} %bitcast.z, bf16[128,8192]{1,0:T(8,128)(2,1)} %refs_2_.3, bf16[128,8192]{1,0:T(8,128)(2,1)} %refs_3_.3, bf16[128,8192]{1,0:T(8,128)(2,1)} %refs_2_.3, bf16[128,8192]{1,0:T(8,128)(2,1)} %refs_3_.3), custom_call_target="tpu_custom_call" | custom-call | bytes 4194304 | tf_op jit(solution)/shard_map/pallas_call | solution.py:115
  14.6 3.6 %all-to-all-start = ((bf16[8,2,128,512]{3,2,1,0:T(8,128)(2,1)}), bf16[8,2,128,512]{3,2,1,0:T(8,128)(2,1)S(1)}, u32[]{:S(2)}, u32[]{:S(2)}) async-start(bf16[8,2,128,512]{3,2,1,0:T(8,128)(2,1)} %shard_map.102), calls=%async_computation | async-start | bytes 4194304 | tf_op jit(solution)/shard_map/all_to_all | solution.py:265
  18.2 5.5 %collective-permute-start.4 = (bf16[4,16,1024]{2,1,0:T(8,128)(2,1)S(1)}, bf16[4,16,1024]{2,1,0:T(8,128)(2,1)S(1)}, u32[]{:S(2)}, u32[]{:S(2)}) collective-permute-start(bf16[4,16,1024]{2,1,0:T(8,128)(2,1)S(1)} %pad_maximum_fusion.8), channel_id=1, source_target_pairs={{0,6},{1,7},{2,0},{3,1},{4,2},{5,3},{6,4},{7,5},{8,14},{9,15},{10,... | collective-permute-start | bytes 393224 | tf_op jit(solution)/shard_map/ppermute | solution.py:37
  23.7 1.4 collective-permute-start.5
  25.2 2.4 %collective-permute-start.6 = (bf16[4,16,1024]{2,1,0:T(8,128)(2,1)S(1)}, bf16[4,16,1024]{2,1,0:T(8,128)(2,1)S(1)}, u32[]{:S(2)}, u32[]{:S(2)}) collective-permute-start(bf16[4,16,1024]{2,1,0:T(8,128)(2,1)S(1)} %pad_maximum_fusion.8), channel_id=1, source_target_pairs={{0,2},{1,3},{2,4},{3,5},{4,6},{5,7},{6,0},{7,1},{8,10},{9,11},{10,... | collective-permute-start | bytes 393224 | tf_op jit(solution)/shard_map/ppermute | solution.py:37
  27.5 1.5 collective-permute-start.10
  29.6 2.1 %collective-permute-start.9 = (bf16[2,128,512]{2,1,0:T(8,128)(2,1)S(1)}, bf16[2,128,512]{2,1,0:T(8,128)(2,1)}, u32[]{:S(2)}, u32[]{:S(2)}) collective-permute-start(bf16[2,128,512]{2,1,0:T(8,128)(2,1)S(1)} %pad_maximum_fusion.7), channel_id=1, source_target_pairs={{0,128},{32,160},{64,192},{96,224},{128,0},{160,32},{192,64},{224,... | collective-permute-start | bytes 786440 | tf_op jit(solution)/shard_map/ppermute | solution.py:60
  31.7 5.9 %collective-permute-done.5 = bf16[4,16,1024]{2,1,0:T(8,128)(2,1)S(1)} collective-permute-done((bf16[4,16,1024]{2,1,0:T(8,128)(2,1)S(1)}, bf16[4,16,1024]{2,1,0:T(8,128)(2,1)S(1)}, u32[]{:S(2)}, u32[]{:S(2)}) %collective-permute-start.5) | collective-permute-done | bytes 131104 | tf_op jit(solution)/shard_map/ppermute | solution.py:37
  37.8 3.9 %shard_map.103 = bf16[8,2,128,512]{3,2,1,0:T(8,128)(2,1)} custom-call(s32[1]{0:T(128)} %bitcast.z, bf16[128,8192]{1,0:T(8,128)(2,1)} %refs_2_.3, bf16[128,8192]{1,0:T(8,128)(2,1)} %refs_3_.3, bf16[128,8192]{1,0:T(8,128)(2,1)} %refs_2_.3, bf16[128,8192]{1,0:T(8,128)(2,1)} %refs_3_.3), custom_call_target="tpu_custom_call" | custom-call | bytes 4194304 | tf_op jit(solution)/shard_map/pallas_call | solution.py:115
  41.7 1.1 collective-permute-done.9
  42.8 1.2 select_bitcast_fusion.5
  44.1 1.1 pad_maximum_fusion.1
  45.3 1.0 reshape.41
  46.4 2.0 %convolution_convert_fusion.2 = bf16[384,512]{1,0:T(8,128)(2,1)S(1)} fusion(bf16[384,1024]{1,0:T(8,128)(2,1)} %reshape.41, bf16[1024,512]{1,0:T(8,128)(2,1)} %bitcast.119), kind=kOutput, calls=%fused_computation.3 | convolution fusion | flops 402849792 | bytes 2228224 | tf_op jit(solution)/shard_map/dot_general | solution.py:266
  48.4 4.5 %all-to-all-start.1 = ((bf16[8,2,128,512]{3,2,1,0:T(8,128)(2,1)}), bf16[8,2,128,512]{3,2,1,0:T(8,128)(2,1)}, u32[]{:S(2)}, u32[]{:S(2)}) async-start(bf16[8,2,128,512]{3,2,1,0:T(8,128)(2,1)} %shard_map.103), calls=%async_computation.1 | async-start | bytes 4194304 | tf_op jit(solution)/shard_map/all_to_all | solution.py:269
  55.4 2.9 %collective-permute-start.11 = (bf16[384,256]{1,0:T(8,128)(2,1)S(1)}, bf16[384,256]{1,0:T(8,128)(2,1)S(1)}, u32[]{:S(2)}, u32[]{:S(2)}) collective-permute-start(bf16[384,256]{1,0:T(8,128)(2,1)S(1)} %get-tuple-element.50), channel_id=1, source_target_pairs={{0,6},{1,7},{2,0},{3,1},{4,2},{5,3},{6,4},{7,5},{8,14},{9,15},{10,... | collective-permute-start | bytes 589832 | tf_op jit(solution)/shard_map/ppermute | solution.py:37
  58.5 6.3 %shard_map.104 = (bf16[8,128,512]{2,1,0:T(8,128)(2,1)}, bf16[1,384,256]{2,1,0:T(8,128)(2,1)S(1)}, bf16[1,384,256]{2,1,0:T(8,128)(2,1)S(1)}) custom-call(s32[6]{0:T(128)S(1)} %pad_add_fusion.ends, bf16[8,2,128,512]{3,2,1,0:T(8,128)(2,1)S(1)} %all-to-all-done.rows, bf16[1,384,256]{2,1,0:T(8,128)(2,1)S(1)} %get-tuple-element.84.key, ...), custom_call_target="tpu_custom_call" | custom-call | flops 1006632960 | bytes 6291456 | tf_op jit(solution)/shard_map/pallas_call | solution.py:212
  64.8 3.3 %collective-permute-done.11 = bf16[384,256]{1,0:T(8,128)(2,1)S(1)} collective-permute-done((bf16[384,256]{1,0:T(8,128)(2,1)S(1)}, bf16[384,256]{1,0:T(8,128)(2,1)S(1)}, u32[]{:S(2)}, u32[]{:S(2)}) %collective-permute-start.11) | collective-permute-done | bytes 196640 | tf_op jit(solution)/shard_map/ppermute | solution.py:37
  68.1 3.0 %collective-permute-start.13 = (bf16[384,256]{1,0:T(8,128)(2,1)S(1)}, bf16[384,256]{1,0:T(8,128)(2,1)S(1)}, u32[]{:S(2)}, u32[]{:S(2)}) collective-permute-start(bf16[384,256]{1,0:T(8,128)(2,1)S(1)} %collective-permute-done.11), channel_id=1, source_target_pairs={{0,6},{1,7},{2,0},{3,1},{4,2},{5,3},{6,4},{7,5},{8,14},{9,15},{10,... | collective-permute-start | bytes 589832 | tf_op jit(solution)/shard_map/ppermute | solution.py:37
  71.1 4.6 %collective-permute-done.13 = bf16[384,256]{1,0:T(8,128)(2,1)S(1)} collective-permute-done((bf16[384,256]{1,0:T(8,128)(2,1)S(1)}, bf16[384,256]{1,0:T(8,128)(2,1)S(1)}, u32[]{:S(2)}, u32[]{:S(2)}) %collective-permute-start.13) | collective-permute-done | bytes 196640 | tf_op jit(solution)/shard_map/ppermute | solution.py:37
  75.7 8.5 %collective-permute-done.14 = bf16[384,256]{1,0:T(8,128)(2,1)S(1)} collective-permute-done((bf16[384,256]{1,0:T(8,128)(2,1)S(1)}, bf16[384,256]{1,0:T(8,128)(2,1)S(1)}, u32[]{:S(2)}, u32[]{:S(2)}) %collective-permute-start.14) | collective-permute-done | bytes 196640 | tf_op jit(solution)/shard_map/ppermute | solution.py:37
  84.2 2.5 %collective-permute-start.16 = (bf16[384,256]{1,0:T(8,128)(2,1)S(1)}, bf16[384,256]{1,0:T(8,128)(2,1)S(1)}, u32[]{:S(2)}, u32[]{:S(2)}) collective-permute-start(bf16[384,256]{1,0:T(8,128)(2,1)S(1)} %get-tuple-element.51), channel_id=1, source_target_pairs={{0,6},{1,7},{2,0},{3,1},{4,2},{5,3},{6,4},{7,5},{8,14},{9,15},{10,... | collective-permute-start | bytes 589832 | tf_op jit(solution)/shard_map/ppermute | solution.py:37
  87.1 6.3 %shard_map.106 = (bf16[8,128,512]{2,1,0:T(8,128)(2,1)}, bf16[1,384,256]{2,1,0:T(8,128)(2,1)S(1)}, bf16[1,384,256]{2,1,0:T(8,128)(2,1)S(1)}) custom-call(s32[6]{0:T(128)S(1)} %pad_add_fusion.ends, bf16[8,2,128,512]{3,2,1,0:T(8,128)(2,1)S(1)} %all-to-all-done.rows, bf16[1,384,256]{2,1,0:T(8,128)(2,1)S(1)} %bitcast.114, ...), custom_call_target="tpu_custom_call", output_to_operand_aliasing={{0}: (4, {})} | custom-call | flops 1006632960 | bytes 6291456 | tf_op jit(solution)/shard_map/pallas_call | solution.py:212
  93.4 3.8 %collective-permute-start.18 = (bf16[384,256]{1,0:T(8,128)(2,1)S(1)}, bf16[384,256]{1,0:T(8,128)(2,1)S(1)}, u32[]{:S(2)}, u32[]{:S(2)}) collective-permute-start(bf16[384,256]{1,0:T(8,128)(2,1)S(1)} %bitcast.113), channel_id=1, source_target_pairs={{0,6},{1,7},{2,0},{3,1},{4,2},{5,3},{6,4},{7,5},{8,14},{9,15},{10,... | collective-permute-start | bytes 589832 | tf_op jit(solution)/shard_map/ppermute | solution.py:37
  97.8 4.8 %all-to-all-start.2 = ((bf16[8,128,512]{2,1,0:T(8,128)(2,1)}), bf16[8,128,512]{2,1,0:T(8,128)(2,1)}, u32[]{:S(2)}, u32[]{:S(2)}) async-start(bf16[8,128,512]{2,1,0:T(8,128)(2,1)} %get-tuple-element.62), calls=%async_computation.2 | async-start | bytes 2097152 | tf_op jit(solution)/shard_map/all_to_all | solution.py:282
  102.6 11.7 %shard_map.105 = (bf16[8,128,512]{2,1,0:T(8,128)(2,1)}, bf16[2,384,256]{2,1,0:T(8,128)(2,1)S(1)}, bf16[2,384,256]{2,1,0:T(8,128)(2,1)S(1)}) custom-call(s32[6]{0:T(128)S(1)} %pad_add_fusion.ends, bf16[8,2,128,512]{3,2,1,0:T(8,128)(2,1)} %all-to-all-done.1.rows, bf16[2,384,256]{2,1,0:T(8,128)(2,1)S(1)} %pad_maximum_fusion.3.key, ...), custom_call_target="tpu_custom_call" | custom-call | flops 2013265920 | bytes 6291456 | tf_op jit(solution)/shard_map/pallas_call | solution.py:212
  114.5 1.8 %collective-permute-start.19 = (bf16[384,512]{1,0:T(8,128)(2,1)S(1)}, bf16[384,512]{1,0:T(8,128)(2,1)}, u32[]{:S(2)}, u32[]{:S(2)}) collective-permute-start(bf16[384,512]{1,0:T(8,128)(2,1)S(1)} %pad_maximum_fusion.5), channel_id=1, source_target_pairs={{0,2},{1,3},{2,4},{3,5},{4,6},{5,7},{6,0},{7,1},{8,10},{9,11},{10,... | collective-permute-start | bytes 1179656 | tf_op jit(solution)/shard_map/ppermute | solution.py:37
  116.3 2.7 %collective-permute-start.20 = (bf16[384,512]{1,0:T(8,128)(2,1)S(1)}, bf16[384,512]{1,0:T(8,128)(2,1)}, u32[]{:S(2)}, u32[]{:S(2)}) collective-permute-start(bf16[384,512]{1,0:T(8,128)(2,1)S(1)} %pad_maximum_fusion.6), channel_id=1, source_target_pairs={{0,6},{1,7},{2,0},{3,1},{4,2},{5,3},{6,4},{7,5},{8,14},{9,15},{10,... | collective-permute-start | bytes 1179656 | tf_op jit(solution)/shard_map/ppermute | solution.py:37
  119.0 5.2 %shard_map.107.refs_0_ = bf16[128,8192]{1,0:T(8,128)(2,1)} custom-call(s32[1]{0:T(128)} %bitcast.z, bf16[8,128,512]{2,1,0:T(8,128)(2,1)} %all-to-all-done.2.source), custom_call_target="tpu_custom_call" | custom-call | bytes 2097152 | tf_op jit(solution)/shard_map/pallas_call | solution.py:140
  124.2 4.9 %all-to-all-start.3 = ((bf16[8,128,512]{2,1,0:T(8,128)(2,1)}), bf16[8,128,512]{2,1,0:T(8,128)(2,1)S(1)}, u32[]{:S(2)}, u32[]{:S(2)}) async-start(bf16[8,128,512]{2,1,0:T(8,128)(2,1)} %get-tuple-element.65), calls=%async_computation.3 | async-start | bytes 2097152 | tf_op jit(solution)/shard_map/all_to_all | solution.py:304
  129.2 8.2 %collective-permute-done.19 = bf16[384,512]{1,0:T(8,128)(2,1)} collective-permute-done((bf16[384,512]{1,0:T(8,128)(2,1)S(1)}, bf16[384,512]{1,0:T(8,128)(2,1)}, u32[]{:S(2)}, u32[]{:S(2)}) %collective-permute-start.19) | collective-permute-done | bytes 393248 | tf_op jit(solution)/shard_map/ppermute | solution.py:37
  137.3 1.3 add_add_fusion
  138.6 1.5 convolution_convert_fusion.1
  140.1 1.3 reshape.42
  142.3 1.8 convolution_convert_fusion
  144.1 1.1 all-to-all-done.3.source
  145.1 5.5 %all-to-all-start.4 = ((bf16[8,128,512]{2,1,0:T(8,128)(2,1)}), bf16[8,128,512]{2,1,0:T(8,128)(2,1)S(1)}, u32[]{:S(2)}, u32[]{:S(2)}) async-start(bf16[8,128,512]{2,1,0:T(8,128)(2,1)} %bitcast.121), calls=%async_computation.4 | async-start | bytes 2097152 | tf_op jit(solution)/shard_map/all_to_all | solution.py:313
  150.7 2.2 %collective-permute-done.21 = bf16[4,4,12,1024]{3,2,1,0:T(8,128)(2,1)} collective-permute-done((bf16[4,4,12,1024]{3,2,1,0:T(8,128)(2,1)}, bf16[4,4,12,1024]{3,2,1,0:T(8,128)(2,1)}, u32[]{:S(2)}, u32[]{:S(2)}) %collective-permute-start.21) | collective-permute-done | bytes 393248 | tf_op jit(solution)/shard_map/ppermute | solution.py:37
  152.9 1.2 fusion
  155.5 2.1 %collective-permute-start.23 = (bf16[4,12,1024]{2,1,0:T(8,128)(2,1)S(1)}, bf16[4,12,1024]{2,1,0:T(8,128)(2,1)S(1)}, u32[]{:S(2)}, u32[]{:S(2)}) collective-permute-start(bf16[4,12,1024]{2,1,0:T(8,128)(2,1)S(1)} %get-tuple-element.78), channel_id=1, source_target_pairs={{0,16},{1,17},{2,18},{3,19},{4,20},{5,21},{6,22},{7,23},{8,24},{9,... | collective-permute-start | bytes 294920 | tf_op jit(solution)/shard_map/ppermute | solution.py:37
  157.6 1.4 collective-permute-start.24
  159.0 5.5 %collective-permute-done.22 = bf16[4,12,1024]{2,1,0:T(8,128)(2,1)S(1)} collective-permute-done((bf16[4,12,1024]{2,1,0:T(8,128)(2,1)S(1)}, bf16[4,12,1024]{2,1,0:T(8,128)(2,1)S(1)}, u32[]{:S(2)}, u32[]{:S(2)}) %collective-permute-start.22) | collective-permute-done | bytes 98336 | tf_op jit(solution)/shard_map/ppermute | solution.py:37
  165.1 1.0 fusion.5
  166.3 4.0 %collective-permute-start.26 = (bf16[12,1024]{1,0:T(8,128)(2,1)S(1)}, bf16[12,1024]{1,0:T(8,128)(2,1)S(1)}, u32[]{:S(2)}, u32[]{:S(2)}) collective-permute-start(bf16[12,1024]{1,0:T(8,128)(2,1)S(1)} %get-tuple-element.93), channel_id=1, source_target_pairs={{0,4},{1,5},{2,6},{3,7},{4,0},{5,1},{6,2},{7,3},{8,12},{9,13},{10,... | collective-permute-start | bytes 73736 | tf_op jit(solution)/shard_map/ppermute | solution.py:37
  170.3 2.0 %collective-permute-start.27 = (bf16[12,1024]{1,0:T(8,128)(2,1)S(1)}, bf16[12,1024]{1,0:T(8,128)(2,1)S(1)}, u32[]{:S(2)}, u32[]{:S(2)}) collective-permute-start(bf16[12,1024]{1,0:T(8,128)(2,1)S(1)} %get-tuple-element.92), channel_id=1, source_target_pairs={{0,6},{1,7},{2,0},{3,1},{4,2},{5,3},{6,4},{7,5},{8,14},{9,15},{10,... | collective-permute-start | bytes 73736 | tf_op jit(solution)/shard_map/ppermute | solution.py:37
  172.3 5.2 %shard_map.108 = bf16[128,8192]{1,0:T(8,128)(2,1)} custom-call(s32[1]{0:T(128)} %bitcast.z, bf16[8,128,512]{2,1,0:T(8,128)(2,1)} %copy-done, bf16[128,8192]{1,0:T(8,128)(2,1)} %shard_map.107.refs_0_), custom_call_target="tpu_custom_call", output_to_operand_aliasing={{}: (2, {})} | custom-call | bytes 2097152 | tf_op jit(solution)/shard_map/pallas_call | solution.py:140
  (85 shorter events, 14.4 us)
Async XLA Ops:
  2.9 11.5 %collective-permute-start = (bf16[16,1024]{1,0:T(8,128)(2,1)S(1)}, bf16[16,1024]{1,0:T(8,128)(2,1)S(1)}, u32[]{:S(2)}, u32[]{:S(2)}) collective-permute-start(bf16[16,1024]{1,0:T(8,128)(2,1)S(1)} %fusion.16), channel_id=1, source_target_pairs={{0,24},{1,25},{2,26},{3,27},{4,28},{5,29},{6,30},{7,31},{8,0},{9,1... | collective-permute-start | bytes 98312 | tf_op jit(solution)/shard_map/ppermute | solution.py:37
  5.9 8.4 %collective-permute-start.1 = (bf16[16,1024]{1,0:T(8,128)(2,1)S(1)}, bf16[16,1024]{1,0:T(8,128)(2,1)S(1)}, u32[]{:S(2)}, u32[]{:S(2)}) collective-permute-start(bf16[16,1024]{1,0:T(8,128)(2,1)S(1)} %fusion.16), channel_id=1, source_target_pairs={{0,16},{1,17},{2,18},{3,19},{4,20},{5,21},{6,22},{7,23},{8,24},{9,... | collective-permute-start | bytes 98312 | tf_op jit(solution)/shard_map/ppermute | solution.py:37
  6.5 7.8 %collective-permute-start.2 = (bf16[16,1024]{1,0:T(8,128)(2,1)S(1)}, bf16[16,1024]{1,0:T(8,128)(2,1)S(1)}, u32[]{:S(2)}, u32[]{:S(2)}) collective-permute-start(bf16[16,1024]{1,0:T(8,128)(2,1)S(1)} %fusion.16), channel_id=1, source_target_pairs={{0,8},{1,9},{2,10},{3,11},{4,12},{5,13},{6,14},{7,15},{8,16},{9,17... | collective-permute-start | bytes 98312 | tf_op jit(solution)/shard_map/ppermute | solution.py:37
  8.4 6.1 %collective-permute-start.3 = (bf16[1,128,512]{2,1,0:T(8,128)(2,1)S(1)}, bf16[1,128,512]{2,1,0:T(8,128)(2,1)S(1)}, u32[]{:S(2)}, u32[]{:S(2)}) collective-permute-start(bf16[1,128,512]{2,1,0:T(8,128)(2,1)S(1)} %maximum_bitcast_fusion), channel_id=1, source_target_pairs={{0,32},{32,0},{64,96},{96,64},{128,160},{160,128},{192,224},{224,1... | collective-permute-start | bytes 393224 | tf_op jit(solution)/shard_map/ppermute | solution.py:50
  10.4 4.0 %copy-start.6 = (bf16[12,1024]{1,0:T(8,128)(2,1)S(1)}, bf16[12,1024]{1,0:T(8,128)(2,1)}, u32[]{:S(2)}) copy-start(bf16[12,1024]{1,0:T(8,128)(2,1)} %param.9) | copy-start | bytes 73732
  10.4 4.1 %copy-start.4 = (bf16[128,256]{1,0:T(8,128)(2,1)S(1)}, bf16[128,256]{1,0:T(8,128)(2,1)}, u32[]{:S(2)}) copy-start(bf16[128,256]{1,0:T(8,128)(2,1)} %param.11) | copy-start | bytes 196612
  10.4 4.1 %copy-start.5 = (bf16[128,256]{1,0:T(8,128)(2,1)S(1)}, bf16[128,256]{1,0:T(8,128)(2,1)}, u32[]{:S(2)}) copy-start(bf16[128,256]{1,0:T(8,128)(2,1)} %param.10) | copy-start | bytes 196612
  14.6 33.8 %all-to-all-start = ((bf16[8,2,128,512]{3,2,1,0:T(8,128)(2,1)}), bf16[8,2,128,512]{3,2,1,0:T(8,128)(2,1)S(1)}, u32[]{:S(2)}, u32[]{:S(2)}) async-start(bf16[8,2,128,512]{3,2,1,0:T(8,128)(2,1)} %shard_map.102), calls=%async_computation | async-start | bytes 4194304 | tf_op jit(solution)/shard_map/all_to_all | solution.py:265
  18.2 11.3 %collective-permute-start.4 = (bf16[4,16,1024]{2,1,0:T(8,128)(2,1)S(1)}, bf16[4,16,1024]{2,1,0:T(8,128)(2,1)S(1)}, u32[]{:S(2)}, u32[]{:S(2)}) collective-permute-start(bf16[4,16,1024]{2,1,0:T(8,128)(2,1)S(1)} %pad_maximum_fusion.8), channel_id=1, source_target_pairs={{0,6},{1,7},{2,0},{3,1},{4,2},{5,3},{6,4},{7,5},{8,14},{9,15},{10,... | collective-permute-start | bytes 393224 | tf_op jit(solution)/shard_map/ppermute | solution.py:37
  23.7 13.8 %collective-permute-start.5 = (bf16[4,16,1024]{2,1,0:T(8,128)(2,1)S(1)}, bf16[4,16,1024]{2,1,0:T(8,128)(2,1)S(1)}, u32[]{:S(2)}, u32[]{:S(2)}) collective-permute-start(bf16[4,16,1024]{2,1,0:T(8,128)(2,1)S(1)} %pad_maximum_fusion.8), channel_id=1, source_target_pairs={{0,4},{1,5},{2,6},{3,7},{4,0},{5,1},{6,2},{7,3},{8,12},{9,13},{10,... | collective-permute-start | bytes 393224 | tf_op jit(solution)/shard_map/ppermute | solution.py:37
  25.2 12.4 %collective-permute-start.6 = (bf16[4,16,1024]{2,1,0:T(8,128)(2,1)S(1)}, bf16[4,16,1024]{2,1,0:T(8,128)(2,1)S(1)}, u32[]{:S(2)}, u32[]{:S(2)}) collective-permute-start(bf16[4,16,1024]{2,1,0:T(8,128)(2,1)S(1)} %pad_maximum_fusion.8), channel_id=1, source_target_pairs={{0,2},{1,3},{2,4},{3,5},{4,6},{5,7},{6,0},{7,1},{8,10},{9,11},{10,... | collective-permute-start | bytes 393224 | tf_op jit(solution)/shard_map/ppermute | solution.py:37
  27.5 14.2 %collective-permute-start.10 = (bf16[2,128,512]{2,1,0:T(8,128)(2,1)S(1)}, bf16[2,128,512]{2,1,0:T(8,128)(2,1)}, u32[]{:S(2)}, u32[]{:S(2)}) collective-permute-start(bf16[2,128,512]{2,1,0:T(8,128)(2,1)S(1)} %pad_maximum_fusion.7), channel_id=1, source_target_pairs={{0,64},{32,96},{64,128},{96,160},{128,192},{160,224},{192,0},{224,... | collective-permute-start | bytes 786440 | tf_op jit(solution)/shard_map/ppermute | solution.py:60
  29.0 12.7 %collective-permute-start.8 = (bf16[2,128,512]{2,1,0:T(8,128)(2,1)S(1)}, bf16[2,128,512]{2,1,0:T(8,128)(2,1)}, u32[]{:S(2)}, u32[]{:S(2)}) collective-permute-start(bf16[2,128,512]{2,1,0:T(8,128)(2,1)S(1)} %pad_maximum_fusion.7), channel_id=1, source_target_pairs={{0,192},{32,224},{64,0},{96,32},{128,64},{160,96},{192,128},{224,1... | collective-permute-start | bytes 786440 | tf_op jit(solution)/shard_map/ppermute | solution.py:60
  29.6 13.3 %collective-permute-start.9 = (bf16[2,128,512]{2,1,0:T(8,128)(2,1)S(1)}, bf16[2,128,512]{2,1,0:T(8,128)(2,1)}, u32[]{:S(2)}, u32[]{:S(2)}) collective-permute-start(bf16[2,128,512]{2,1,0:T(8,128)(2,1)S(1)} %pad_maximum_fusion.7), channel_id=1, source_target_pairs={{0,128},{32,160},{64,192},{96,224},{128,0},{160,32},{192,64},{224,... | collective-permute-start | bytes 786440 | tf_op jit(solution)/shard_map/ppermute | solution.py:60
  37.7 7.5 %collective-permute-start.7 = (bf16[4,4,16,1024]{3,2,0,1:T(8,128)(2,1)S(1)}, bf16[4,4,16,1024]{3,2,0,1:T(8,128)(2,1)S(1)}, u32[]{:S(2)}, u32[]{:S(2)}) collective-permute-start(bf16[4,4,16,1024]{3,2,0,1:T(8,128)(2,1)S(1)} %pad_maximum_fusion.2), channel_id=1, source_target_pairs={{0,1},{1,0},{2,3},{3,2},{4,5},{5,4},{6,7},{7,6},{8,9},{9,8},{10,11... | collective-permute-start | bytes 1572872 | tf_op jit(solution)/shard_map/ppermute | solution.py:37
  48.4 49.4 %all-to-all-start.1 = ((bf16[8,2,128,512]{3,2,1,0:T(8,128)(2,1)}), bf16[8,2,128,512]{3,2,1,0:T(8,128)(2,1)}, u32[]{:S(2)}, u32[]{:S(2)}) async-start(bf16[8,2,128,512]{3,2,1,0:T(8,128)(2,1)} %shard_map.103), calls=%async_computation.1 | async-start | bytes 4194304 | tf_op jit(solution)/shard_map/all_to_all | solution.py:269
  55.4 12.7 %collective-permute-start.11 = (bf16[384,256]{1,0:T(8,128)(2,1)S(1)}, bf16[384,256]{1,0:T(8,128)(2,1)S(1)}, u32[]{:S(2)}, u32[]{:S(2)}) collective-permute-start(bf16[384,256]{1,0:T(8,128)(2,1)S(1)} %get-tuple-element.50), channel_id=1, source_target_pairs={{0,6},{1,7},{2,0},{3,1},{4,2},{5,3},{6,4},{7,5},{8,14},{9,15},{10,... | collective-permute-start | bytes 589832 | tf_op jit(solution)/shard_map/ppermute | solution.py:37
  58.3 9.8 %collective-permute-start.12 = (bf16[384,256]{1,0:T(8,128)(2,1)S(1)}, bf16[384,256]{1,0:T(8,128)(2,1)S(1)}, u32[]{:S(2)}, u32[]{:S(2)}) collective-permute-start(bf16[384,256]{1,0:T(8,128)(2,1)S(1)} %get-tuple-element.51), channel_id=1, source_target_pairs={{0,2},{1,3},{2,4},{3,5},{4,6},{5,7},{6,0},{7,1},{8,10},{9,11},{10,... | collective-permute-start | bytes 589832 | tf_op jit(solution)/shard_map/ppermute | solution.py:37
  68.1 7.6 %collective-permute-start.13 = (bf16[384,256]{1,0:T(8,128)(2,1)S(1)}, bf16[384,256]{1,0:T(8,128)(2,1)S(1)}, u32[]{:S(2)}, u32[]{:S(2)}) collective-permute-start(bf16[384,256]{1,0:T(8,128)(2,1)S(1)} %collective-permute-done.11), channel_id=1, source_target_pairs={{0,6},{1,7},{2,0},{3,1},{4,2},{5,3},{6,4},{7,5},{8,14},{9,15},{10,... | collective-permute-start | bytes 589832 | tf_op jit(solution)/shard_map/ppermute | solution.py:37
  71.1 13.0 %collective-permute-start.14 = (bf16[384,256]{1,0:T(8,128)(2,1)S(1)}, bf16[384,256]{1,0:T(8,128)(2,1)S(1)}, u32[]{:S(2)}, u32[]{:S(2)}) collective-permute-start(bf16[384,256]{1,0:T(8,128)(2,1)S(1)} %collective-permute-done.12), channel_id=1, source_target_pairs={{0,2},{1,3},{2,4},{3,5},{4,6},{5,7},{6,0},{7,1},{8,10},{9,11},{10,... | collective-permute-start | bytes 589832 | tf_op jit(solution)/shard_map/ppermute | solution.py:37
  84.2 13.0 %collective-permute-start.16 = (bf16[384,256]{1,0:T(8,128)(2,1)S(1)}, bf16[384,256]{1,0:T(8,128)(2,1)S(1)}, u32[]{:S(2)}, u32[]{:S(2)}) collective-permute-start(bf16[384,256]{1,0:T(8,128)(2,1)S(1)} %get-tuple-element.51), channel_id=1, source_target_pairs={{0,6},{1,7},{2,0},{3,1},{4,2},{5,3},{6,4},{7,5},{8,14},{9,15},{10,... | collective-permute-start | bytes 589832 | tf_op jit(solution)/shard_map/ppermute | solution.py:37
  86.7 11.0 %collective-permute-start.15 = (bf16[384,256]{1,0:T(8,128)(2,1)S(1)}, bf16[384,256]{1,0:T(8,128)(2,1)S(1)}, u32[]{:S(2)}, u32[]{:S(2)}) collective-permute-start(bf16[384,256]{1,0:T(8,128)(2,1)S(1)} %get-tuple-element.50), channel_id=1, source_target_pairs={{0,2},{1,3},{2,4},{3,5},{4,6},{5,7},{6,0},{7,1},{8,10},{9,11},{10,... | collective-permute-start | bytes 589832 | tf_op jit(solution)/shard_map/ppermute | solution.py:37
  93.4 20.9 %collective-permute-start.18 = (bf16[384,256]{1,0:T(8,128)(2,1)S(1)}, bf16[384,256]{1,0:T(8,128)(2,1)S(1)}, u32[]{:S(2)}, u32[]{:S(2)}) collective-permute-start(bf16[384,256]{1,0:T(8,128)(2,1)S(1)} %bitcast.113), channel_id=1, source_target_pairs={{0,6},{1,7},{2,0},{3,1},{4,2},{5,3},{6,4},{7,5},{8,14},{9,15},{10,... | collective-permute-start | bytes 589832 | tf_op jit(solution)/shard_map/ppermute | solution.py:37
  97.2 17.3 %collective-permute-start.17 = (bf16[384,256]{1,0:T(8,128)(2,1)S(1)}, bf16[384,256]{1,0:T(8,128)(2,1)S(1)}, u32[]{:S(2)}, u32[]{:S(2)}) collective-permute-start(bf16[384,256]{1,0:T(8,128)(2,1)S(1)} %bitcast.112), channel_id=1, source_target_pairs={{0,2},{1,3},{2,4},{3,5},{4,6},{5,7},{6,0},{7,1},{8,10},{9,11},{10,... | collective-permute-start | bytes 589832 | tf_op jit(solution)/shard_map/ppermute | solution.py:37
  97.8 21.2 %all-to-all-start.2 = ((bf16[8,128,512]{2,1,0:T(8,128)(2,1)}), bf16[8,128,512]{2,1,0:T(8,128)(2,1)}, u32[]{:S(2)}, u32[]{:S(2)}) async-start(bf16[8,128,512]{2,1,0:T(8,128)(2,1)} %get-tuple-element.62), calls=%async_computation.2 | async-start | bytes 2097152 | tf_op jit(solution)/shard_map/all_to_all | solution.py:282
  114.5 22.8 %collective-permute-start.19 = (bf16[384,512]{1,0:T(8,128)(2,1)S(1)}, bf16[384,512]{1,0:T(8,128)(2,1)}, u32[]{:S(2)}, u32[]{:S(2)}) collective-permute-start(bf16[384,512]{1,0:T(8,128)(2,1)S(1)} %pad_maximum_fusion.5), channel_id=1, source_target_pairs={{0,2},{1,3},{2,4},{3,5},{4,6},{5,7},{6,0},{7,1},{8,10},{9,11},{10,... | collective-permute-start | bytes 1179656 | tf_op jit(solution)/shard_map/ppermute | solution.py:37
  116.3 21.0 %collective-permute-start.20 = (bf16[384,512]{1,0:T(8,128)(2,1)S(1)}, bf16[384,512]{1,0:T(8,128)(2,1)}, u32[]{:S(2)}, u32[]{:S(2)}) collective-permute-start(bf16[384,512]{1,0:T(8,128)(2,1)S(1)} %pad_maximum_fusion.6), channel_id=1, source_target_pairs={{0,6},{1,7},{2,0},{3,1},{4,2},{5,3},{6,4},{7,5},{8,14},{9,15},{10,... | collective-permute-start | bytes 1179656 | tf_op jit(solution)/shard_map/ppermute | solution.py:37
  124.2 14.4 %copy-start.2 = (bf16[4,2,128,512]{3,2,1,0:T(8,128)(2,1)S(1)}, bf16[4,2,128,512]{3,2,1,0:T(8,128)(2,1)}, u32[]{:S(2)}) copy-start(bf16[4,2,128,512]{3,2,1,0:T(8,128)(2,1)} %pad_maximum_fusion.1) | copy-start | bytes 3145732
  124.2 20.9 %all-to-all-start.3 = ((bf16[8,128,512]{2,1,0:T(8,128)(2,1)}), bf16[8,128,512]{2,1,0:T(8,128)(2,1)S(1)}, u32[]{:S(2)}, u32[]{:S(2)}) async-start(bf16[8,128,512]{2,1,0:T(8,128)(2,1)} %get-tuple-element.65), calls=%async_computation.3 | async-start | bytes 2097152 | tf_op jit(solution)/shard_map/all_to_all | solution.py:304
  140.1 2.2 %copy-start.3 = (bf16[384,1024]{1,0:T(8,128)(2,1)S(1)}, bf16[384,1024]{1,0:T(8,128)(2,1)}, u32[]{:S(2)}) copy-start(bf16[384,1024]{1,0:T(8,128)(2,1)} %reshape.41) | copy-start | bytes 2359300
  145.1 9.1 %copy-start = (bf16[8,128,512]{2,1,0:T(8,128)(2,1)}, bf16[8,128,512]{2,1,0:T(8,128)(2,1)S(1)}, u32[]{:S(2)}) copy-start(bf16[8,128,512]{2,1,0:T(8,128)(2,1)S(1)} %all-to-all-done.3.source) | copy-start | bytes 3145732
  145.1 33.0 %all-to-all-start.4 = ((bf16[8,128,512]{2,1,0:T(8,128)(2,1)}), bf16[8,128,512]{2,1,0:T(8,128)(2,1)S(1)}, u32[]{:S(2)}, u32[]{:S(2)}) async-start(bf16[8,128,512]{2,1,0:T(8,128)(2,1)} %bitcast.121), calls=%async_computation.4 | async-start | bytes 2097152 | tf_op jit(solution)/shard_map/all_to_all | solution.py:313
  150.7 2.3 %collective-permute-start.21 = (bf16[4,4,12,1024]{3,2,1,0:T(8,128)(2,1)}, bf16[4,4,12,1024]{3,2,1,0:T(8,128)(2,1)}, u32[]{:S(2)}, u32[]{:S(2)}) collective-permute-start(bf16[4,4,12,1024]{3,2,1,0:T(8,128)(2,1)} %dynamic-slice_bitcast_fusion), channel_id=1, source_target_pairs={{0,1},{1,0},{2,3},{3,2},{4,5},{5,4},{6,7},{7,6},{8,9},{9,8},{10,11... | collective-permute-start | bytes 1179656 | tf_op jit(solution)/shard_map/ppermute | solution.py:37
  154.2 0.8 copy-start.1
  155.0 9.6 %collective-permute-start.22 = (bf16[4,12,1024]{2,1,0:T(8,128)(2,1)S(1)}, bf16[4,12,1024]{2,1,0:T(8,128)(2,1)S(1)}, u32[]{:S(2)}, u32[]{:S(2)}) collective-permute-start(bf16[4,12,1024]{2,1,0:T(8,128)(2,1)S(1)} %get-tuple-element.76), channel_id=1, source_target_pairs={{0,8},{1,9},{2,10},{3,11},{4,12},{5,13},{6,14},{7,15},{8,16},{9,17... | collective-permute-start | bytes 294920 | tf_op jit(solution)/shard_map/ppermute | solution.py:37
  155.5 9.0 %collective-permute-start.23 = (bf16[4,12,1024]{2,1,0:T(8,128)(2,1)S(1)}, bf16[4,12,1024]{2,1,0:T(8,128)(2,1)S(1)}, u32[]{:S(2)}, u32[]{:S(2)}) collective-permute-start(bf16[4,12,1024]{2,1,0:T(8,128)(2,1)S(1)} %get-tuple-element.78), channel_id=1, source_target_pairs={{0,16},{1,17},{2,18},{3,19},{4,20},{5,21},{6,22},{7,23},{8,24},{9,... | collective-permute-start | bytes 294920 | tf_op jit(solution)/shard_map/ppermute | solution.py:37
  157.6 7.5 %collective-permute-start.24 = (bf16[4,12,1024]{2,1,0:T(8,128)(2,1)S(1)}, bf16[4,12,1024]{2,1,0:T(8,128)(2,1)S(1)}, u32[]{:S(2)}, u32[]{:S(2)}) collective-permute-start(bf16[4,12,1024]{2,1,0:T(8,128)(2,1)S(1)} %get-tuple-element.77), channel_id=1, source_target_pairs={{0,24},{1,25},{2,26},{3,27},{4,28},{5,29},{6,30},{7,31},{8,0},{9,1... | collective-permute-start | bytes 294920 | tf_op jit(solution)/shard_map/ppermute | solution.py:37
  166.1 11.4 %collective-permute-start.25 = (bf16[12,1024]{1,0:T(8,128)(2,1)S(1)}, bf16[12,1024]{1,0:T(8,128)(2,1)S(1)}, u32[]{:S(2)}, u32[]{:S(2)}) collective-permute-start(bf16[12,1024]{1,0:T(8,128)(2,1)S(1)} %get-tuple-element.91), channel_id=1, source_target_pairs={{0,2},{1,3},{2,4},{3,5},{4,6},{5,7},{6,0},{7,1},{8,10},{9,11},{10,... | collective-permute-start | bytes 73736 | tf_op jit(solution)/shard_map/ppermute | solution.py:37
  166.3 11.2 %collective-permute-start.26 = (bf16[12,1024]{1,0:T(8,128)(2,1)S(1)}, bf16[12,1024]{1,0:T(8,128)(2,1)S(1)}, u32[]{:S(2)}, u32[]{:S(2)}) collective-permute-start(bf16[12,1024]{1,0:T(8,128)(2,1)S(1)} %get-tuple-element.93), channel_id=1, source_target_pairs={{0,4},{1,5},{2,6},{3,7},{4,0},{5,1},{6,2},{7,3},{8,12},{9,13},{10,... | collective-permute-start | bytes 73736 | tf_op jit(solution)/shard_map/ppermute | solution.py:37
  170.3 7.2 %collective-permute-start.27 = (bf16[12,1024]{1,0:T(8,128)(2,1)S(1)}, bf16[12,1024]{1,0:T(8,128)(2,1)S(1)}, u32[]{:S(2)}, u32[]{:S(2)}) collective-permute-start(bf16[12,1024]{1,0:T(8,128)(2,1)S(1)} %get-tuple-element.92), channel_id=1, source_target_pairs={{0,6},{1,7},{2,0},{3,1},{4,2},{5,3},{6,4},{7,5},{8,14},{9,15},{10,... | collective-permute-start | bytes 73736 | tf_op jit(solution)/shard_map/ppermute | solution.py:37

commit v5 on v4

--- a/solution.py
+++ b/solution.py
@@ -17,7 +17,7 @@
 ENC_ROWS = 12
 FEATURES = 256
 SHARED_Z = [[(y * NZ + z) * NC + c for y in range(NY) for c in range(NC)] for z in range(NZ)]
-GROUPS = ((0, 2), (1, 3))
+GROUPS = ((1, 3), (0, 2))
 
 BF16, F32 = jnp.bfloat16, jnp.float32
 
@@ -77,23 +77,34 @@
     return gathered.reshape(NY * NZ * NC, *block.shape), weight.reshape(-1, weight.shape[2]), packed, later
 
 
-def sum_encoder(part, later, last):
+def at(value, index, axis):
+    start = [0] * value.ndim
+    start[axis] = index
+    size = [1 if i == axis else n for i, n in enumerate(value.shape)]
+    return lax.dynamic_slice(value, start, size, allow_negative_indices=False).squeeze(axis)
+
+
+def half_sum(part, axis, bit):
+    mine = (lax.axis_index("dp") & bit) == 0
+    low, high = (lax.index_in_dim(part, i, axis, keepdims=False) for i in range(2))
+    other = lax.ppermute(jnp.where(mine, high, low), "dp", [(d, d ^ bit) for d in range(NX * NL)])
+    return jnp.where(mine, low, high).astype(F32) + other.astype(F32)
+
+
+def sums(part, encoder, rounded, returned):
     y, z, c = place()
-
-    def at(value, index, axis):
-        start = [0] * value.ndim
-        start[axis] = index
-        size = [1 if i == axis else n for i, n in enumerate(value.shape)]
-        return lax.dynamic_slice(value, start, size, allow_negative_indices=False).squeeze(axis)
-
-    sent, later = lax.optimization_barrier((at(part, 1 - c, 2), later))
-    arrived = shift(sent, dc=1)
+    arrived = shift(at(part, 1 - c, 2), dc=1)
     total = (at(part, c, 2).astype(F32) + arrived.astype(F32)).astype(BF16)
+    term = lax.dot_general(encoder, rounded, (((0,), (0,)), ((), ())), preferred_element_type=F32)
+    term = half_sum(term.astype(BF16).reshape(2, 2, 2, -1, 2 * FEATURES), 1, 2).astype(BF16)
+    total, returned = lax.optimization_barrier((total, returned))
     arrived = [shift(at(total, (y + d) & 3, 0), dy=d) for d in range(1, NY)]
     total = sum((a.astype(F32) for a in arrived), at(total, y, 0).astype(F32)).astype(BF16)
-    total, last = lax.optimization_barrier((total, last))
+    _, term, returned = lax.optimization_barrier((total, term, returned))
     arrived = [shift(at(total, (z + d) & 3, 0), dz=d) for d in range(1, NZ)]
-    return sum((a.astype(F32) for a in arrived), at(total, z, 0).astype(F32)).astype(BF16), later, last
+    enc_grad = sum((a.astype(F32) for a in arrived), at(total, z, 0).astype(F32)).astype(BF16)
+    weight_grad = half_sum(half_sum(term, 0, 4).astype(BF16), 0, 1)
+    return enc_grad, weight_grad, returned
 
 
 def pack_kernel(z, *refs):
@@ -127,35 +138,33 @@
     )(z, *[queries, grads] * len(group))
 
 
-def unpack_kernel(z, source, *refs):
-    out = refs[-1]
-    for c in range(NC):
-        out[:, pl.ds(c * FEATURES, FEATURES)] = source[c]
-
-
-def unpack(group, z, arrived, into=None):
-    assert group[1] == group[0] + 2
-    width = NC * FEATURES
-    given = [] if into is None else [into]
+def unpack_kernel(z, *refs):
+    sources, out = refs[:-1], refs[-1]
+    for group, source in zip(GROUPS, sources, strict=True):
+        for i, distance in enumerate(group):
+            for c in range(NC):
+                start = (lax.rem(z[0] + distance, NZ) * NC + c) * FEATURES
+                columns = pl.ds(pl.multiple_of(start, FEATURES), FEATURES)
+                out[:, columns] = source[c, :, pl.ds(i * FEATURES, FEATURES)]
+
+
+def unpack(z, arrived):
+    width = NZ * NC * FEATURES
     return pl.pallas_call(
         unpack_kernel,
-        out_shape=jax.ShapeDtypeStruct((ROWS, NY * NZ * width), BF16),
+        out_shape=jax.ShapeDtypeStruct((ROWS, NY * width), BF16),
         grid_spec=pltpu.PrefetchScalarGridSpec(
             num_scalar_prefetch=1,
-            grid=(NY, 2),
+            grid=(NY,),
             in_specs=[
-                pl.BlockSpec((NC, ROWS, FEATURES), lambda y, i, z: (y, 0, i)),
-                *[pl.BlockSpec(memory_space=pl.ANY) for _ in given],
+                pl.BlockSpec((NC, ROWS, a.shape[2]), lambda y, z: (y, 0, 0)) for a in arrived
             ],
-            out_specs=pl.BlockSpec(
-                (ROWS, width), lambda y, i, z: (0, y * NZ + lax.rem(z[0] + group[0] + 2 * i, NZ))
-            ),
-        ),
-        input_output_aliases={2: 0} if given else {},
+            out_specs=pl.BlockSpec((ROWS, width), lambda y, z: (0, y)),
+        ),
         cost_estimate=pl.CostEstimate(
-            flops=0, bytes_accessed=4 * ROWS * NY * 2 * width, transcendentals=0
-        ),
-    )(z, arrived, *given)
+            flops=0, bytes_accessed=4 * ROWS * NY * width, transcendentals=0
+        ),
+    )(z, *arrived)
 
 
 def attend_kernel(ends, rows, key, value, *refs):
@@ -178,27 +187,20 @@
             bias[:, pl.ds(y * tile, tile)] = jnp.where(allowed, 0.0, -jnp.inf)
 
     keys, values = key[0], value[0]
-    keys_turned = keys.T
-    key_total = jnp.zeros((KEYS, HEAD_DIM), F32)
-    value_total = jnp.zeros((KEYS, HEAD_DIM), F32)
-    last = (((1,), (1,)), ((), ()))
-    for y in range(NY):
-        query = rows[pl.ds(y * NC, NC), 0].reshape(tile, HEAD_DIM)
-        grad = rows[pl.ds(y * NC, NC), 1].reshape(tile, HEAD_DIM)
-        scores = lax.dot_general(keys, query, last, preferred_element_type=F32)
-        scores = scores + bias[:, pl.ds(y * tile, tile)]
-        weights = jnp.exp(scores - jnp.max(scores, axis=0, keepdims=True))
-        probability = weights * (1.0 / jnp.sum(weights, axis=0, keepdims=True))
-        upstream = lax.dot_general(values, grad, last, preferred_element_type=F32)
-        row_dot = jnp.sum(probability * upstream, axis=0, keepdims=True)
-        score_grad = (probability * (upstream - row_dot)).astype(BF16)
-        rounded = probability.astype(BF16)
-        key_total += jnp.dot(score_grad, query, preferred_element_type=F32)
-        value_total += jnp.dot(rounded, grad, preferred_element_type=F32)
-        turned = jnp.dot(keys_turned, score_grad, preferred_element_type=F32)
-        query_grad[pl.ds(y * NC, NC)] = turned.T.astype(BF16).reshape(NC, ROWS, HEAD_DIM)
-    key_grad[0] = key_total.astype(BF16)
-    value_grad[0] = value_total.astype(BF16)
+    last, first = (((1,), (1,)), ((), ())), (((0,), (0,)), ((), ()))
+    query = rows[:, 0].reshape(PEERS * ROWS, HEAD_DIM)
+    grad = rows[:, 1].reshape(PEERS * ROWS, HEAD_DIM)
+    scores = lax.dot_general(keys, query, last, preferred_element_type=F32) + bias[...]
+    weights = jnp.exp(scores - jnp.max(scores, axis=0, keepdims=True))
+    probability = weights * (1.0 / jnp.sum(weights, axis=0, keepdims=True))
+    upstream = lax.dot_general(values, grad, last, preferred_element_type=F32)
+    row_dot = jnp.sum(probability * upstream, axis=0, keepdims=True)
+    score_grad = (probability * (upstream - row_dot)).astype(BF16)
+    rounded = probability.astype(BF16)
+    key_grad[0] = jnp.dot(score_grad, query, preferred_element_type=F32).astype(BF16)
+    value_grad[0] = jnp.dot(rounded, grad, preferred_element_type=F32).astype(BF16)
+    returned = lax.dot_general(score_grad, keys, first, preferred_element_type=F32)
+    query_grad[...] = returned.astype(BF16).reshape(PEERS, ROWS, HEAD_DIM)
 
 
 def attend(ends, rows, first, keys, values, into=None):
@@ -269,49 +271,49 @@
     far = swap(far_packed)
 
     own_key, own_value = own[:, :FEATURES], own[:, FEATURES:]
-    key_ahead, value_behind = shift(own_key, dz=-1), shift(own_value, dz=1)
-    back, key_0, value_0 = attend(ends, near, 0, own_key[None], own_value[None])
-    key_ahead, value_behind, back = lax.optimization_barrier((key_ahead, value_behind, back))
+    ahead, behind = shift(own, dz=-1), shift(own, dz=1)
+    key_ahead, value_ahead = ahead[:, :FEATURES], ahead[:, FEATURES:]
+    key_behind, value_behind = behind[:, :FEATURES], behind[:, FEATURES:]
     key_opposite, value_opposite = shift(key_ahead, dz=-1), shift(value_behind, dz=1)
-    later_key, later_value, key_opposite, value_opposite = lax.optimization_barrier(
-        (own_key, own_value, key_opposite, value_opposite)
-    )
-    key_behind, value_ahead = shift(later_key, dz=1), shift(later_value, dz=-1)
-
-    back, key_2, value_2 = attend(ends, near, 1, key_opposite[None], value_opposite[None], back)
-    back_near = swap(back)
-    back, key_1, value_1 = attend(
+
+    back_near, key_1, value_1 = attend(
         ends,
-        far,
+        near,
         0,
         jnp.stack([key_ahead, key_behind]),
         jnp.stack([value_ahead, value_behind]),
     )
+    key_opposite, value_opposite, key_1, value_1 = lax.optimization_barrier(
+        (key_opposite, value_opposite, key_1, value_1)
+    )
+    value_part, key_part = shift(value_1[0], dz=1), shift(key_1[1], dz=-1)
+    back, key_2, value_2 = attend(ends, far, 1, key_opposite[None], value_opposite[None])
+    key_2, value_2, own_key, own_value = lax.optimization_barrier(
+        (key_2, value_2, own_key, own_value)
+    )
+    key_sum, value_sum = shift(key_2[0], dz=1), shift(value_2[0], dz=-1)
+    back, key_0, value_0 = attend(ends, far, 0, own_key[None], own_value[None], back)
+    back_near = swap(back_near)
+    key_sum, value_sum, key_part, value_part, key_0, value_0, back, back_near = (
+        lax.optimization_barrier(
+            (key_sum, value_sum, key_part, value_part, key_0, value_0, back, back_near)
+        )
+    )
 
     def joined(a, b):
         return (a.astype(F32) + b.astype(F32)).astype(BF16)
 
-    key_sum = joined(key_1[0], shift(key_2[0], dz=1))
-    value_sum = joined(value_1[1], shift(value_2[0], dz=-1))
-    for_ahead = jnp.concatenate([key_sum, value_1[0]], axis=1)
-    for_behind = jnp.concatenate([key_1[1], value_sum], axis=1)
-    for_ahead, for_behind, back = lax.optimization_barrier((for_ahead, for_behind, back))
-    total = jnp.concatenate([key_0[0], value_0[0]], axis=1).astype(F32)
-    total += shift(for_ahead, dz=1).astype(F32) + shift(for_behind, dz=-1).astype(F32)
-
-    query_grad = unpack(GROUPS[0], z_index, back_near)
-    total, query_grad = lax.optimization_barrier((total, query_grad))
-    back = swap(back)
-    rounded = total.astype(BF16)
+    key_sum, value_sum = joined(key_1[0], key_sum), joined(value_1[1], value_sum)
+    own_terms = jnp.concatenate([key_0[0], value_0[0]], axis=1).astype(F32)
+    own_terms += jnp.concatenate([key_part, value_part], axis=1).astype(F32)
+    arrived = jnp.concatenate([shift(key_sum, dz=1), shift(value_sum, dz=-1)], axis=1)
+    rounded = (own_terms + arrived.astype(F32)).astype(BF16)
+    back_far = swap(back)
+
     part = lax.dot_general(rounded, weight, (((1,), (1,)), ((), ())), preferred_element_type=F32)
     part = part.astype(BF16).reshape(NY, NZ, NC, ENC_ROWS, -1)
-    enc_grad, encoder, back = sum_encoder(part, encoder, back)
-    query_grad = unpack(GROUPS[1], z_index, back, query_grad)
-
-    term = lax.dot_general(encoder, rounded, (((0,), (0,)), ((), ())), preferred_element_type=F32)
-    pieces = term.astype(BF16).reshape(NX * NL, -1, 2 * FEATURES)
-    pieces = lax.all_to_all(pieces, "dp", 0, 0, tiled=True)
-    weight_grad = pieces.astype(F32).sum(axis=0)
+    enc_grad, weight_grad, returned = sums(part, encoder, rounded, [back_near, back_far])
+    query_grad = unpack(z_index, returned)
     return query_grad, enc_grad, weight_grad[:, :FEATURES], weight_grad[:, FEATURES:]
 
 

time: 180 us -> 176 us (0.978)
  Pallas kernels: 42.5 us -> 31.8 us
  waiting for transfers between devices: 41.4 us -> 44.4 us
    ppermute x0 -> x3, waiting for transfers between devices: none -> 7.46 us  [half_sum(): lax.ppermute(jnp.where(mine, high, low), 'dp', [(d, d ^ bit) for d in ran...]
    ppermute x24, waiting for transfers between devices: 39.2 us -> 32.4 us  [shift(): return lax.ppermute(value, 'ctx', pairs)]
    pallas_call x2 -> x1, Pallas kernels: 10.4 us -> 3.82 us  [unpack(): pl.pallas_call(unpack_kernel, out_shape=jax.ShapeDtypeStruct((ROWS, NY *...]
    all_to_all x3 -> x2, starting transfers between devices: 15.2 us -> 9.01 us  [the longest x1 4.58 us: body(): back_near = swap(back_near)]
    ppermute x0 -> x3, starting transfers between devices: none -> 5.6 us  [half_sum(): lax.ppermute(jnp.where(mine, high, low), 'dp', [(d, d ^ bit) for d in ran...]
    pallas_call x3, Pallas kernels: 24.3 us -> 20.2 us  [attend(): pl.pallas_call(attend_kernel, out_shape=(jax.ShapeDtypeStruct((PEERS, ROW...]
    convert_element_type x3 -> x5, other arithmetic: 2.85 us -> 4.99 us  [the longest x1 2.03 us: sums(): total = (at(part, c, 2).astype(F32) + arrived.astype(F32)).astype(BF16)]
  transfers between devices with their start and end apart: 33 -> 35, of which waited for: 11 -> 14; matrix products, arithmetic and copies ran while one was open for 11% -> 13% of each run, Pallas kernels for 24% -> 18%
where the time goes in v5:
time: 176 us; the launch traced here: 174 us
  starting transfers between devices  70 us (40%)
  waiting for transfers between devices  44.4 us (25%)
  Pallas kernels  31.8 us (18%)
  other arithmetic  14.4 us (8%)
  local copies, waits for them, and re-layouts  6.32 us (4%)
  matrix products  6.17 us (4%)
    ppermute x24, starting transfers between devices, shift(): return lax.ppermute(value, 'ctx', pairs)  41.8 us
    ppermute x24, waiting for transfers between devices, shift(): return lax.ppermute(value, 'ctx', pairs)  32.4 us
    pallas_call x3, Pallas kernels, attend(): pl.pallas_call(attend_kernel, out_shape=(jax.ShapeDtypeStruct((PEERS, ROW...  20.2 us
    pallas_call x2, Pallas kernels, pack(): pl.pallas_call(pack_kernel, out_shape=jax.ShapeDtypeStruct((PEERS, *shape...  7.74 us
    ppermute x3, waiting for transfers between devices, half_sum(): lax.ppermute(jnp.where(mine, high, low), 'dp', [(d, d ^ bit) for d in ran...  7.46 us
    ppermute x3, starting transfers between devices, half_sum(): lax.ppermute(jnp.where(mine, high, low), 'dp', [(d, d ^ bit) for d in ran...  5.6 us
    all_to_all x1, starting transfers between devices, body(): back_near = swap(back_near)  4.58 us
    all_to_all x1, starting transfers between devices, body(): far = swap(far_packed)  4.48 us
  transfers between devices with their start and end apart: 35, of which 14 were waited for; matrix products, arithmetic and copies ran while one was open for 13% of the time, Pallas kernels for 18%

profile of v5, /device:TPU:2, one launch (start us, length us, event | category | flops | bytes accessed | tf_op | source)
XLA Modules:
  0.0 174.0 jit_solution(10722953896873647915)
XLA Ops:
  2.9 3.2 %collective-permute-start.1 = (bf16[16,1024]{1,0:T(8,128)(2,1)S(1)}, bf16[16,1024]{1,0:T(8,128)(2,1)S(1)}, u32[]{:S(2)}, u32[]{:S(2)}) collective-permute-start(bf16[16,1024]{1,0:T(8,128)(2,1)S(1)} %fusion.16), channel_id=1, source_target_pairs={{0,16},{1,17},{2,18},{3,19},{4,20},{5,21},{6,22},{7,23},{8,24},{9,... | collective-permute-start | bytes 98312 | tf_op jit(solution)/shard_map/ppermute | solution.py:37
  6.8 2.6 %collective-permute-start = (bf16[16,1024]{1,0:T(8,128)(2,1)S(1)}, bf16[16,1024]{1,0:T(8,128)(2,1)S(1)}, u32[]{:S(2)}, u32[]{:S(2)}) collective-permute-start(bf16[16,1024]{1,0:T(8,128)(2,1)S(1)} %fusion.16), channel_id=1, source_target_pairs={{0,24},{1,25},{2,26},{3,27},{4,28},{5,29},{6,30},{7,31},{8,0},{9,1... | collective-permute-start | bytes 98312 | tf_op jit(solution)/shard_map/ppermute | solution.py:37
  10.2 2.0 %collective-permute-start.3 = (bf16[1,128,512]{2,1,0:T(8,128)(2,1)S(1)}, bf16[1,128,512]{2,1,0:T(8,128)(2,1)S(1)}, u32[]{:S(2)}, u32[]{:S(2)}) collective-permute-start(bf16[1,128,512]{2,1,0:T(8,128)(2,1)S(1)} %maximum_bitcast_fusion), channel_id=1, source_target_pairs={{0,32},{32,0},{64,96},{96,64},{128,160},{160,128},{192,224},{224,1... | collective-permute-start | bytes 393224 | tf_op jit(solution)/shard_map/ppermute | solution.py:50
  12.2 3.9 %shard_map.102 = bf16[8,2,128,512]{3,2,1,0:T(8,128)(2,1)} custom-call(s32[1]{0:T(128)} %bitcast.z, bf16[128,8192]{1,0:T(8,128)(2,1)} %refs_2_.3, bf16[128,8192]{1,0:T(8,128)(2,1)} %refs_3_.3, bf16[128,8192]{1,0:T(8,128)(2,1)} %refs_2_.3, bf16[128,8192]{1,0:T(8,128)(2,1)} %refs_3_.3), custom_call_target="tpu_custom_call" | custom-call | bytes 4194304 | tf_op jit(solution)/shard_map/pallas_call | solution.py:126
  16.4 3.6 %all-to-all-start = ((bf16[8,2,128,512]{3,2,1,0:T(8,128)(2,1)}), bf16[8,2,128,512]{3,2,1,0:T(8,128)(2,1)S(1)}, u32[]{:S(2)}, u32[]{:S(2)}) async-start(bf16[8,2,128,512]{3,2,1,0:T(8,128)(2,1)} %shard_map.102), calls=%async_computation | async-start | bytes 4194304 | tf_op jit(solution)/shard_map/all_to_all | solution.py:267
  20.0 6.4 %collective-permute-start.5 = (bf16[4,16,1024]{2,1,0:T(8,128)(2,1)S(1)}, bf16[4,16,1024]{2,1,0:T(8,128)(2,1)S(1)}, u32[]{:S(2)}, u32[]{:S(2)}) collective-permute-start(bf16[4,16,1024]{2,1,0:T(8,128)(2,1)S(1)} %pad_maximum_fusion.6), channel_id=1, source_target_pairs={{0,4},{1,5},{2,6},{3,7},{4,0},{5,1},{6,2},{7,3},{8,12},{9,13},{10,... | collective-permute-start | bytes 393224 | tf_op jit(solution)/shard_map/ppermute | solution.py:37
  26.4 1.5 collective-permute-start.6
  27.9 2.7 %collective-permute-start.4 = (bf16[4,16,1024]{2,1,0:T(8,128)(2,1)S(1)}, bf16[4,16,1024]{2,1,0:T(8,128)(2,1)S(1)}, u32[]{:S(2)}, u32[]{:S(2)}) collective-permute-start(bf16[4,16,1024]{2,1,0:T(8,128)(2,1)S(1)} %pad_maximum_fusion.6), channel_id=1, source_target_pairs={{0,6},{1,7},{2,0},{3,1},{4,2},{5,3},{6,4},{7,5},{8,14},{9,15},{10,... | collective-permute-start | bytes 393224 | tf_op jit(solution)/shard_map/ppermute | solution.py:37
  30.5 2.1 %collective-permute-start.9 = (bf16[2,128,512]{2,1,0:T(8,128)(2,1)S(1)}, bf16[2,128,512]{2,1,0:T(8,128)(2,1)}, u32[]{:S(2)}, u32[]{:S(2)}) collective-permute-start(bf16[2,128,512]{2,1,0:T(8,128)(2,1)S(1)} %pad_maximum_fusion.5), channel_id=1, source_target_pairs={{0,128},{32,160},{64,192},{96,224},{128,0},{160,32},{192,64},{224,... | collective-permute-start | bytes 786440 | tf_op jit(solution)/shard_map/ppermute | solution.py:60
  33.4 1.3 collective-permute-start.8
  34.7 3.4 %collective-permute-done.6 = bf16[4,16,1024]{2,1,0:T(8,128)(2,1)S(1)} collective-permute-done((bf16[4,16,1024]{2,1,0:T(8,128)(2,1)S(1)}, bf16[4,16,1024]{2,1,0:T(8,128)(2,1)S(1)}, u32[]{:S(2)}, u32[]{:S(2)}) %collective-permute-start.6) | collective-permute-done | bytes 131104 | tf_op jit(solution)/shard_map/ppermute | solution.py:37
  38.1 1.2 collective-permute-done.4
  39.7 3.9 %shard_map.103 = bf16[8,2,128,512]{3,2,1,0:T(8,128)(2,1)} custom-call(s32[1]{0:T(128)} %bitcast.z, bf16[128,8192]{1,0:T(8,128)(2,1)} %refs_2_.3, bf16[128,8192]{1,0:T(8,128)(2,1)} %refs_3_.3, bf16[128,8192]{1,0:T(8,128)(2,1)} %refs_2_.3, bf16[128,8192]{1,0:T(8,128)(2,1)} %refs_3_.3), custom_call_target="tpu_custom_call" | custom-call | bytes 4194304 | tf_op jit(solution)/shard_map/pallas_call | solution.py:126
  43.5 2.0 %collective-permute-done.10 = bf16[2,128,512]{2,1,0:T(8,128)(2,1)} collective-permute-done((bf16[2,128,512]{2,1,0:T(8,128)(2,1)S(1)}, bf16[2,128,512]{2,1,0:T(8,128)(2,1)}, u32[]{:S(2)}, u32[]{:S(2)}) %collective-permute-start.10) | collective-permute-done | bytes 262176 | tf_op jit(solution)/shard_map/ppermute | solution.py:60
  49.2 2.0 %convolution_convert_fusion.2 = bf16[384,512]{1,0:T(8,128)(2,1)S(1)} fusion(bf16[384,1024]{1,0:T(8,128)(2,1)} %reshape.59, bf16[1024,512]{1,0:T(8,128)(2,1)} %bitcast.152), kind=kOutput, calls=%fused_computation.2 | convolution fusion | flops 402849792 | bytes 2228224 | tf_op jit(solution)/shard_map/dot_general | solution.py:268
  51.2 4.5 %all-to-all-start.1 = ((bf16[8,2,128,512]{3,2,1,0:T(8,128)(2,1)}), bf16[8,2,128,512]{3,2,1,0:T(8,128)(2,1)}, u32[]{:S(2)}, u32[]{:S(2)}) async-start(bf16[8,2,128,512]{3,2,1,0:T(8,128)(2,1)} %shard_map.103), calls=%async_computation.1 | async-start | bytes 4194304 | tf_op jit(solution)/shard_map/all_to_all | solution.py:271
  55.7 1.7 collective-permute-start.11
  58.9 1.3 collective-permute-start.13
  61.2 15.5 %collective-permute-done.11 = bf16[384,512]{1,0:T(8,128)(2,1)} collective-permute-done((bf16[384,512]{1,0:T(8,128)(2,1)S(1)}, bf16[384,512]{1,0:T(8,128)(2,1)}, u32[]{:S(2)}, u32[]{:S(2)}) %collective-permute-start.11) | collective-permute-done | bytes 393248 | tf_op jit(solution)/shard_map/ppermute | solution.py:37
  76.7 1.7 slice_bitcast_fusion.2
  78.4 2.8 %collective-permute-start.12 = (bf16[384,256]{1,0:T(8,128)(2,1)}, bf16[384,256]{1,0:T(8,128)(2,1)S(1)}, u32[]{:S(2)}, u32[]{:S(2)}) collective-permute-start(bf16[384,256]{1,0:T(8,128)(2,1)} %get-tuple-element.99), channel_id=1, source_target_pairs={{0,6},{1,7},{2,0},{3,1},{4,2},{5,3},{6,4},{7,5},{8,14},{9,15},{10,... | collective-permute-start | bytes 589832 | tf_op jit(solution)/shard_map/ppermute | solution.py:37
  81.5 8.6 %shard_map.104 = (bf16[8,128,512]{2,1,0:T(8,128)(2,1)}, bf16[2,384,256]{2,1,0:T(8,128)(2,1)S(1)}, bf16[2,384,256]{2,1,0:T(8,128)(2,1)S(1)}) custom-call(s32[6]{0:T(128)S(1)} %pad_add_fusion.ends, bf16[8,2,128,512]{3,2,1,0:T(8,128)(2,1)S(1)} %all-to-all-done.rows, bf16[2,384,256]{2,1,0:T(8,128)(2,1)S(1)} %get-tuple-element.114.key, ...), custom_call_target="tpu_custom_call" | custom-call | flops 2013265920 | bytes 6291456 | tf_op jit(solution)/shard_map/pallas_call | solution.py:214
  90.2 4.6 %all-to-all-start.2 = ((bf16[8,128,512]{2,1,0:T(8,128)(2,1)}), bf16[8,128,512]{2,1,0:T(8,128)(2,1)}, u32[]{:S(2)}, u32[]{:S(2)}) async-start(bf16[8,128,512]{2,1,0:T(8,128)(2,1)} %get-tuple-element.67), calls=%async_computation.2 | async-start | bytes 2097152 | tf_op jit(solution)/shard_map/all_to_all | solution.py:296
  94.8 4.1 %collective-permute-start.17 = (bf16[384,256]{1,0:T(8,128)(2,1)S(1)}, bf16[384,256]{1,0:T(8,128)(2,1)S(1)}, u32[]{:S(2)}, u32[]{:S(2)}) collective-permute-start(bf16[384,256]{1,0:T(8,128)(2,1)S(1)} %slice_bitcast_fusion.5), channel_id=1, source_target_pairs={{0,6},{1,7},{2,0},{3,1},{4,2},{5,3},{6,4},{7,5},{8,14},{9,15},{10,... | collective-permute-start | bytes 589832 | tf_op jit(solution)/shard_map/ppermute | solution.py:37
  99.1 5.8 %shard_map.105 = (bf16[8,128,512]{2,1,0:T(8,128)(2,1)}, bf16[1,384,256]{2,1,0:T(8,128)(2,1)S(1)}, bf16[1,384,256]{2,1,0:T(8,128)(2,1)S(1)}) custom-call(s32[6]{0:T(128)S(1)} %pad_add_fusion.ends, bf16[8,2,128,512]{3,2,1,0:T(8,128)(2,1)} %all-to-all-done.1.rows, bf16[1,384,256]{2,1,0:T(8,128)(2,1)S(1)} %bitcast.139, bf16[1,384,256]{2,1,0:T(8,128)(2,1)S(1)} %bitcast.140), custom_call_target="tpu_custom_call" | custom-call | flops 1006632960 | bytes 6291456 | tf_op jit(solution)/shard_map/pallas_call | solution.py:214
  104.9 2.7 %collective-permute-start.15 = (bf16[384,256]{1,0:T(8,128)(2,1)S(1)}, bf16[384,256]{1,0:T(8,128)(2,1)S(1)}, u32[]{:S(2)}, u32[]{:S(2)}) collective-permute-start(bf16[384,256]{1,0:T(8,128)(2,1)S(1)} %bitcast.142), channel_id=1, source_target_pairs={{0,2},{1,3},{2,4},{3,5},{4,6},{5,7},{6,0},{7,1},{8,10},{9,11},{10,... | collective-permute-start | bytes 589832 | tf_op jit(solution)/shard_map/ppermute | solution.py:37
  107.6 1.4 collective-permute-start.16
  109.0 5.8 %shard_map.106 = (bf16[8,128,512]{2,1,0:T(8,128)(2,1)}, bf16[1,384,256]{2,1,0:T(8,128)(2,1)S(1)}, bf16[1,384,256]{2,1,0:T(8,128)(2,1)S(1)}) custom-call(s32[6]{0:T(128)S(1)} %pad_add_fusion.ends, bf16[8,2,128,512]{3,2,1,0:T(8,128)(2,1)} %all-to-all-done.1.rows, bf16[1,384,256]{2,1,0:T(8,128)(2,1)S(1)} %bitcast.138, ...), custom_call_target="tpu_custom_call", output_to_operand_aliasing={{0}: (4, {})} | custom-call | flops 1006632960 | bytes 6291456 | tf_op jit(solution)/shard_map/pallas_call | solution.py:214
  114.8 1.7 collective-permute-done.18
  116.6 3.4 %collective-permute-done.15 = bf16[384,256]{1,0:T(8,128)(2,1)S(1)} collective-permute-done((bf16[384,256]{1,0:T(8,128)(2,1)S(1)}, bf16[384,256]{1,0:T(8,128)(2,1)S(1)}, u32[]{:S(2)}, u32[]{:S(2)}) %collective-permute-start.15) | collective-permute-done | bytes 196640 | tf_op jit(solution)/shard_map/ppermute | solution.py:37
  121.2 2.0 %collective-permute-start.19 = (bf16[384,256]{1,0:T(8,128)(2,1)S(1)}, bf16[384,256]{1,0:T(8,128)(2,1)S(1)}, u32[]{:S(2)}, u32[]{:S(2)}) collective-permute-start(bf16[384,256]{1,0:T(8,128)(2,1)S(1)} %fusion.4), channel_id=1, source_target_pairs={{0,2},{1,3},{2,4},{3,5},{4,6},{5,7},{6,0},{7,1},{8,10},{9,11},{10,... | collective-permute-start | bytes 589832 | tf_op jit(solution)/shard_map/ppermute | solution.py:37
  123.2 4.4 %all-to-all-start.3 = ((bf16[8,128,512]{2,1,0:T(8,128)(2,1)}), bf16[8,128,512]{2,1,0:T(8,128)(2,1)S(1)}, u32[]{:S(2)}, u32[]{:S(2)}) async-start(bf16[8,128,512]{2,1,0:T(8,128)(2,1)} %get-tuple-element.75), calls=%async_computation.3 | async-start | bytes 2097152 | tf_op jit(solution)/shard_map/all_to_all | solution.py:311
  128.8 3.3 %collective-permute-done.19 = bf16[384,256]{1,0:T(8,128)(2,1)S(1)} collective-permute-done((bf16[384,256]{1,0:T(8,128)(2,1)S(1)}, bf16[384,256]{1,0:T(8,128)(2,1)S(1)}, u32[]{:S(2)}, u32[]{:S(2)}) %collective-permute-start.19) | collective-permute-done | bytes 196640 | tf_op jit(solution)/shard_map/ppermute | solution.py:37
  132.1 2.0 %convolution_convert_fusion.1 = bf16[384,1024]{1,0:T(8,128)(2,1)S(1)} fusion(bf16[1024,512]{1,0:T(8,128)(2,1)} %bitcast.153, bf16[384,256]{1,0:T(8,128)(2,1)S(1)} %bitcast.145, bf16[384,256]{1,0:T(8,128)(2,1)S(1)} %bitcast.143, bf16[384,256]{1,0:T(8,128)(2,1)} %collective-permute-done.18, bf16[384,256]{1,0:T(8,128)(2,1)S(1)} %collective-permute-done.17, ...), kind=kOutput, calls=%fused_computation.1 | convolution fusion | flops 405995520 | bytes 3014656 | tf_op jit(solution)/shard_map/dot_general | solution.py:313
  135.2 2.1 %convolution_convert_fusion = bf16[1024,512]{1,0:T(8,128)(2,1)S(1)} fusion(bf16[384,1024]{1,0:T(8,128)(2,1)} %reshape.59, bf16[384,256]{1,0:T(8,128)(2,1)S(1)} %bitcast.146, bf16[384,256]{1,0:T(8,128)(2,1)S(1)} %bitcast.144, bf16[384,256]{1,0:T(8,128)(2,1)} %collective-permute-done.18, bf16[384,256]{1,0:T(8,128)(2,1)} %copy-done.6, ...), kind=kOutput, calls=%fused_computation | convolution fusion | flops 406126592 | bytes 3014656 | tf_op jit(solution)/shard_map/dot_general | solution.py:98
  139.0 2.0 %fusion.1 = bf16[4,4,12,1024]{3,2,1,0:T(8,128)(2,1)} fusion(bf16[4,4,12,1024]{3,2,1,0:T(8,128)(2,1)} %collective-permute-done.21, bf16[4,4,2,12,1024]{4,3,2,1,0:T(8,128)(2,1)S(1)} %reshape.60, s32[]{:T(128)S(6)} %and.76), kind=kLoop, calls=%fused_computation.8 | loop fusion | flops 786432 | bytes 1179652 | tf_op jit(solution)/shard_map/convert_element_type | solution.py:97
  141.0 2.6 %all-to-all-done.3.refs_1_ = bf16[8,128,512]{2,1,0:T(8,128)(2,1)S(1)} async-done(((bf16[8,128,512]{2,1,0:T(8,128)(2,1)}), bf16[8,128,512]{2,1,0:T(8,128)(2,1)S(1)}, u32[]{:S(2)}, u32[]{:S(2)}) %all-to-all-start.3) | async-done | bytes 1048608 | tf_op jit(solution)/shard_map/all_to_all | solution.py:311
  143.6 1.4 dynamic-slice_bitcast_fusion.3
  145.0 1.2 collective-permute-start.24
  146.2 1.5 collective-permute-start.23
  147.7 5.1 %collective-permute-done.25 = bf16[2,2,128,512]{3,2,1,0:T(8,128)(2,1)} collective-permute-done((bf16[2,2,128,512]{3,2,1,0:T(8,128)(2,1)}, bf16[2,2,128,512]{3,2,1,0:T(8,128)(2,1)}, u32[]{:S(2)}, u32[]{:S(2)}) %collective-permute-start.25) | collective-permute-done | bytes 524320 | tf_op jit(solution)/shard_map/ppermute | solution.py:90
  152.8 1.2 fusion
  156.3 3.4 %collective-permute-start.29 = (bf16[2,128,512]{2,1,0:T(8,128)(2,1)S(1)}, bf16[2,128,512]{2,1,0:T(8,128)(2,1)S(1)}, u32[]{:S(2)}, u32[]{:S(2)}) collective-permute-start(bf16[2,128,512]{2,1,0:T(8,128)(2,1)S(1)} %select_bitcast_fusion.3), channel_id=1, source_target_pairs={{0,128},{32,160},{64,192},{96,224},{128,0},{160,32},{192,64},{224,... | collective-permute-start | bytes 786440 | tf_op jit(solution)/shard_map/ppermute | solution.py:90
  159.7 1.5 collective-permute-start.28
  161.2 3.0 %collective-permute-start.27 = (bf16[12,1024]{1,0:T(8,128)(2,1)S(1)}, bf16[12,1024]{1,0:T(8,128)(2,1)S(1)}, u32[]{:S(2)}, u32[]{:S(2)}) collective-permute-start(bf16[12,1024]{1,0:T(8,128)(2,1)S(1)} %get-tuple-element.109), channel_id=1, source_target_pairs={{0,4},{1,5},{2,6},{3,7},{4,0},{5,1},{6,2},{7,3},{8,12},{9,13},{10,... | collective-permute-start | bytes 73736 | tf_op jit(solution)/shard_map/ppermute | solution.py:37
  164.3 3.8 %shard_map.107 = bf16[128,8192]{1,0:T(8,128)(2,1)} custom-call(s32[1]{0:T(128)} %bitcast.z, bf16[8,128,512]{2,1,0:T(8,128)(2,1)} %all-to-all-done.2.refs_0_, bf16[8,128,512]{2,1,0:T(8,128)(2,1)} %copy-done), custom_call_target="tpu_custom_call" | custom-call | bytes 4194304 | tf_op jit(solution)/shard_map/pallas_call | solution.py:153
  168.2 1.4 collective-permute-start.30
  170.9 2.4 %collective-permute-done.30 = bf16[128,512]{1,0:T(8,128)(2,1)S(1)} collective-permute-done((bf16[128,512]{1,0:T(8,128)(2,1)S(1)}, bf16[128,512]{1,0:T(8,128)(2,1)S(1)}, u32[]{:S(2)}, u32[]{:S(2)}) %collective-permute-start.30) | collective-permute-done | bytes 131104 | tf_op jit(solution)/shard_map/ppermute | solution.py:90
  (96 shorter events, 21.1 us)
Async XLA Ops:
  2.9 13.3 %collective-permute-start.1 = (bf16[16,1024]{1,0:T(8,128)(2,1)S(1)}, bf16[16,1024]{1,0:T(8,128)(2,1)S(1)}, u32[]{:S(2)}, u32[]{:S(2)}) collective-permute-start(bf16[16,1024]{1,0:T(8,128)(2,1)S(1)} %fusion.16), channel_id=1, source_target_pairs={{0,16},{1,17},{2,18},{3,19},{4,20},{5,21},{6,22},{7,23},{8,24},{9,... | collective-permute-start | bytes 98312 | tf_op jit(solution)/shard_map/ppermute | solution.py:37
  6.1 10.0 %collective-permute-start.2 = (bf16[16,1024]{1,0:T(8,128)(2,1)S(1)}, bf16[16,1024]{1,0:T(8,128)(2,1)S(1)}, u32[]{:S(2)}, u32[]{:S(2)}) collective-permute-start(bf16[16,1024]{1,0:T(8,128)(2,1)S(1)} %fusion.16), channel_id=1, source_target_pairs={{0,8},{1,9},{2,10},{3,11},{4,12},{5,13},{6,14},{7,15},{8,16},{9,17... | collective-permute-start | bytes 98312 | tf_op jit(solution)/shard_map/ppermute | solution.py:37
  6.8 9.4 %collective-permute-start = (bf16[16,1024]{1,0:T(8,128)(2,1)S(1)}, bf16[16,1024]{1,0:T(8,128)(2,1)S(1)}, u32[]{:S(2)}, u32[]{:S(2)}) collective-permute-start(bf16[16,1024]{1,0:T(8,128)(2,1)S(1)} %fusion.16), channel_id=1, source_target_pairs={{0,24},{1,25},{2,26},{3,27},{4,28},{5,29},{6,30},{7,31},{8,0},{9,1... | collective-permute-start | bytes 98312 | tf_op jit(solution)/shard_map/ppermute | solution.py:37
  10.2 6.1 %collective-permute-start.3 = (bf16[1,128,512]{2,1,0:T(8,128)(2,1)S(1)}, bf16[1,128,512]{2,1,0:T(8,128)(2,1)S(1)}, u32[]{:S(2)}, u32[]{:S(2)}) collective-permute-start(bf16[1,128,512]{2,1,0:T(8,128)(2,1)S(1)} %maximum_bitcast_fusion), channel_id=1, source_target_pairs={{0,32},{32,0},{64,96},{96,64},{128,160},{160,128},{192,224},{224,1... | collective-permute-start | bytes 393224 | tf_op jit(solution)/shard_map/ppermute | solution.py:50
  12.2 3.9 %copy-start.5 = (bf16[12,1024]{1,0:T(8,128)(2,1)S(1)}, bf16[12,1024]{1,0:T(8,128)(2,1)}, u32[]{:S(2)}) copy-start(bf16[12,1024]{1,0:T(8,128)(2,1)} %param.9) | copy-start | bytes 73732
  12.2 4.1 %copy-start.3 = (bf16[128,256]{1,0:T(8,128)(2,1)S(1)}, bf16[128,256]{1,0:T(8,128)(2,1)}, u32[]{:S(2)}) copy-start(bf16[128,256]{1,0:T(8,128)(2,1)} %param.11) | copy-start | bytes 196612
  12.2 4.1 %copy-start.4 = (bf16[128,256]{1,0:T(8,128)(2,1)S(1)}, bf16[128,256]{1,0:T(8,128)(2,1)}, u32[]{:S(2)}) copy-start(bf16[128,256]{1,0:T(8,128)(2,1)} %param.10) | copy-start | bytes 196612
  16.4 34.8 %all-to-all-start = ((bf16[8,2,128,512]{3,2,1,0:T(8,128)(2,1)}), bf16[8,2,128,512]{3,2,1,0:T(8,128)(2,1)S(1)}, u32[]{:S(2)}, u32[]{:S(2)}) async-start(bf16[8,2,128,512]{3,2,1,0:T(8,128)(2,1)} %shard_map.102), calls=%async_computation | async-start | bytes 4194304 | tf_op jit(solution)/shard_map/all_to_all | solution.py:267
  20.0 13.4 %collective-permute-start.5 = (bf16[4,16,1024]{2,1,0:T(8,128)(2,1)S(1)}, bf16[4,16,1024]{2,1,0:T(8,128)(2,1)S(1)}, u32[]{:S(2)}, u32[]{:S(2)}) collective-permute-start(bf16[4,16,1024]{2,1,0:T(8,128)(2,1)S(1)} %pad_maximum_fusion.6), channel_id=1, source_target_pairs={{0,4},{1,5},{2,6},{3,7},{4,0},{5,1},{6,2},{7,3},{8,12},{9,13},{10,... | collective-permute-start | bytes 393224 | tf_op jit(solution)/shard_map/ppermute | solution.py:37
  26.4 11.7 %collective-permute-start.6 = (bf16[4,16,1024]{2,1,0:T(8,128)(2,1)S(1)}, bf16[4,16,1024]{2,1,0:T(8,128)(2,1)S(1)}, u32[]{:S(2)}, u32[]{:S(2)}) collective-permute-start(bf16[4,16,1024]{2,1,0:T(8,128)(2,1)S(1)} %pad_maximum_fusion.6), channel_id=1, source_target_pairs={{0,2},{1,3},{2,4},{3,5},{4,6},{5,7},{6,0},{7,1},{8,10},{9,11},{10,... | collective-permute-start | bytes 393224 | tf_op jit(solution)/shard_map/ppermute | solution.py:37
  27.9 11.5 %collective-permute-start.4 = (bf16[4,16,1024]{2,1,0:T(8,128)(2,1)S(1)}, bf16[4,16,1024]{2,1,0:T(8,128)(2,1)S(1)}, u32[]{:S(2)}, u32[]{:S(2)}) collective-permute-start(bf16[4,16,1024]{2,1,0:T(8,128)(2,1)S(1)} %pad_maximum_fusion.6), channel_id=1, source_target_pairs={{0,6},{1,7},{2,0},{3,1},{4,2},{5,3},{6,4},{7,5},{8,14},{9,15},{10,... | collective-permute-start | bytes 393224 | tf_op jit(solution)/shard_map/ppermute | solution.py:37
  30.5 13.0 %collective-permute-start.9 = (bf16[2,128,512]{2,1,0:T(8,128)(2,1)S(1)}, bf16[2,128,512]{2,1,0:T(8,128)(2,1)}, u32[]{:S(2)}, u32[]{:S(2)}) collective-permute-start(bf16[2,128,512]{2,1,0:T(8,128)(2,1)S(1)} %pad_maximum_fusion.5), channel_id=1, source_target_pairs={{0,128},{32,160},{64,192},{96,224},{128,0},{160,32},{192,64},{224,... | collective-permute-start | bytes 786440 | tf_op jit(solution)/shard_map/ppermute | solution.py:60
  32.7 12.9 %collective-permute-start.10 = (bf16[2,128,512]{2,1,0:T(8,128)(2,1)S(1)}, bf16[2,128,512]{2,1,0:T(8,128)(2,1)}, u32[]{:S(2)}, u32[]{:S(2)}) collective-permute-start(bf16[2,128,512]{2,1,0:T(8,128)(2,1)S(1)} %pad_maximum_fusion.5), channel_id=1, source_target_pairs={{0,64},{32,96},{64,128},{96,160},{128,192},{160,224},{192,0},{224,... | collective-permute-start | bytes 786440 | tf_op jit(solution)/shard_map/ppermute | solution.py:60
  33.4 12.1 %collective-permute-start.8 = (bf16[2,128,512]{2,1,0:T(8,128)(2,1)S(1)}, bf16[2,128,512]{2,1,0:T(8,128)(2,1)}, u32[]{:S(2)}, u32[]{:S(2)}) collective-permute-start(bf16[2,128,512]{2,1,0:T(8,128)(2,1)S(1)} %pad_maximum_fusion.5), channel_id=1, source_target_pairs={{0,192},{32,224},{64,0},{96,32},{128,64},{160,96},{192,128},{224,1... | collective-permute-start | bytes 786440 | tf_op jit(solution)/shard_map/ppermute | solution.py:60
  39.5 8.4 %collective-permute-start.7 = (bf16[4,4,16,1024]{3,2,0,1:T(8,128)(2,1)S(1)}, bf16[4,4,16,1024]{3,2,0,1:T(8,128)(2,1)S(1)}, u32[]{:S(2)}, u32[]{:S(2)}) collective-permute-start(bf16[4,4,16,1024]{3,2,0,1:T(8,128)(2,1)S(1)} %pad_maximum_fusion.2), channel_id=1, source_target_pairs={{0,1},{1,0},{2,3},{3,2},{4,5},{5,4},{6,7},{7,6},{8,9},{9,8},{10,11... | collective-permute-start | bytes 1572872 | tf_op jit(solution)/shard_map/ppermute | solution.py:37
  51.2 7.7 %copy-start.1 = (bf16[384,512]{1,0:T(8,128)(2,1)}, bf16[384,512]{1,0:T(8,128)(2,1)S(1)}, u32[]{:S(2)}) copy-start(bf16[384,512]{1,0:T(8,128)(2,1)S(1)} %convolution_convert_fusion.2) | copy-start | bytes 1179652
  51.2 39.0 %all-to-all-start.1 = ((bf16[8,2,128,512]{3,2,1,0:T(8,128)(2,1)}), bf16[8,2,128,512]{3,2,1,0:T(8,128)(2,1)}, u32[]{:S(2)}, u32[]{:S(2)}) async-start(bf16[8,2,128,512]{3,2,1,0:T(8,128)(2,1)} %shard_map.103), calls=%async_computation.1 | async-start | bytes 4194304 | tf_op jit(solution)/shard_map/all_to_all | solution.py:271
  55.7 21.0 %collective-permute-start.11 = (bf16[384,512]{1,0:T(8,128)(2,1)S(1)}, bf16[384,512]{1,0:T(8,128)(2,1)}, u32[]{:S(2)}, u32[]{:S(2)}) collective-permute-start(bf16[384,512]{1,0:T(8,128)(2,1)S(1)} %convolution_convert_fusion.2), channel_id=1, source_target_pairs={{0,6},{1,7},{2,0},{3,1},{4,2},{5,3},{6,4},{7,5},{8,14},{9,15},{10,... | collective-permute-start | bytes 1179656 | tf_op jit(solution)/shard_map/ppermute | solution.py:37
  58.9 22.3 %collective-permute-start.13 = (bf16[384,512]{1,0:T(8,128)(2,1)S(1)}, bf16[384,512]{1,0:T(8,128)(2,1)S(1)}, u32[]{:S(2)}, u32[]{:S(2)}) collective-permute-start(bf16[384,512]{1,0:T(8,128)(2,1)S(1)} %convolution_convert_fusion.2), channel_id=1, source_target_pairs={{0,2},{1,3},{2,4},{3,5},{4,6},{5,7},{6,0},{7,1},{8,10},{9,11},{10,... | collective-permute-start | bytes 1179656 | tf_op jit(solution)/shard_map/ppermute | solution.py:37
  78.4 16.4 %collective-permute-start.12 = (bf16[384,256]{1,0:T(8,128)(2,1)}, bf16[384,256]{1,0:T(8,128)(2,1)S(1)}, u32[]{:S(2)}, u32[]{:S(2)}) collective-permute-start(bf16[384,256]{1,0:T(8,128)(2,1)} %get-tuple-element.99), channel_id=1, source_target_pairs={{0,6},{1,7},{2,0},{3,1},{4,2},{5,3},{6,4},{7,5},{8,14},{9,15},{10,... | collective-permute-start | bytes 589832 | tf_op jit(solution)/shard_map/ppermute | solution.py:37
  81.3 13.5 %collective-permute-start.14 = (bf16[384,256]{1,0:T(8,128)(2,1)S(1)}, bf16[384,256]{1,0:T(8,128)(2,1)S(1)}, u32[]{:S(2)}, u32[]{:S(2)}) collective-permute-start(bf16[384,256]{1,0:T(8,128)(2,1)S(1)} %get-tuple-element.102), channel_id=1, source_target_pairs={{0,2},{1,3},{2,4},{3,5},{4,6},{5,7},{6,0},{7,1},{8,10},{9,11},{10,... | collective-permute-start | bytes 589832 | tf_op jit(solution)/shard_map/ppermute | solution.py:37
  90.2 4.6 %copy-start.2 = (bf16[384,512]{1,0:T(8,128)(2,1)S(1)}, bf16[384,512]{1,0:T(8,128)(2,1)}, u32[]{:S(2)}) copy-start(bf16[384,512]{1,0:T(8,128)(2,1)} %copy-done.1) | copy-start | bytes 1179652
  90.2 26.4 %all-to-all-start.2 = ((bf16[8,128,512]{2,1,0:T(8,128)(2,1)}), bf16[8,128,512]{2,1,0:T(8,128)(2,1)}, u32[]{:S(2)}, u32[]{:S(2)}) async-start(bf16[8,128,512]{2,1,0:T(8,128)(2,1)} %get-tuple-element.67), calls=%async_computation.2 | async-start | bytes 2097152 | tf_op jit(solution)/shard_map/all_to_all | solution.py:296
  94.8 20.0 %collective-permute-start.17 = (bf16[384,256]{1,0:T(8,128)(2,1)S(1)}, bf16[384,256]{1,0:T(8,128)(2,1)S(1)}, u32[]{:S(2)}, u32[]{:S(2)}) collective-permute-start(bf16[384,256]{1,0:T(8,128)(2,1)S(1)} %slice_bitcast_fusion.5), channel_id=1, source_target_pairs={{0,6},{1,7},{2,0},{3,1},{4,2},{5,3},{6,4},{7,5},{8,14},{9,15},{10,... | collective-permute-start | bytes 589832 | tf_op jit(solution)/shard_map/ppermute | solution.py:37
  99.0 17.6 %collective-permute-start.18 = (bf16[384,256]{1,0:T(8,128)(2,1)S(1)}, bf16[384,256]{1,0:T(8,128)(2,1)}, u32[]{:S(2)}, u32[]{:S(2)}) collective-permute-start(bf16[384,256]{1,0:T(8,128)(2,1)S(1)} %slice_bitcast_fusion.4), channel_id=1, source_target_pairs={{0,2},{1,3},{2,4},{3,5},{4,6},{5,7},{6,0},{7,1},{8,10},{9,11},{10,... | collective-permute-start | bytes 589832 | tf_op jit(solution)/shard_map/ppermute | solution.py:37
  104.9 15.1 %collective-permute-start.15 = (bf16[384,256]{1,0:T(8,128)(2,1)S(1)}, bf16[384,256]{1,0:T(8,128)(2,1)S(1)}, u32[]{:S(2)}, u32[]{:S(2)}) collective-permute-start(bf16[384,256]{1,0:T(8,128)(2,1)S(1)} %bitcast.142), channel_id=1, source_target_pairs={{0,2},{1,3},{2,4},{3,5},{4,6},{5,7},{6,0},{7,1},{8,10},{9,11},{10,... | collective-permute-start | bytes 589832 | tf_op jit(solution)/shard_map/ppermute | solution.py:37
  107.6 12.4 %collective-permute-start.16 = (bf16[384,256]{1,0:T(8,128)(2,1)S(1)}, bf16[384,256]{1,0:T(8,128)(2,1)S(1)}, u32[]{:S(2)}, u32[]{:S(2)}) collective-permute-start(bf16[384,256]{1,0:T(8,128)(2,1)S(1)} %bitcast.141), channel_id=1, source_target_pairs={{0,6},{1,7},{2,0},{3,1},{4,2},{5,3},{6,4},{7,5},{8,14},{9,15},{10,... | collective-permute-start | bytes 589832 | tf_op jit(solution)/shard_map/ppermute | solution.py:37
  114.8 17.3 %copy-start.6 = (bf16[384,256]{1,0:T(8,128)(2,1)}, bf16[384,256]{1,0:T(8,128)(2,1)S(1)}, u32[]{:S(2)}) copy-start(bf16[384,256]{1,0:T(8,128)(2,1)S(1)} %collective-permute-done.17) | copy-start | bytes 589828
  120.0 8.7 %collective-permute-start.20 = (bf16[384,256]{1,0:T(8,128)(2,1)S(1)}, bf16[384,256]{1,0:T(8,128)(2,1)S(1)}, u32[]{:S(2)}, u32[]{:S(2)}) collective-permute-start(bf16[384,256]{1,0:T(8,128)(2,1)S(1)} %fusion.3), channel_id=1, source_target_pairs={{0,6},{1,7},{2,0},{3,1},{4,2},{5,3},{6,4},{7,5},{8,14},{9,15},{10,... | collective-permute-start | bytes 589832 | tf_op jit(solution)/shard_map/ppermute | solution.py:37
  121.2 10.9 %collective-permute-start.19 = (bf16[384,256]{1,0:T(8,128)(2,1)S(1)}, bf16[384,256]{1,0:T(8,128)(2,1)S(1)}, u32[]{:S(2)}, u32[]{:S(2)}) collective-permute-start(bf16[384,256]{1,0:T(8,128)(2,1)S(1)} %fusion.4), channel_id=1, source_target_pairs={{0,2},{1,3},{2,4},{3,5},{4,6},{5,7},{6,0},{7,1},{8,10},{9,11},{10,... | collective-permute-start | bytes 589832 | tf_op jit(solution)/shard_map/ppermute | solution.py:37
  123.2 20.4 %all-to-all-start.3 = ((bf16[8,128,512]{2,1,0:T(8,128)(2,1)}), bf16[8,128,512]{2,1,0:T(8,128)(2,1)S(1)}, u32[]{:S(2)}, u32[]{:S(2)}) async-start(bf16[8,128,512]{2,1,0:T(8,128)(2,1)} %get-tuple-element.75), calls=%async_computation.3 | async-start | bytes 2097152 | tf_op jit(solution)/shard_map/all_to_all | solution.py:311
  128.8 3.4 %copy-start.7 = (bf16[384,256]{1,0:T(8,128)(2,1)}, bf16[384,256]{1,0:T(8,128)(2,1)S(1)}, u32[]{:S(2)}) copy-start(bf16[384,256]{1,0:T(8,128)(2,1)S(1)} %collective-permute-done.20) | copy-start | bytes 589828
  132.1 2.2 %copy-start.8 = (bf16[384,256]{1,0:T(8,128)(2,1)}, bf16[384,256]{1,0:T(8,128)(2,1)S(1)}, u32[]{:S(2)}) copy-start(bf16[384,256]{1,0:T(8,128)(2,1)S(1)} %collective-permute-done.19) | copy-start | bytes 589828
  135.2 3.8 %collective-permute-start.21 = (bf16[4,4,12,1024]{3,2,1,0:T(8,128)(2,1)}, bf16[4,4,12,1024]{3,2,1,0:T(8,128)(2,1)}, u32[]{:S(2)}, u32[]{:S(2)}) collective-permute-start(bf16[4,4,12,1024]{3,2,1,0:T(8,128)(2,1)} %dynamic-slice_bitcast_fusion), channel_id=1, source_target_pairs={{0,1},{1,0},{2,3},{3,2},{4,5},{5,4},{6,7},{7,6},{8,9},{9,8},{10,11... | collective-permute-start | bytes 1179656 | tf_op jit(solution)/shard_map/ppermute | solution.py:37
  138.2 14.7 %collective-permute-start.25 = (bf16[2,2,128,512]{3,2,1,0:T(8,128)(2,1)}, bf16[2,2,128,512]{3,2,1,0:T(8,128)(2,1)}, u32[]{:S(2)}, u32[]{:S(2)}) collective-permute-start(bf16[2,2,128,512]{3,2,1,0:T(8,128)(2,1)} %select_bitcast_fusion), channel_id=1, source_target_pairs={{0,64},{32,96},{64,0},{96,32},{128,192},{160,224},{192,128},{224,1... | collective-permute-start | bytes 1572872 | tf_op jit(solution)/shard_map/ppermute | solution.py:90
  143.6 12.8 %copy-start = (bf16[8,128,512]{2,1,0:T(8,128)(2,1)}, bf16[8,128,512]{2,1,0:T(8,128)(2,1)S(1)}, u32[]{:S(2)}) copy-start(bf16[8,128,512]{2,1,0:T(8,128)(2,1)S(1)} %all-to-all-done.3.refs_1_) | copy-start | bytes 3145732
  145.0 9.1 %collective-permute-start.24 = (bf16[4,12,1024]{2,1,0:T(8,128)(2,1)S(1)}, bf16[4,12,1024]{2,1,0:T(8,128)(2,1)S(1)}, u32[]{:S(2)}, u32[]{:S(2)}) collective-permute-start(bf16[4,12,1024]{2,1,0:T(8,128)(2,1)S(1)} %get-tuple-element.89), channel_id=1, source_target_pairs={{0,24},{1,25},{2,26},{3,27},{4,28},{5,29},{6,30},{7,31},{8,0},{9,1... | collective-permute-start | bytes 294920 | tf_op jit(solution)/shard_map/ppermute | solution.py:37
  146.2 7.8 %collective-permute-start.23 = (bf16[4,12,1024]{2,1,0:T(8,128)(2,1)S(1)}, bf16[4,12,1024]{2,1,0:T(8,128)(2,1)S(1)}, u32[]{:S(2)}, u32[]{:S(2)}) collective-permute-start(bf16[4,12,1024]{2,1,0:T(8,128)(2,1)S(1)} %get-tuple-element.90), channel_id=1, source_target_pairs={{0,16},{1,17},{2,18},{3,19},{4,20},{5,21},{6,22},{7,23},{8,24},{9,... | collective-permute-start | bytes 294920 | tf_op jit(solution)/shard_map/ppermute | solution.py:37
  147.7 7.6 %collective-permute-start.22 = (bf16[4,12,1024]{2,1,0:T(8,128)(2,1)S(1)}, bf16[4,12,1024]{2,1,0:T(8,128)(2,1)S(1)}, u32[]{:S(2)}, u32[]{:S(2)}) collective-permute-start(bf16[4,12,1024]{2,1,0:T(8,128)(2,1)S(1)} %get-tuple-element.88), channel_id=1, source_target_pairs={{0,8},{1,9},{2,10},{3,11},{4,12},{5,13},{6,14},{7,15},{8,16},{9,17... | collective-permute-start | bytes 294920 | tf_op jit(solution)/shard_map/ppermute | solution.py:37
  156.3 11.7 %collective-permute-start.29 = (bf16[2,128,512]{2,1,0:T(8,128)(2,1)S(1)}, bf16[2,128,512]{2,1,0:T(8,128)(2,1)S(1)}, u32[]{:S(2)}, u32[]{:S(2)}) collective-permute-start(bf16[2,128,512]{2,1,0:T(8,128)(2,1)S(1)} %select_bitcast_fusion.3), channel_id=1, source_target_pairs={{0,128},{32,160},{64,192},{96,224},{128,0},{160,32},{192,64},{224,... | collective-permute-start | bytes 786440 | tf_op jit(solution)/shard_map/ppermute | solution.py:90
  159.7 9.9 %collective-permute-start.28 = (bf16[12,1024]{1,0:T(8,128)(2,1)S(1)}, bf16[12,1024]{1,0:T(8,128)(2,1)S(1)}, u32[]{:S(2)}, u32[]{:S(2)}) collective-permute-start(bf16[12,1024]{1,0:T(8,128)(2,1)S(1)} %get-tuple-element.108), channel_id=1, source_target_pairs={{0,6},{1,7},{2,0},{3,1},{4,2},{5,3},{6,4},{7,5},{8,14},{9,15},{10,... | collective-permute-start | bytes 73736 | tf_op jit(solution)/shard_map/ppermute | solution.py:37
  161.2 8.4 %collective-permute-start.27 = (bf16[12,1024]{1,0:T(8,128)(2,1)S(1)}, bf16[12,1024]{1,0:T(8,128)(2,1)S(1)}, u32[]{:S(2)}, u32[]{:S(2)}) collective-permute-start(bf16[12,1024]{1,0:T(8,128)(2,1)S(1)} %get-tuple-element.109), channel_id=1, source_target_pairs={{0,4},{1,5},{2,6},{3,7},{4,0},{5,1},{6,2},{7,3},{8,12},{9,13},{10,... | collective-permute-start | bytes 73736 | tf_op jit(solution)/shard_map/ppermute | solution.py:37
  164.3 6.0 %collective-permute-start.26 = (bf16[12,1024]{1,0:T(8,128)(2,1)S(1)}, bf16[12,1024]{1,0:T(8,128)(2,1)S(1)}, u32[]{:S(2)}, u32[]{:S(2)}) collective-permute-start(bf16[12,1024]{1,0:T(8,128)(2,1)S(1)} %get-tuple-element.107), channel_id=1, source_target_pairs={{0,2},{1,3},{2,4},{3,5},{4,6},{5,7},{6,0},{7,1},{8,10},{9,11},{10,... | collective-permute-start | bytes 73736 | tf_op jit(solution)/shard_map/ppermute | solution.py:37
  168.2 5.1 %collective-permute-start.30 = (bf16[128,512]{1,0:T(8,128)(2,1)S(1)}, bf16[128,512]{1,0:T(8,128)(2,1)S(1)}, u32[]{:S(2)}, u32[]{:S(2)}) collective-permute-start(bf16[128,512]{1,0:T(8,128)(2,1)S(1)} %select_bitcast_fusion.8), channel_id=1, source_target_pairs={{0,32},{32,0},{64,96},{96,64},{128,160},{160,128},{192,224},{224,1... | collective-permute-start | bytes 393224 | tf_op jit(solution)/shard_map/ppermute | solution.py:90

commit v6 on v5

--- a/solution.py
+++ b/solution.py
@@ -267,7 +267,7 @@
     near = swap(near_packed)
     own = jnp.dot(encoder, weight, preferred_element_type=F32).astype(BF16)
     far_packed = pack(GROUPS[1], z_later, queries, out_grad)
-    far_packed, near, own = lax.optimization_barrier((far_packed, near, own))
+    far_packed, near = lax.optimization_barrier((far_packed, near))
     far = swap(far_packed)
 
     own_key, own_value = own[:, :FEATURES], own[:, FEATURES:]

time: 176 us -> 182 us (1.034)
  starting transfers between devices: 70 us -> 77.6 us
  waiting for transfers between devices: 44.4 us -> 40.7 us
    ppermute x24, starting transfers between devices: 41.8 us -> 50.5 us  [shift(): return lax.ppermute(value, 'ctx', pairs)]
    ppermute x3, starting transfers between devices: 5.6 us -> 2.79 us  [half_sum(): lax.ppermute(jnp.where(mine, high, low), 'dp', [(d, d ^ bit) for d in ran...]
    all_to_all x1, waiting for transfers between devices: 2.56 us -> 0.01 us  [body(): back_far = swap(back)]
    ppermute x24, waiting for transfers between devices: 32.4 us -> 30.1 us  [shift(): return lax.ppermute(value, 'ctx', pairs)]
  transfers between devices with their start and end apart: 35 -> 35, of which waited for: 14 -> 12; matrix products, arithmetic and copies ran while one was open for 13% -> 14% of each run, Pallas kernels for 18% -> 18%
where the time goes in v6:
time: 182 us; the launch traced here: 180 us
  starting transfers between devices  77.6 us (43%)
  waiting for transfers between devices  40.7 us (22%)
  Pallas kernels  31.8 us (17%)
  other arithmetic  14.4 us (8%)
  local copies, waits for them, and re-layouts  8.02 us (4%)
  matrix products  6.18 us (3%)
    ppermute x24, starting transfers between devices, shift(): return lax.ppermute(value, 'ctx', pairs)  50.5 us
    ppermute x24, waiting for transfers between devices, shift(): return lax.ppermute(value, 'ctx', pairs)  30.1 us
    pallas_call x3, Pallas kernels, attend(): pl.pallas_call(attend_kernel, out_shape=(jax.ShapeDtypeStruct((PEERS, ROW...  20.3 us
    ppermute x3, waiting for transfers between devices, half_sum(): lax.ppermute(jnp.where(mine, high, low), 'dp', [(d, d ^ bit) for d in ran...  8.65 us
    pallas_call x2, Pallas kernels, pack(): pl.pallas_call(pack_kernel, out_shape=jax.ShapeDtypeStruct((PEERS, *shape...  7.74 us
    all_to_all x1, starting transfers between devices, body(): back_near = swap(back_near)  6.4 us
    all_to_all x1, starting transfers between devices, body(): far = swap(far_packed)  4.47 us
    all_to_all x1, starting transfers between devices, body(): back_far = swap(back)  4.45 us
  transfers between devices with their start and end apart: 35, of which 12 were waited for; matrix products, arithmetic and copies ran while one was open for 14% of the time, Pallas kernels for 18%

profile of v6, /device:TPU:2, one launch (start us, length us, event | category | flops | bytes accessed | tf_op | source)
XLA Modules:
  0.0 179.8 jit_solution(11966757226210686718)
XLA Ops:
  2.9 3.2 %collective-permute-start.1 = (bf16[16,1024]{1,0:T(8,128)(2,1)S(1)}, bf16[16,1024]{1,0:T(8,128)(2,1)S(1)}, u32[]{:S(2)}, u32[]{:S(2)}) collective-permute-start(bf16[16,1024]{1,0:T(8,128)(2,1)S(1)} %fusion.16), channel_id=1, source_target_pairs={{0,16},{1,17},{2,18},{3,19},{4,20},{5,21},{6,22},{7,23},{8,24},{9,... | collective-permute-start | bytes 98312 | tf_op jit(solution)/shard_map/ppermute | solution.py:37
  6.8 2.6 %collective-permute-start = (bf16[16,1024]{1,0:T(8,128)(2,1)S(1)}, bf16[16,1024]{1,0:T(8,128)(2,1)S(1)}, u32[]{:S(2)}, u32[]{:S(2)}) collective-permute-start(bf16[16,1024]{1,0:T(8,128)(2,1)S(1)} %fusion.16), channel_id=1, source_target_pairs={{0,24},{1,25},{2,26},{3,27},{4,28},{5,29},{6,30},{7,31},{8,0},{9,1... | collective-permute-start | bytes 98312 | tf_op jit(solution)/shard_map/ppermute | solution.py:37
  10.2 2.0 %collective-permute-start.3 = (bf16[1,128,512]{2,1,0:T(8,128)(2,1)S(1)}, bf16[1,128,512]{2,1,0:T(8,128)(2,1)S(1)}, u32[]{:S(2)}, u32[]{:S(2)}) collective-permute-start(bf16[1,128,512]{2,1,0:T(8,128)(2,1)S(1)} %maximum_bitcast_fusion), channel_id=1, source_target_pairs={{0,32},{32,0},{64,96},{96,64},{128,160},{160,128},{192,224},{224,1... | collective-permute-start | bytes 393224 | tf_op jit(solution)/shard_map/ppermute | solution.py:50
  12.2 3.9 %shard_map.102 = bf16[8,2,128,512]{3,2,1,0:T(8,128)(2,1)} custom-call(s32[1]{0:T(128)} %bitcast.z, bf16[128,8192]{1,0:T(8,128)(2,1)} %refs_2_.3, bf16[128,8192]{1,0:T(8,128)(2,1)} %refs_3_.3, bf16[128,8192]{1,0:T(8,128)(2,1)} %refs_2_.3, bf16[128,8192]{1,0:T(8,128)(2,1)} %refs_3_.3), custom_call_target="tpu_custom_call" | custom-call | bytes 4194304 | tf_op jit(solution)/shard_map/pallas_call | solution.py:126
  16.4 3.6 %all-to-all-start = ((bf16[8,2,128,512]{3,2,1,0:T(8,128)(2,1)}), bf16[8,2,128,512]{3,2,1,0:T(8,128)(2,1)S(1)}, u32[]{:S(2)}, u32[]{:S(2)}) async-start(bf16[8,2,128,512]{3,2,1,0:T(8,128)(2,1)} %shard_map.102), calls=%async_computation | async-start | bytes 4194304 | tf_op jit(solution)/shard_map/all_to_all | solution.py:267
  20.0 6.4 %collective-permute-start.5 = (bf16[4,16,1024]{2,1,0:T(8,128)(2,1)S(1)}, bf16[4,16,1024]{2,1,0:T(8,128)(2,1)S(1)}, u32[]{:S(2)}, u32[]{:S(2)}) collective-permute-start(bf16[4,16,1024]{2,1,0:T(8,128)(2,1)S(1)} %pad_maximum_fusion.6), channel_id=1, source_target_pairs={{0,4},{1,5},{2,6},{3,7},{4,0},{5,1},{6,2},{7,3},{8,12},{9,13},{10,... | collective-permute-start | bytes 393224 | tf_op jit(solution)/shard_map/ppermute | solution.py:37
  26.4 1.5 collective-permute-start.6
  27.9 2.7 %collective-permute-start.4 = (bf16[4,16,1024]{2,1,0:T(8,128)(2,1)S(1)}, bf16[4,16,1024]{2,1,0:T(8,128)(2,1)S(1)}, u32[]{:S(2)}, u32[]{:S(2)}) collective-permute-start(bf16[4,16,1024]{2,1,0:T(8,128)(2,1)S(1)} %pad_maximum_fusion.6), channel_id=1, source_target_pairs={{0,6},{1,7},{2,0},{3,1},{4,2},{5,3},{6,4},{7,5},{8,14},{9,15},{10,... | collective-permute-start | bytes 393224 | tf_op jit(solution)/shard_map/ppermute | solution.py:37
  30.5 2.1 %collective-permute-start.9 = (bf16[2,128,512]{2,1,0:T(8,128)(2,1)S(1)}, bf16[2,128,512]{2,1,0:T(8,128)(2,1)}, u32[]{:S(2)}, u32[]{:S(2)}) collective-permute-start(bf16[2,128,512]{2,1,0:T(8,128)(2,1)S(1)} %pad_maximum_fusion.5), channel_id=1, source_target_pairs={{0,128},{32,160},{64,192},{96,224},{128,0},{160,32},{192,64},{224,... | collective-permute-start | bytes 786440 | tf_op jit(solution)/shard_map/ppermute | solution.py:60
  33.4 1.3 collective-permute-start.8
  34.7 3.4 %collective-permute-done.6 = bf16[4,16,1024]{2,1,0:T(8,128)(2,1)S(1)} collective-permute-done((bf16[4,16,1024]{2,1,0:T(8,128)(2,1)S(1)}, bf16[4,16,1024]{2,1,0:T(8,128)(2,1)S(1)}, u32[]{:S(2)}, u32[]{:S(2)}) %collective-permute-start.6) | collective-permute-done | bytes 131104 | tf_op jit(solution)/shard_map/ppermute | solution.py:37
  38.1 1.2 collective-permute-done.4
  39.7 3.9 %shard_map.103 = bf16[8,2,128,512]{3,2,1,0:T(8,128)(2,1)} custom-call(s32[1]{0:T(128)} %bitcast.z, bf16[128,8192]{1,0:T(8,128)(2,1)} %refs_2_.3, bf16[128,8192]{1,0:T(8,128)(2,1)} %refs_3_.3, bf16[128,8192]{1,0:T(8,128)(2,1)} %refs_2_.3, bf16[128,8192]{1,0:T(8,128)(2,1)} %refs_3_.3), custom_call_target="tpu_custom_call" | custom-call | bytes 4194304 | tf_op jit(solution)/shard_map/pallas_call | solution.py:126
  43.5 2.0 %collective-permute-done.10 = bf16[2,128,512]{2,1,0:T(8,128)(2,1)} collective-permute-done((bf16[2,128,512]{2,1,0:T(8,128)(2,1)S(1)}, bf16[2,128,512]{2,1,0:T(8,128)(2,1)}, u32[]{:S(2)}, u32[]{:S(2)}) %collective-permute-start.10) | collective-permute-done | bytes 262176 | tf_op jit(solution)/shard_map/ppermute | solution.py:60
  45.5 1.2 select_bitcast_fusion.7
  46.8 1.1 pad_maximum_fusion.1
  47.9 4.5 %all-to-all-start.1 = ((bf16[8,2,128,512]{3,2,1,0:T(8,128)(2,1)}), bf16[8,2,128,512]{3,2,1,0:T(8,128)(2,1)}, u32[]{:S(2)}, u32[]{:S(2)}) async-start(bf16[8,2,128,512]{3,2,1,0:T(8,128)(2,1)} %shard_map.103), calls=%async_computation.1 | async-start | bytes 4194304 | tf_op jit(solution)/shard_map/all_to_all | solution.py:271
  53.6 2.0 %convolution_convert_fusion.2 = bf16[384,512]{1,0:T(8,128)(2,1)S(1)} fusion(bf16[384,1024]{1,0:T(8,128)(2,1)} %reshape.59, bf16[1024,512]{1,0:T(8,128)(2,1)} %bitcast.152), kind=kOutput, calls=%fused_computation.2 | convolution fusion | flops 402849792 | bytes 2228224 | tf_op jit(solution)/shard_map/dot_general | solution.py:268
  55.7 4.6 %collective-permute-start.11 = (bf16[384,512]{1,0:T(8,128)(2,1)S(1)}, bf16[384,512]{1,0:T(8,128)(2,1)}, u32[]{:S(2)}, u32[]{:S(2)}) collective-permute-start(bf16[384,512]{1,0:T(8,128)(2,1)S(1)} %convolution_convert_fusion.2), channel_id=1, source_target_pairs={{0,6},{1,7},{2,0},{3,1},{4,2},{5,3},{6,4},{7,5},{8,14},{9,15},{10,... | collective-permute-start | bytes 1179656 | tf_op jit(solution)/shard_map/ppermute | solution.py:37
  62.9 13.9 %collective-permute-done.11 = bf16[384,512]{1,0:T(8,128)(2,1)} collective-permute-done((bf16[384,512]{1,0:T(8,128)(2,1)S(1)}, bf16[384,512]{1,0:T(8,128)(2,1)}, u32[]{:S(2)}, u32[]{:S(2)}) %collective-permute-start.11) | collective-permute-done | bytes 393248 | tf_op jit(solution)/shard_map/ppermute | solution.py:37
  76.8 1.7 slice_bitcast_fusion.2
  78.5 3.7 %collective-permute-start.12 = (bf16[384,256]{1,0:T(8,128)(2,1)}, bf16[384,256]{1,0:T(8,128)(2,1)S(1)}, u32[]{:S(2)}, u32[]{:S(2)}) collective-permute-start(bf16[384,256]{1,0:T(8,128)(2,1)} %get-tuple-element.97), channel_id=1, source_target_pairs={{0,6},{1,7},{2,0},{3,1},{4,2},{5,3},{6,4},{7,5},{8,14},{9,15},{10,... | collective-permute-start | bytes 589832 | tf_op jit(solution)/shard_map/ppermute | solution.py:37
  82.2 1.7 slice_bitcast_fusion.6
  84.0 8.6 %shard_map.104 = (bf16[8,128,512]{2,1,0:T(8,128)(2,1)}, bf16[2,384,256]{2,1,0:T(8,128)(2,1)S(1)}, bf16[2,384,256]{2,1,0:T(8,128)(2,1)S(1)}) custom-call(s32[6]{0:T(128)S(1)} %pad_add_fusion.ends, bf16[8,2,128,512]{3,2,1,0:T(8,128)(2,1)S(1)} %all-to-all-done.rows, bf16[2,384,256]{2,1,0:T(8,128)(2,1)S(1)} %get-tuple-element.112.key, ...), custom_call_target="tpu_custom_call" | custom-call | flops 2013265920 | bytes 6291456 | tf_op jit(solution)/shard_map/pallas_call | solution.py:214
  92.7 6.4 %all-to-all-start.2 = ((bf16[8,128,512]{2,1,0:T(8,128)(2,1)}), bf16[8,128,512]{2,1,0:T(8,128)(2,1)}, u32[]{:S(2)}, u32[]{:S(2)}) async-start(bf16[8,128,512]{2,1,0:T(8,128)(2,1)} %get-tuple-element.65), calls=%async_computation.2 | async-start | bytes 2097152 | tf_op jit(solution)/shard_map/all_to_all | solution.py:296
  99.2 4.2 %collective-permute-start.17 = (bf16[384,256]{1,0:T(8,128)(2,1)S(1)}, bf16[384,256]{1,0:T(8,128)(2,1)S(1)}, u32[]{:S(2)}, u32[]{:S(2)}) collective-permute-start(bf16[384,256]{1,0:T(8,128)(2,1)S(1)} %slice_bitcast_fusion.5), channel_id=1, source_target_pairs={{0,6},{1,7},{2,0},{3,1},{4,2},{5,3},{6,4},{7,5},{8,14},{9,15},{10,... | collective-permute-start | bytes 589832 | tf_op jit(solution)/shard_map/ppermute | solution.py:37
  103.5 5.8 %shard_map.105 = (bf16[8,128,512]{2,1,0:T(8,128)(2,1)}, bf16[1,384,256]{2,1,0:T(8,128)(2,1)S(1)}, bf16[1,384,256]{2,1,0:T(8,128)(2,1)S(1)}) custom-call(s32[6]{0:T(128)S(1)} %pad_add_fusion.ends, bf16[8,2,128,512]{3,2,1,0:T(8,128)(2,1)} %all-to-all-done.1.rows, bf16[1,384,256]{2,1,0:T(8,128)(2,1)S(1)} %bitcast.139, bf16[1,384,256]{2,1,0:T(8,128)(2,1)S(1)} %bitcast.140), custom_call_target="tpu_custom_call" | custom-call | flops 1006632960 | bytes 6291456 | tf_op jit(solution)/shard_map/pallas_call | solution.py:214
  109.3 2.0 %collective-permute-start.15 = (bf16[384,256]{1,0:T(8,128)(2,1)S(1)}, bf16[384,256]{1,0:T(8,128)(2,1)S(1)}, u32[]{:S(2)}, u32[]{:S(2)}) collective-permute-start(bf16[384,256]{1,0:T(8,128)(2,1)S(1)} %bitcast.142), channel_id=1, source_target_pairs={{0,2},{1,3},{2,4},{3,5},{4,6},{5,7},{6,0},{7,1},{8,10},{9,11},{10,... | collective-permute-start | bytes 589832 | tf_op jit(solution)/shard_map/ppermute | solution.py:37
  111.3 2.2 %collective-permute-start.16 = (bf16[384,256]{1,0:T(8,128)(2,1)S(1)}, bf16[384,256]{1,0:T(8,128)(2,1)S(1)}, u32[]{:S(2)}, u32[]{:S(2)}) collective-permute-start(bf16[384,256]{1,0:T(8,128)(2,1)S(1)} %bitcast.141), channel_id=1, source_target_pairs={{0,6},{1,7},{2,0},{3,1},{4,2},{5,3},{6,4},{7,5},{8,14},{9,15},{10,... | collective-permute-start | bytes 589832 | tf_op jit(solution)/shard_map/ppermute | solution.py:37
  113.5 5.8 %shard_map.106 = (bf16[8,128,512]{2,1,0:T(8,128)(2,1)}, bf16[1,384,256]{2,1,0:T(8,128)(2,1)S(1)}, bf16[1,384,256]{2,1,0:T(8,128)(2,1)S(1)}) custom-call(s32[6]{0:T(128)S(1)} %pad_add_fusion.ends, bf16[8,2,128,512]{3,2,1,0:T(8,128)(2,1)} %all-to-all-done.1.rows, bf16[1,384,256]{2,1,0:T(8,128)(2,1)S(1)} %bitcast.138, ...), custom_call_target="tpu_custom_call", output_to_operand_aliasing={{0}: (4, {})} | custom-call | flops 1006632960 | bytes 6291456 | tf_op jit(solution)/shard_map/pallas_call | solution.py:214
  119.3 2.3 %collective-permute-done.15 = bf16[384,256]{1,0:T(8,128)(2,1)S(1)} collective-permute-done((bf16[384,256]{1,0:T(8,128)(2,1)S(1)}, bf16[384,256]{1,0:T(8,128)(2,1)S(1)}, u32[]{:S(2)}, u32[]{:S(2)}) %collective-permute-start.15) | collective-permute-done | bytes 196640 | tf_op jit(solution)/shard_map/ppermute | solution.py:37
  122.0 3.7 %collective-permute-start.20 = (bf16[384,256]{1,0:T(8,128)(2,1)S(1)}, bf16[384,256]{1,0:T(8,128)(2,1)S(1)}, u32[]{:S(2)}, u32[]{:S(2)}) collective-permute-start(bf16[384,256]{1,0:T(8,128)(2,1)S(1)} %fusion.3), channel_id=1, source_target_pairs={{0,6},{1,7},{2,0},{3,1},{4,2},{5,3},{6,4},{7,5},{8,14},{9,15},{10,... | collective-permute-start | bytes 589832 | tf_op jit(solution)/shard_map/ppermute | solution.py:37
  125.8 4.4 %all-to-all-start.3 = ((bf16[8,128,512]{2,1,0:T(8,128)(2,1)}), bf16[8,128,512]{2,1,0:T(8,128)(2,1)S(1)}, u32[]{:S(2)}, u32[]{:S(2)}) async-start(bf16[8,128,512]{2,1,0:T(8,128)(2,1)} %get-tuple-element.73), calls=%async_computation.3 | async-start | bytes 2097152 | tf_op jit(solution)/shard_map/all_to_all | solution.py:311
  130.2 4.6 %collective-permute-done.20 = bf16[384,256]{1,0:T(8,128)(2,1)S(1)} collective-permute-done((bf16[384,256]{1,0:T(8,128)(2,1)S(1)}, bf16[384,256]{1,0:T(8,128)(2,1)S(1)}, u32[]{:S(2)}, u32[]{:S(2)}) %collective-permute-start.20) | collective-permute-done | bytes 196640 | tf_op jit(solution)/shard_map/ppermute | solution.py:37
  134.8 2.8 %collective-permute-done.19 = bf16[384,256]{1,0:T(8,128)(2,1)S(1)} collective-permute-done((bf16[384,256]{1,0:T(8,128)(2,1)S(1)}, bf16[384,256]{1,0:T(8,128)(2,1)S(1)}, u32[]{:S(2)}, u32[]{:S(2)}) %collective-permute-start.19) | collective-permute-done | bytes 196640 | tf_op jit(solution)/shard_map/ppermute | solution.py:37
  137.6 2.0 %convolution_convert_fusion.1 = bf16[384,1024]{1,0:T(8,128)(2,1)S(1)} fusion(bf16[1024,512]{1,0:T(8,128)(2,1)} %bitcast.153, bf16[384,256]{1,0:T(8,128)(2,1)S(1)} %bitcast.145, bf16[384,256]{1,0:T(8,128)(2,1)S(1)} %bitcast.143, bf16[384,256]{1,0:T(8,128)(2,1)} %collective-permute-done.18, bf16[384,256]{1,0:T(8,128)(2,1)S(1)} %collective-permute-done.17, ...), kind=kOutput, calls=%fused_computation.1 | convolution fusion | flops 405995520 | bytes 3014656 | tf_op jit(solution)/shard_map/dot_general | solution.py:313
  140.7 2.1 %convolution_convert_fusion = bf16[1024,512]{1,0:T(8,128)(2,1)S(1)} fusion(bf16[384,1024]{1,0:T(8,128)(2,1)} %reshape.59, bf16[384,256]{1,0:T(8,128)(2,1)S(1)} %bitcast.146, bf16[384,256]{1,0:T(8,128)(2,1)S(1)} %bitcast.144, bf16[384,256]{1,0:T(8,128)(2,1)} %collective-permute-done.18, bf16[384,256]{1,0:T(8,128)(2,1)} %copy-done.6, ...), kind=kOutput, calls=%fused_computation | convolution fusion | flops 406126592 | bytes 3014656 | tf_op jit(solution)/shard_map/dot_general | solution.py:98
  144.2 2.0 %fusion.1 = bf16[4,4,12,1024]{3,2,1,0:T(8,128)(2,1)} fusion(bf16[4,4,12,1024]{3,2,1,0:T(8,128)(2,1)} %collective-permute-done.21, bf16[4,4,2,12,1024]{4,3,2,1,0:T(8,128)(2,1)S(1)} %reshape.60, s32[]{:T(128)S(6)} %and.76), kind=kLoop, calls=%fused_computation.8 | loop fusion | flops 786432 | bytes 1179652 | tf_op jit(solution)/shard_map/convert_element_type | solution.py:97
  146.3 1.4 dynamic-slice_bitcast_fusion.3
  147.7 2.9 %collective-permute-start.24 = (bf16[4,12,1024]{2,1,0:T(8,128)(2,1)S(1)}, bf16[4,12,1024]{2,1,0:T(8,128)(2,1)S(1)}, u32[]{:S(2)}, u32[]{:S(2)}) collective-permute-start(bf16[4,12,1024]{2,1,0:T(8,128)(2,1)S(1)} %get-tuple-element.87), channel_id=1, source_target_pairs={{0,24},{1,25},{2,26},{3,27},{4,28},{5,29},{6,30},{7,31},{8,0},{9,1... | collective-permute-start | bytes 294920 | tf_op jit(solution)/shard_map/ppermute | solution.py:37
  152.4 6.0 %collective-permute-done.25 = bf16[2,2,128,512]{3,2,1,0:T(8,128)(2,1)} collective-permute-done((bf16[2,2,128,512]{3,2,1,0:T(8,128)(2,1)}, bf16[2,2,128,512]{3,2,1,0:T(8,128)(2,1)}, u32[]{:S(2)}, u32[]{:S(2)}) %collective-permute-start.25) | collective-permute-done | bytes 524320 | tf_op jit(solution)/shard_map/ppermute | solution.py:90
  158.3 1.2 fusion
  161.9 1.8 %collective-permute-start.28 = (bf16[12,1024]{1,0:T(8,128)(2,1)S(1)}, bf16[12,1024]{1,0:T(8,128)(2,1)S(1)}, u32[]{:S(2)}, u32[]{:S(2)}) collective-permute-start(bf16[12,1024]{1,0:T(8,128)(2,1)S(1)} %get-tuple-element.106), channel_id=1, source_target_pairs={{0,6},{1,7},{2,0},{3,1},{4,2},{5,3},{6,4},{7,5},{8,14},{9,15},{10,... | collective-permute-start | bytes 73736 | tf_op jit(solution)/shard_map/ppermute | solution.py:37
  163.7 5.0 %collective-permute-start.27 = (bf16[12,1024]{1,0:T(8,128)(2,1)S(1)}, bf16[12,1024]{1,0:T(8,128)(2,1)S(1)}, u32[]{:S(2)}, u32[]{:S(2)}) collective-permute-start(bf16[12,1024]{1,0:T(8,128)(2,1)S(1)} %get-tuple-element.107), channel_id=1, source_target_pairs={{0,4},{1,5},{2,6},{3,7},{4,0},{5,1},{6,2},{7,3},{8,12},{9,13},{10,... | collective-permute-start | bytes 73736 | tf_op jit(solution)/shard_map/ppermute | solution.py:37
  168.7 1.2 collective-permute-start.26
  170.0 3.8 %shard_map.107 = bf16[128,8192]{1,0:T(8,128)(2,1)} custom-call(s32[1]{0:T(128)} %bitcast.z, bf16[8,128,512]{2,1,0:T(8,128)(2,1)} %all-to-all-done.2.refs_0_, bf16[8,128,512]{2,1,0:T(8,128)(2,1)} %copy-done), custom_call_target="tpu_custom_call" | custom-call | bytes 4194304 | tf_op jit(solution)/shard_map/pallas_call | solution.py:153
  173.9 1.7 collective-permute-start.30
  176.3 2.7 %collective-permute-done.30 = bf16[128,512]{1,0:T(8,128)(2,1)S(1)} collective-permute-done((bf16[128,512]{1,0:T(8,128)(2,1)S(1)}, bf16[128,512]{1,0:T(8,128)(2,1)S(1)}, u32[]{:S(2)}, u32[]{:S(2)}) %collective-permute-start.30) | collective-permute-done | bytes 131104 | tf_op jit(solution)/shard_map/ppermute | solution.py:90
  (96 shorter events, 17.6 us)
Async XLA Ops:
  2.9 13.3 %collective-permute-start.1 = (bf16[16,1024]{1,0:T(8,128)(2,1)S(1)}, bf16[16,1024]{1,0:T(8,128)(2,1)S(1)}, u32[]{:S(2)}, u32[]{:S(2)}) collective-permute-start(bf16[16,1024]{1,0:T(8,128)(2,1)S(1)} %fusion.16), channel_id=1, source_target_pairs={{0,16},{1,17},{2,18},{3,19},{4,20},{5,21},{6,22},{7,23},{8,24},{9,... | collective-permute-start | bytes 98312 | tf_op jit(solution)/shard_map/ppermute | solution.py:37
  6.1 10.0 %collective-permute-start.2 = (bf16[16,1024]{1,0:T(8,128)(2,1)S(1)}, bf16[16,1024]{1,0:T(8,128)(2,1)S(1)}, u32[]{:S(2)}, u32[]{:S(2)}) collective-permute-start(bf16[16,1024]{1,0:T(8,128)(2,1)S(1)} %fusion.16), channel_id=1, source_target_pairs={{0,8},{1,9},{2,10},{3,11},{4,12},{5,13},{6,14},{7,15},{8,16},{9,17... | collective-permute-start | bytes 98312 | tf_op jit(solution)/shard_map/ppermute | solution.py:37
  6.8 9.4 %collective-permute-start = (bf16[16,1024]{1,0:T(8,128)(2,1)S(1)}, bf16[16,1024]{1,0:T(8,128)(2,1)S(1)}, u32[]{:S(2)}, u32[]{:S(2)}) collective-permute-start(bf16[16,1024]{1,0:T(8,128)(2,1)S(1)} %fusion.16), channel_id=1, source_target_pairs={{0,24},{1,25},{2,26},{3,27},{4,28},{5,29},{6,30},{7,31},{8,0},{9,1... | collective-permute-start | bytes 98312 | tf_op jit(solution)/shard_map/ppermute | solution.py:37
  10.2 6.1 %collective-permute-start.3 = (bf16[1,128,512]{2,1,0:T(8,128)(2,1)S(1)}, bf16[1,128,512]{2,1,0:T(8,128)(2,1)S(1)}, u32[]{:S(2)}, u32[]{:S(2)}) collective-permute-start(bf16[1,128,512]{2,1,0:T(8,128)(2,1)S(1)} %maximum_bitcast_fusion), channel_id=1, source_target_pairs={{0,32},{32,0},{64,96},{96,64},{128,160},{160,128},{192,224},{224,1... | collective-permute-start | bytes 393224 | tf_op jit(solution)/shard_map/ppermute | solution.py:50
  12.2 3.9 %copy-start.5 = (bf16[12,1024]{1,0:T(8,128)(2,1)S(1)}, bf16[12,1024]{1,0:T(8,128)(2,1)}, u32[]{:S(2)}) copy-start(bf16[12,1024]{1,0:T(8,128)(2,1)} %param.9) | copy-start | bytes 73732
  12.2 4.1 %copy-start.3 = (bf16[128,256]{1,0:T(8,128)(2,1)S(1)}, bf16[128,256]{1,0:T(8,128)(2,1)}, u32[]{:S(2)}) copy-start(bf16[128,256]{1,0:T(8,128)(2,1)} %param.11) | copy-start | bytes 196612
  12.2 4.1 %copy-start.4 = (bf16[128,256]{1,0:T(8,128)(2,1)S(1)}, bf16[128,256]{1,0:T(8,128)(2,1)}, u32[]{:S(2)}) copy-start(bf16[128,256]{1,0:T(8,128)(2,1)} %param.10) | copy-start | bytes 196612
  16.4 31.5 %all-to-all-start = ((bf16[8,2,128,512]{3,2,1,0:T(8,128)(2,1)}), bf16[8,2,128,512]{3,2,1,0:T(8,128)(2,1)S(1)}, u32[]{:S(2)}, u32[]{:S(2)}) async-start(bf16[8,2,128,512]{3,2,1,0:T(8,128)(2,1)} %shard_map.102), calls=%async_computation | async-start | bytes 4194304 | tf_op jit(solution)/shard_map/all_to_all | solution.py:267
  20.0 13.4 %collective-permute-start.5 = (bf16[4,16,1024]{2,1,0:T(8,128)(2,1)S(1)}, bf16[4,16,1024]{2,1,0:T(8,128)(2,1)S(1)}, u32[]{:S(2)}, u32[]{:S(2)}) collective-permute-start(bf16[4,16,1024]{2,1,0:T(8,128)(2,1)S(1)} %pad_maximum_fusion.6), channel_id=1, source_target_pairs={{0,4},{1,5},{2,6},{3,7},{4,0},{5,1},{6,2},{7,3},{8,12},{9,13},{10,... | collective-permute-start | bytes 393224 | tf_op jit(solution)/shard_map/ppermute | solution.py:37
  26.4 11.7 %collective-permute-start.6 = (bf16[4,16,1024]{2,1,0:T(8,128)(2,1)S(1)}, bf16[4,16,1024]{2,1,0:T(8,128)(2,1)S(1)}, u32[]{:S(2)}, u32[]{:S(2)}) collective-permute-start(bf16[4,16,1024]{2,1,0:T(8,128)(2,1)S(1)} %pad_maximum_fusion.6), channel_id=1, source_target_pairs={{0,2},{1,3},{2,4},{3,5},{4,6},{5,7},{6,0},{7,1},{8,10},{9,11},{10,... | collective-permute-start | bytes 393224 | tf_op jit(solution)/shard_map/ppermute | solution.py:37
  27.9 11.5 %collective-permute-start.4 = (bf16[4,16,1024]{2,1,0:T(8,128)(2,1)S(1)}, bf16[4,16,1024]{2,1,0:T(8,128)(2,1)S(1)}, u32[]{:S(2)}, u32[]{:S(2)}) collective-permute-start(bf16[4,16,1024]{2,1,0:T(8,128)(2,1)S(1)} %pad_maximum_fusion.6), channel_id=1, source_target_pairs={{0,6},{1,7},{2,0},{3,1},{4,2},{5,3},{6,4},{7,5},{8,14},{9,15},{10,... | collective-permute-start | bytes 393224 | tf_op jit(solution)/shard_map/ppermute | solution.py:37
  30.5 13.0 %collective-permute-start.9 = (bf16[2,128,512]{2,1,0:T(8,128)(2,1)S(1)}, bf16[2,128,512]{2,1,0:T(8,128)(2,1)}, u32[]{:S(2)}, u32[]{:S(2)}) collective-permute-start(bf16[2,128,512]{2,1,0:T(8,128)(2,1)S(1)} %pad_maximum_fusion.5), channel_id=1, source_target_pairs={{0,128},{32,160},{64,192},{96,224},{128,0},{160,32},{192,64},{224,... | collective-permute-start | bytes 786440 | tf_op jit(solution)/shard_map/ppermute | solution.py:60
  32.7 12.9 %collective-permute-start.10 = (bf16[2,128,512]{2,1,0:T(8,128)(2,1)S(1)}, bf16[2,128,512]{2,1,0:T(8,128)(2,1)}, u32[]{:S(2)}, u32[]{:S(2)}) collective-permute-start(bf16[2,128,512]{2,1,0:T(8,128)(2,1)S(1)} %pad_maximum_fusion.5), channel_id=1, source_target_pairs={{0,64},{32,96},{64,128},{96,160},{128,192},{160,224},{192,0},{224,... | collective-permute-start | bytes 786440 | tf_op jit(solution)/shard_map/ppermute | solution.py:60
  33.4 12.1 %collective-permute-start.8 = (bf16[2,128,512]{2,1,0:T(8,128)(2,1)S(1)}, bf16[2,128,512]{2,1,0:T(8,128)(2,1)}, u32[]{:S(2)}, u32[]{:S(2)}) collective-permute-start(bf16[2,128,512]{2,1,0:T(8,128)(2,1)S(1)} %pad_maximum_fusion.5), channel_id=1, source_target_pairs={{0,192},{32,224},{64,0},{96,32},{128,64},{160,96},{192,128},{224,1... | collective-permute-start | bytes 786440 | tf_op jit(solution)/shard_map/ppermute | solution.py:60
  39.5 12.8 %collective-permute-start.7 = (bf16[4,4,16,1024]{3,2,0,1:T(8,128)(2,1)S(1)}, bf16[4,4,16,1024]{3,2,0,1:T(8,128)(2,1)S(1)}, u32[]{:S(2)}, u32[]{:S(2)}) collective-permute-start(bf16[4,4,16,1024]{3,2,0,1:T(8,128)(2,1)S(1)} %pad_maximum_fusion.2), channel_id=1, source_target_pairs={{0,1},{1,0},{2,3},{3,2},{4,5},{5,4},{6,7},{7,6},{8,9},{9,8},{10,11... | collective-permute-start | bytes 1572872 | tf_op jit(solution)/shard_map/ppermute | solution.py:37
  47.9 44.8 %all-to-all-start.1 = ((bf16[8,2,128,512]{3,2,1,0:T(8,128)(2,1)}), bf16[8,2,128,512]{3,2,1,0:T(8,128)(2,1)}, u32[]{:S(2)}, u32[]{:S(2)}) async-start(bf16[8,2,128,512]{3,2,1,0:T(8,128)(2,1)} %shard_map.103), calls=%async_computation.1 | async-start | bytes 4194304 | tf_op jit(solution)/shard_map/all_to_all | solution.py:271
  55.7 28.3 %copy-start.1 = (bf16[384,512]{1,0:T(8,128)(2,1)}, bf16[384,512]{1,0:T(8,128)(2,1)S(1)}, u32[]{:S(2)}) copy-start(bf16[384,512]{1,0:T(8,128)(2,1)S(1)} %convolution_convert_fusion.2) | copy-start | bytes 1179652
  55.7 21.1 %collective-permute-start.11 = (bf16[384,512]{1,0:T(8,128)(2,1)S(1)}, bf16[384,512]{1,0:T(8,128)(2,1)}, u32[]{:S(2)}, u32[]{:S(2)}) collective-permute-start(bf16[384,512]{1,0:T(8,128)(2,1)S(1)} %convolution_convert_fusion.2), channel_id=1, source_target_pairs={{0,6},{1,7},{2,0},{3,1},{4,2},{5,3},{6,4},{7,5},{8,14},{9,15},{10,... | collective-permute-start | bytes 1179656 | tf_op jit(solution)/shard_map/ppermute | solution.py:37
  60.9 21.4 %collective-permute-start.13 = (bf16[384,512]{1,0:T(8,128)(2,1)S(1)}, bf16[384,512]{1,0:T(8,128)(2,1)}, u32[]{:S(2)}, u32[]{:S(2)}) collective-permute-start(bf16[384,512]{1,0:T(8,128)(2,1)S(1)} %convolution_convert_fusion.2), channel_id=1, source_target_pairs={{0,2},{1,3},{2,4},{3,5},{4,6},{5,7},{6,0},{7,1},{8,10},{9,11},{10,... | collective-permute-start | bytes 1179656 | tf_op jit(solution)/shard_map/ppermute | solution.py:37
  78.5 20.6 %collective-permute-start.12 = (bf16[384,256]{1,0:T(8,128)(2,1)}, bf16[384,256]{1,0:T(8,128)(2,1)S(1)}, u32[]{:S(2)}, u32[]{:S(2)}) collective-permute-start(bf16[384,256]{1,0:T(8,128)(2,1)} %get-tuple-element.97), channel_id=1, source_target_pairs={{0,6},{1,7},{2,0},{3,1},{4,2},{5,3},{6,4},{7,5},{8,14},{9,15},{10,... | collective-permute-start | bytes 589832 | tf_op jit(solution)/shard_map/ppermute | solution.py:37
  84.0 15.2 %collective-permute-start.14 = (bf16[384,256]{1,0:T(8,128)(2,1)}, bf16[384,256]{1,0:T(8,128)(2,1)S(1)}, u32[]{:S(2)}, u32[]{:S(2)}) collective-permute-start(bf16[384,256]{1,0:T(8,128)(2,1)} %get-tuple-element.100), channel_id=1, source_target_pairs={{0,2},{1,3},{2,4},{3,5},{4,6},{5,7},{6,0},{7,1},{8,10},{9,11},{10,... | collective-permute-start | bytes 589832 | tf_op jit(solution)/shard_map/ppermute | solution.py:37
  92.7 6.4 %copy-start.2 = (bf16[384,512]{1,0:T(8,128)(2,1)S(1)}, bf16[384,512]{1,0:T(8,128)(2,1)}, u32[]{:S(2)}) copy-start(bf16[384,512]{1,0:T(8,128)(2,1)} %copy-done.1) | copy-start | bytes 1179652
  92.7 26.6 %all-to-all-start.2 = ((bf16[8,128,512]{2,1,0:T(8,128)(2,1)}), bf16[8,128,512]{2,1,0:T(8,128)(2,1)}, u32[]{:S(2)}, u32[]{:S(2)}) async-start(bf16[8,128,512]{2,1,0:T(8,128)(2,1)} %get-tuple-element.65), calls=%async_computation.2 | async-start | bytes 2097152 | tf_op jit(solution)/shard_map/all_to_all | solution.py:296
  99.2 20.1 %collective-permute-start.17 = (bf16[384,256]{1,0:T(8,128)(2,1)S(1)}, bf16[384,256]{1,0:T(8,128)(2,1)S(1)}, u32[]{:S(2)}, u32[]{:S(2)}) collective-permute-start(bf16[384,256]{1,0:T(8,128)(2,1)S(1)} %slice_bitcast_fusion.5), channel_id=1, source_target_pairs={{0,6},{1,7},{2,0},{3,1},{4,2},{5,3},{6,4},{7,5},{8,14},{9,15},{10,... | collective-permute-start | bytes 589832 | tf_op jit(solution)/shard_map/ppermute | solution.py:37
  103.4 15.9 %collective-permute-start.18 = (bf16[384,256]{1,0:T(8,128)(2,1)S(1)}, bf16[384,256]{1,0:T(8,128)(2,1)}, u32[]{:S(2)}, u32[]{:S(2)}) collective-permute-start(bf16[384,256]{1,0:T(8,128)(2,1)S(1)} %slice_bitcast_fusion.4), channel_id=1, source_target_pairs={{0,2},{1,3},{2,4},{3,5},{4,6},{5,7},{6,0},{7,1},{8,10},{9,11},{10,... | collective-permute-start | bytes 589832 | tf_op jit(solution)/shard_map/ppermute | solution.py:37
  109.3 12.2 %collective-permute-start.15 = (bf16[384,256]{1,0:T(8,128)(2,1)S(1)}, bf16[384,256]{1,0:T(8,128)(2,1)S(1)}, u32[]{:S(2)}, u32[]{:S(2)}) collective-permute-start(bf16[384,256]{1,0:T(8,128)(2,1)S(1)} %bitcast.142), channel_id=1, source_target_pairs={{0,2},{1,3},{2,4},{3,5},{4,6},{5,7},{6,0},{7,1},{8,10},{9,11},{10,... | collective-permute-start | bytes 589832 | tf_op jit(solution)/shard_map/ppermute | solution.py:37
  111.3 10.6 %collective-permute-start.16 = (bf16[384,256]{1,0:T(8,128)(2,1)S(1)}, bf16[384,256]{1,0:T(8,128)(2,1)S(1)}, u32[]{:S(2)}, u32[]{:S(2)}) collective-permute-start(bf16[384,256]{1,0:T(8,128)(2,1)S(1)} %bitcast.141), channel_id=1, source_target_pairs={{0,6},{1,7},{2,0},{3,1},{4,2},{5,3},{6,4},{7,5},{8,14},{9,15},{10,... | collective-permute-start | bytes 589832 | tf_op jit(solution)/shard_map/ppermute | solution.py:37
  119.3 18.4 %copy-start.6 = (bf16[384,256]{1,0:T(8,128)(2,1)}, bf16[384,256]{1,0:T(8,128)(2,1)S(1)}, u32[]{:S(2)}) copy-start(bf16[384,256]{1,0:T(8,128)(2,1)S(1)} %collective-permute-done.17) | copy-start | bytes 589828
  122.0 12.8 %collective-permute-start.20 = (bf16[384,256]{1,0:T(8,128)(2,1)S(1)}, bf16[384,256]{1,0:T(8,128)(2,1)S(1)}, u32[]{:S(2)}, u32[]{:S(2)}) collective-permute-start(bf16[384,256]{1,0:T(8,128)(2,1)S(1)} %fusion.3), channel_id=1, source_target_pairs={{0,6},{1,7},{2,0},{3,1},{4,2},{5,3},{6,4},{7,5},{8,14},{9,15},{10,... | collective-permute-start | bytes 589832 | tf_op jit(solution)/shard_map/ppermute | solution.py:37
  125.7 11.9 %collective-permute-start.19 = (bf16[384,256]{1,0:T(8,128)(2,1)S(1)}, bf16[384,256]{1,0:T(8,128)(2,1)S(1)}, u32[]{:S(2)}, u32[]{:S(2)}) collective-permute-start(bf16[384,256]{1,0:T(8,128)(2,1)S(1)} %fusion.4), channel_id=1, source_target_pairs={{0,2},{1,3},{2,4},{3,5},{4,6},{5,7},{6,0},{7,1},{8,10},{9,11},{10,... | collective-permute-start | bytes 589832 | tf_op jit(solution)/shard_map/ppermute | solution.py:37
  125.8 20.5 %all-to-all-start.3 = ((bf16[8,128,512]{2,1,0:T(8,128)(2,1)}), bf16[8,128,512]{2,1,0:T(8,128)(2,1)S(1)}, u32[]{:S(2)}, u32[]{:S(2)}) async-start(bf16[8,128,512]{2,1,0:T(8,128)(2,1)} %get-tuple-element.73), calls=%async_computation.3 | async-start | bytes 2097152 | tf_op jit(solution)/shard_map/all_to_all | solution.py:311
  134.8 2.8 %copy-start.7 = (bf16[384,256]{1,0:T(8,128)(2,1)}, bf16[384,256]{1,0:T(8,128)(2,1)S(1)}, u32[]{:S(2)}) copy-start(bf16[384,256]{1,0:T(8,128)(2,1)S(1)} %collective-permute-done.20) | copy-start | bytes 589828
  137.6 2.2 %copy-start.8 = (bf16[384,256]{1,0:T(8,128)(2,1)}, bf16[384,256]{1,0:T(8,128)(2,1)S(1)}, u32[]{:S(2)}) copy-start(bf16[384,256]{1,0:T(8,128)(2,1)S(1)} %collective-permute-done.19) | copy-start | bytes 589828
  140.7 3.5 %collective-permute-start.21 = (bf16[4,4,12,1024]{3,2,1,0:T(8,128)(2,1)}, bf16[4,4,12,1024]{3,2,1,0:T(8,128)(2,1)}, u32[]{:S(2)}, u32[]{:S(2)}) collective-permute-start(bf16[4,4,12,1024]{3,2,1,0:T(8,128)(2,1)} %dynamic-slice_bitcast_fusion), channel_id=1, source_target_pairs={{0,1},{1,0},{2,3},{3,2},{4,5},{5,4},{6,7},{7,6},{8,9},{9,8},{10,11... | collective-permute-start | bytes 1179656 | tf_op jit(solution)/shard_map/ppermute | solution.py:37
  143.7 14.6 %collective-permute-start.25 = (bf16[2,2,128,512]{3,2,1,0:T(8,128)(2,1)}, bf16[2,2,128,512]{3,2,1,0:T(8,128)(2,1)}, u32[]{:S(2)}, u32[]{:S(2)}) collective-permute-start(bf16[2,2,128,512]{3,2,1,0:T(8,128)(2,1)} %select_bitcast_fusion), channel_id=1, source_target_pairs={{0,64},{32,96},{64,0},{96,32},{128,192},{160,224},{192,128},{224,1... | collective-permute-start | bytes 1572872 | tf_op jit(solution)/shard_map/ppermute | solution.py:90
  146.3 15.1 %copy-start = (bf16[8,128,512]{2,1,0:T(8,128)(2,1)}, bf16[8,128,512]{2,1,0:T(8,128)(2,1)S(1)}, u32[]{:S(2)}) copy-start(bf16[8,128,512]{2,1,0:T(8,128)(2,1)S(1)} %all-to-all-done.3.refs_1_) | copy-start | bytes 3145732
  147.7 11.9 %collective-permute-start.24 = (bf16[4,12,1024]{2,1,0:T(8,128)(2,1)S(1)}, bf16[4,12,1024]{2,1,0:T(8,128)(2,1)S(1)}, u32[]{:S(2)}, u32[]{:S(2)}) collective-permute-start(bf16[4,12,1024]{2,1,0:T(8,128)(2,1)S(1)} %get-tuple-element.87), channel_id=1, source_target_pairs={{0,24},{1,25},{2,26},{3,27},{4,28},{5,29},{6,30},{7,31},{8,0},{9,1... | collective-permute-start | bytes 294920 | tf_op jit(solution)/shard_map/ppermute | solution.py:37
  150.6 9.0 %collective-permute-start.23 = (bf16[4,12,1024]{2,1,0:T(8,128)(2,1)S(1)}, bf16[4,12,1024]{2,1,0:T(8,128)(2,1)S(1)}, u32[]{:S(2)}, u32[]{:S(2)}) collective-permute-start(bf16[4,12,1024]{2,1,0:T(8,128)(2,1)S(1)} %get-tuple-element.88), channel_id=1, source_target_pairs={{0,16},{1,17},{2,18},{3,19},{4,20},{5,21},{6,22},{7,23},{8,24},{9,... | collective-permute-start | bytes 294920 | tf_op jit(solution)/shard_map/ppermute | solution.py:37
  151.5 8.8 %collective-permute-start.22 = (bf16[4,12,1024]{2,1,0:T(8,128)(2,1)S(1)}, bf16[4,12,1024]{2,1,0:T(8,128)(2,1)S(1)}, u32[]{:S(2)}, u32[]{:S(2)}) collective-permute-start(bf16[4,12,1024]{2,1,0:T(8,128)(2,1)S(1)} %get-tuple-element.86), channel_id=1, source_target_pairs={{0,8},{1,9},{2,10},{3,11},{4,12},{5,13},{6,14},{7,15},{8,16},{9,17... | collective-permute-start | bytes 294920 | tf_op jit(solution)/shard_map/ppermute | solution.py:37
  161.3 12.5 %collective-permute-start.29 = (bf16[2,128,512]{2,1,0:T(8,128)(2,1)S(1)}, bf16[2,128,512]{2,1,0:T(8,128)(2,1)S(1)}, u32[]{:S(2)}, u32[]{:S(2)}) collective-permute-start(bf16[2,128,512]{2,1,0:T(8,128)(2,1)S(1)} %select_bitcast_fusion.3), channel_id=1, source_target_pairs={{0,128},{32,160},{64,192},{96,224},{128,0},{160,32},{192,64},{224,... | collective-permute-start | bytes 786440 | tf_op jit(solution)/shard_map/ppermute | solution.py:90
  161.9 13.8 %collective-permute-start.28 = (bf16[12,1024]{1,0:T(8,128)(2,1)S(1)}, bf16[12,1024]{1,0:T(8,128)(2,1)S(1)}, u32[]{:S(2)}, u32[]{:S(2)}) collective-permute-start(bf16[12,1024]{1,0:T(8,128)(2,1)S(1)} %get-tuple-element.106), channel_id=1, source_target_pairs={{0,6},{1,7},{2,0},{3,1},{4,2},{5,3},{6,4},{7,5},{8,14},{9,15},{10,... | collective-permute-start | bytes 73736 | tf_op jit(solution)/shard_map/ppermute | solution.py:37
  163.7 12.0 %collective-permute-start.27 = (bf16[12,1024]{1,0:T(8,128)(2,1)S(1)}, bf16[12,1024]{1,0:T(8,128)(2,1)S(1)}, u32[]{:S(2)}, u32[]{:S(2)}) collective-permute-start(bf16[12,1024]{1,0:T(8,128)(2,1)S(1)} %get-tuple-element.107), channel_id=1, source_target_pairs={{0,4},{1,5},{2,6},{3,7},{4,0},{5,1},{6,2},{7,3},{8,12},{9,13},{10,... | collective-permute-start | bytes 73736 | tf_op jit(solution)/shard_map/ppermute | solution.py:37
  168.7 6.9 %collective-permute-start.26 = (bf16[12,1024]{1,0:T(8,128)(2,1)S(1)}, bf16[12,1024]{1,0:T(8,128)(2,1)S(1)}, u32[]{:S(2)}, u32[]{:S(2)}) collective-permute-start(bf16[12,1024]{1,0:T(8,128)(2,1)S(1)} %get-tuple-element.105), channel_id=1, source_target_pairs={{0,2},{1,3},{2,4},{3,5},{4,6},{5,7},{6,0},{7,1},{8,10},{9,11},{10,... | collective-permute-start | bytes 73736 | tf_op jit(solution)/shard_map/ppermute | solution.py:37
  173.9 5.1 %collective-permute-start.30 = (bf16[128,512]{1,0:T(8,128)(2,1)S(1)}, bf16[128,512]{1,0:T(8,128)(2,1)S(1)}, u32[]{:S(2)}, u32[]{:S(2)}) collective-permute-start(bf16[128,512]{1,0:T(8,128)(2,1)S(1)} %select_bitcast_fusion.8), channel_id=1, source_target_pairs={{0,32},{32,0},{64,96},{96,64},{128,160},{160,128},{192,224},{224,1... | collective-permute-start | bytes 393224 | tf_op jit(solution)/shard_map/ppermute | solution.py:90
